TPU v7x, 32 devices: a whole 2x2x4 slice. The times are simulated.
32 devices in a mesh: gen: 8 (over z, y), grp: 4 (over x, core).
Axes of the slice: x: 2, y: 2, z: 4, core: 2. Of those that a mesh axis runs over, the one named last changes fastest.
Arguments:
- query_in: bfloat16 [4, 1024, 4096], P('grp', 'gen'), may hold values from -8 to 8, as said below
- key_in: bfloat16 [4, 1024, 4096], P('grp', 'gen'), may hold values from -8 to 8
- value_in: bfloat16 [4, 1024, 4096], P('grp', 'gen'), may hold values from -6 to 6
- teacher_w: bfloat16 [4096, 5120], P('gen'), may hold values from -0.09375 to 0.09375
- disc_heads: float32 [8, 5120], replicated, may hold values from -0.078125 to 0.078125
- frame_of_token: int32 [4, 1024], P('grp'), may hold values from 0 to 20, never falling along the last dimension, each value on 1 to 97 neighbouring positions
- head_of_frame: int32 [4, 21], P('grp'), may hold values from 0 to 7
- timestep: int32 [4], P('grp'), may hold values from 0 to 999
Outputs:
- latents: bfloat16 [4, 1024, 4096], P('grp', 'gen')
- grad_query: bfloat16 [4, 1024, 4096], P('grp', 'gen')
- grad_key: bfloat16 [4, 1024, 4096], P('grp', 'gen')
- grad_value: bfloat16 [4, 1024, 4096], P('grp', 'gen')
- grad_heads: float32 [8, 5120], replicated
Inputs may be any that keep to these rules, and one draw needn't show every extreme that they name: `query_in`: entries lie within the range; in some draws a few queries equal some keys. `frame_of_token`: within a clip the frame numbers never fall along the tokens; every frame holds 1 to 97 tokens and some frame exactly 97.
All inputs are finite; a program needn't handle non-finite values.
Results may differ from a plain program's by a relative error of at most 0.035.
Values may be sent and summed in bfloat16 or wider, within the bound.
No kernel may reach another device: no remote copies, remote signals or barrier semaphores. Data moves between devices by JAX's collectives and lax.ppermute only.
A program may use at most 64 MiB of HBM per device.

v0:
```python
import math

import jax
import jax.numpy as jnp
from jax import lax
from jax.sharding import PartitionSpec as P

HS = 128
FRAMES = 21
NDH = 8
NSTEPS = 1000


epsilon = 1e-06


def forward_rows(query_rows, key_three, value_three):
    inv_scale = 1.0 / math.sqrt(HS)
    scores = (
        jnp.einsum("rhd,thd->hrt", query_rows, key_three, preferred_element_type=jnp.float32)
        * inv_scale
    )
    peak = jnp.max(scores, axis=2, keepdims=True)
    weights = jnp.exp(scores - peak)
    total = jnp.sum(weights, axis=2, keepdims=True)
    mixed = jnp.einsum(
        "hrt,thd->rhd",
        weights.astype(jnp.bfloat16),
        value_three,
        preferred_element_type=jnp.float32,
    )
    mixed = mixed / jnp.transpose(total, (1, 0, 2))
    lse_rows = jnp.transpose((peak + jnp.log(total))[:, :, 0], (1, 0))
    return (mixed.astype(jnp.bfloat16), lse_rows)


def backward_rows(carry, items, key_three, value_three):
    inv_scale = 1.0 / math.sqrt(HS)
    grad_key, grad_value = carry
    query_rows, lse_rows, grad_rows, delta_rows = items
    scores = (
        jnp.einsum("rhd,thd->hrt", query_rows, key_three, preferred_element_type=jnp.float32)
        * inv_scale
    )
    probs = jnp.exp(scores - jnp.transpose(lse_rows, (1, 0))[:, :, None])
    grad_value = grad_value + jnp.einsum(
        "hrt,rhd->thd", probs.astype(jnp.bfloat16), grad_rows, preferred_element_type=jnp.float32
    )
    grad_probs = jnp.einsum(
        "rhd,thd->hrt", grad_rows, value_three, preferred_element_type=jnp.float32
    )
    dscore = (
        probs * (grad_probs - jnp.transpose(delta_rows, (1, 0))[:, :, None]) * inv_scale
    ).astype(jnp.bfloat16)
    grad_query = jnp.einsum(
        "hrt,thd->rhd", dscore, key_three, preferred_element_type=jnp.float32
    ).astype(jnp.bfloat16)
    grad_key = grad_key + jnp.einsum(
        "hrt,rhd->thd", dscore, query_rows, preferred_element_type=jnp.float32
    )
    return ((grad_key, grad_value), grad_query)


def on_device(
    query_in, key_in, value_in, teacher_w, disc_heads, frame_of_token, head_of_frame, timestep
):
    group = lax.axis_size("gen")
    tok_dev = query_in.shape[1]
    width = query_in.shape[2]
    tokens = tok_dev * group
    heads_dev = width // HS // group
    local_width = heads_dev * HS
    row_block = min(512, tokens)
    block_count = tokens // row_block
    seq_rows = (query_in[0], key_in[0], value_in[0])
    head_query, head_key, head_value = (
        lax.all_to_all(seq_rows[0], "gen", split_axis=1, concat_axis=0, tiled=True),
        lax.all_to_all(seq_rows[1], "gen", split_axis=1, concat_axis=0, tiled=True),
        lax.all_to_all(seq_rows[2], "gen", split_axis=1, concat_axis=0, tiled=True),
    )
    key_three = head_key.reshape(tokens, heads_dev, HS)
    value_three = head_value.reshape(tokens, heads_dev, HS)

    def forward_block(query_rows):
        return forward_rows(query_rows, key_three, value_three)

    mixed_blocks, lse_blocks = lax.map(
        forward_block, head_query.reshape(block_count, row_block, heads_dev, HS)
    )
    mixed = mixed_blocks.reshape(tokens, local_width)
    latents = lax.all_to_all(mixed, "gen", split_axis=0, concat_axis=1, tiled=True)
    frames = frame_of_token[0]
    frame_ids = lax.broadcasted_iota(jnp.int32, (FRAMES, tokens), 0)
    member = frames[None, :] == frame_ids
    counts = jnp.sum(member.astype(jnp.float32), axis=1)
    pooled = (
        jnp.dot(member.astype(jnp.bfloat16), mixed, preferred_element_type=jnp.float32)
        / counts[:, None]
    )
    square_part = jnp.sum(pooled * pooled, axis=1)
    project_part = jnp.dot(
        pooled.astype(jnp.bfloat16), teacher_w, preferred_element_type=jnp.float32
    )
    head_ids = lax.broadcasted_iota(jnp.int32, (FRAMES, NDH), 1)
    picked = (head_of_frame[0][:, None] == head_ids).astype(jnp.float32)
    head_rows = jnp.dot(picked, disc_heads, precision=lax.Precision.HIGHEST)
    weight = (timestep[0].astype(jnp.float32) + 1.0) / NSTEPS
    projected, squares = (
        lax.psum(project_part.astype(jnp.bfloat16), "gen").astype(jnp.float32),
        lax.psum(square_part.astype(jnp.bfloat16), "gen").astype(jnp.float32),
    )
    root = jnp.sqrt(squares / width + epsilon)
    pre = projected / root[:, None]
    gate = jax.nn.sigmoid(pre)
    feature = pre * gate
    score = jnp.sum(feature * head_rows, axis=1)
    grad_score = -weight * jax.nn.sigmoid(-score) / FRAMES
    head_part = jnp.dot(picked.T, grad_score[:, None] * feature, precision=lax.Precision.HIGHEST)
    grad_pre = grad_score[:, None] * head_rows * gate * (1.0 + pre * (1.0 - gate))
    grad_projected = (grad_pre / root[:, None]).astype(jnp.bfloat16)
    grad_root = -jnp.sum(grad_pre * pre, axis=1) / root
    grad_heads = lax.psum(head_part.astype(jnp.bfloat16), "grp").astype(jnp.float32)
    grad_pooled = (
        jnp.dot(grad_projected, teacher_w.T, preferred_element_type=jnp.float32)
        + (grad_root / root / width)[:, None] * pooled
    )
    spread = grad_pooled / counts[:, None]
    grad_mixed = (tokens * jnp.take(spread, frames, axis=0)).astype(jnp.bfloat16)
    product = grad_mixed.astype(jnp.float32) * mixed.astype(jnp.float32)
    delta = jnp.sum(product.reshape(tokens, heads_dev, HS), axis=2)
    back_query, back_key, back_value = (head_query, head_key, head_value)
    back_key_three = back_key.reshape(tokens, heads_dev, HS)
    back_value_three = back_value.reshape(tokens, heads_dev, HS)

    def back_block(carry, items):
        return backward_rows(carry, items, back_key_three, back_value_three)

    block_items = (
        back_query.reshape(block_count, row_block, heads_dev, HS),
        lse_blocks,
        grad_mixed.reshape(block_count, row_block, heads_dev, HS),
        delta.reshape(block_count, row_block, heads_dev),
    )
    zeros_start = jnp.zeros((tokens, heads_dev, HS), jnp.float32)
    sums_out, query_blocks = lax.scan(back_block, (zeros_start, zeros_start), block_items)
    grads = (
        query_blocks.reshape(tokens, local_width),
        sums_out[0].astype(jnp.bfloat16).reshape(tokens, local_width),
        sums_out[1].astype(jnp.bfloat16).reshape(tokens, local_width),
    )
    out_query, out_key, out_value = (
        lax.all_to_all(grads[0], "gen", split_axis=0, concat_axis=1, tiled=True),
        lax.all_to_all(grads[1], "gen", split_axis=0, concat_axis=1, tiled=True),
        lax.all_to_all(grads[2], "gen", split_axis=0, concat_axis=1, tiled=True),
    )
    return (latents[None], out_query[None], out_key[None], out_value[None], grad_heads)


def solution(mesh):
    return jax.shard_map(
        on_device,
        mesh=mesh,
        in_specs=(
            P("grp", "gen", None),
            P("grp", "gen", None),
            P("grp", "gen", None),
            P("gen", None),
            P(),
            P("grp", None),
            P("grp", None),
            P("grp"),
        ),
        out_specs=(
            P("grp", "gen", None),
            P("grp", "gen", None),
            P("grp", "gen", None),
            P("grp", "gen", None),
            P(),
        ),
        check_vma=False,
    )
```

profile of v0, /device:TPU:8, one launch (start us, length us, event | category | flops | bytes accessed | tf_op | source)
XLA Modules:
  0.0 386.6 jit_solution(8259418407635553326)
XLA Ops:
  7.2 1.7 copy.150
  8.9 1.3 copy.116
  10.2 6.3 %all-to-all-start = ((bf16[128,8,512]{2,0,1:T(8,128)(2,1)}), bf16[128,8,512]{2,0,1:T(8,128)(2,1)S(1)}, u32[]{:S(2)}, u32[]{:S(2)}) async-start(bf16[128,8,512]{2,0,1:T(8,128)(2,1)} %copy.116), calls=%async_computation | async-start | bytes 2097152 | tf_op jit(solution)/shard_map/all_to_all | solution.py:77
  16.5 1.3 copy.117
  17.8 22.1 %all-to-all-done = bf16[128,8,512]{2,0,1:T(8,128)(2,1)S(1)} async-done(((bf16[128,8,512]{2,0,1:T(8,128)(2,1)}), bf16[128,8,512]{2,0,1:T(8,128)(2,1)S(1)}, u32[]{:S(2)}, u32[]{:S(2)}) %all-to-all-start) | async-done | bytes 1048608 | tf_op jit(solution)/shard_map/all_to_all | solution.py:77
  39.9 6.0 %all-to-all-start.1 = ((bf16[128,8,512]{0,2,1:T(8,128)(2,1)}), bf16[128,8,512]{0,2,1:T(8,128)(2,1)S(1)}, u32[]{:S(2)}, u32[]{:S(2)}) async-start(bf16[128,8,512]{0,2,1:T(8,128)(2,1)} %bitcast.9), calls=%async_computation.1 | async-start | bytes 2097152 | tf_op jit(solution)/shard_map/all_to_all | solution.py:78
  45.8 2.2 copy.119
  48.1 21.3 %all-to-all-done.1 = bf16[128,8,512]{0,2,1:T(8,128)(2,1)S(1)} async-done(((bf16[128,8,512]{0,2,1:T(8,128)(2,1)}), bf16[128,8,512]{0,2,1:T(8,128)(2,1)S(1)}, u32[]{:S(2)}, u32[]{:S(2)}) %all-to-all-start.1) | async-done | bytes 1048608 | tf_op jit(solution)/shard_map/all_to_all | solution.py:78
  69.4 6.5 %all-to-all-start.2 = ((bf16[128,8,512]{0,2,1:T(8,128)(2,1)}), bf16[128,8,512]{0,2,1:T(8,128)(2,1)}, u32[]{:S(2)}, u32[]{:S(2)}) async-start(bf16[128,8,512]{0,2,1:T(8,128)(2,1)} %bitcast.11), calls=%async_computation.2 | async-start | bytes 2097152 | tf_op jit(solution)/shard_map/all_to_all | solution.py:79
  80.8 2.3 copy.121
  83.1 1.9 copy.118
  85.0 1.3 reshape.141
  86.3 1.6 copy.122
  87.9 11.2 %all-to-all-done.2 = bf16[128,8,512]{0,2,1:T(8,128)(2,1)} async-done(((bf16[128,8,512]{0,2,1:T(8,128)(2,1)}), bf16[128,8,512]{0,2,1:T(8,128)(2,1)}, u32[]{:S(2)}, u32[]{:S(2)}) %all-to-all-start.2) | async-done | bytes 1048608 | tf_op jit(solution)/shard_map/all_to_all | solution.py:79
  99.1 2.9 copy.120
  102.0 2.3 reshape.142
  104.3 2.3 copy.123
  106.6 14.5 %while.27 = (s32[]{:T(128)}, bf16[2,512,4,128]{3,1,2,0:T(8,128)(2,1)}, f32[2,512,4]{1,2,0:T(4,128)S(1)}, bf16[2,512,4,128]{3,1,2,0:T(8,128)(2,1)}, bf16[1024,4,1...) while((s32[]{:T(128)}, bf16[2,512,4,128]{3,1,2,0:T(8,128)(2,1)}, ...), condition=%wide.region_3.4_spmd, body=%wide.region_0.3_spmd.sunk | while | flops 1091041280 | bytes 40960180 | solution.py:87
  106.6 2.4 multiply_reduce_fusion.5
  108.9 1.9 fusion.95
  110.8 2.0 fusion.96
  113.8 2.4 multiply_reduce_fusion.5
  116.2 1.9 fusion.95
  118.1 2.0 fusion.96
  121.1 3.0 copy.124
  124.1 2.4 copy.129
  126.5 2.2 all_to_all.93
  128.7 1.6 multiply_reduce_fusion.3
  130.3 18.5 %psum.22 = bf16[21]{0:T(256)(128)(2,1)S(1)} all-reduce(bf16[21]{0:T(256)(128)(2,1)S(1)} %get-tuple-element.266), channel_id=1, replica_groups=mesh['gen'=8,'grp'=4] {'gen'}, use_global_device_ids=true, to_apply=%region_7.8 | all-reduce | flops 21 | bytes 84 | tf_op jit(solution)/shard_map/psum | solution.py:110
  148.8 4.0 %convolution_convert_fusion.1 = bf16[21,5120]{1,0:T(8,128)(2,1)} fusion(bf16[512,5120]{1,0:T(8,128)(2,1)} %param.15, f32[21,512]{1,0:T(8,128)S(1)} %get-tuple-element.267), kind=kOutput, calls=%fused_computation.45 | convolution fusion | flops 110218752 | bytes 5500928 | tf_op jit(solution)/shard_map/dot_general | solution.py:101
  152.9 7.4 %all-to-all-start.3 = ((bf16[8,128,512]{2,1,0:T(8,128)(2,1)}), bf16[8,128,512]{2,1,0:T(8,128)(2,1)}, u32[]{:S(2)}, u32[]{:S(2)}) async-start(bf16[8,128,512]{2,1,0:T(8,128)(2,1)} %all_to_all.93), calls=%async_computation.3 | async-start | bytes 2097152 | tf_op jit(solution)/shard_map/all_to_all | solution.py:91
  160.9 66.9 %all-reduce.3.cloned.1.call-done = bf16[21,5120]{1,0:T(8,128)(2,1)} async-done(((bf16[21,5120]{1,0:T(8,128)(2,1)}), bf16[21,5120]{1,0:T(8,128)(2,1)}) %all-reduce.3.cloned.1.call-update) | async-done | bytes 215056 | tf_op jit(solution)/shard_map/psum | solution.py:109
  227.8 1.6 multiply_reduce_fusion.2
  230.6 4.0 %fusion.49 = f32[21,512]{1,0:T(8,128)S(1)} fusion(bf16[512,5120]{1,0:T(8,128)(2,1)} %param.15, f32[21]{0:T(128)S(1)} %copy-done.25, f32[21,512]{1,0:T(8,128)S(1)} %copy-done.21, f32[21]{0:T(128)S(1)} %fusion.62, f32[21]{0:T(128)} %copy-done.29, f32[21,5120]{1,0:T(8,128)S(1)} %get-tuple-element.269, f32[21]{0:T(128)S(1)} %multiply_multiply_fusion, ...), kind=kOutput, calls=%fused_computation.56 | convolution fusion | flops 111530496 | bytes 5974352 | tf_op jit(solution)/shard_map/dot_general | solution.py:124
  234.6 4.9 %gather_fusion = f32[1024,512]{1,0:T(8,128)} fusion(f32[21,512]{1,0:T(8,128)S(1)} %fusion.49, s32[1024]{0:T(1024)S(1)} %copy-done.22), kind=kCustom, calls=%fused_computation | custom fusion | bytes 4198400 | tf_op jit(solution)/shard_map/jit(_take)/gather | solution.py:128
  239.5 2.9 gather.9
  242.4 2.8 fusion.46
  245.3 1.3 fusion.48
  246.6 23.1 %while.28 = (s32[]{:T(128)}, f32[1024,4,128]{0,2,1:T(8,128)S(1)}, f32[1024,4,128]{0,2,1:T(8,128)}, bf16[2,512,4,128]{3,2,1,0:T(4,128)(2,1)}, bf16[2,512,4,128]{3...) while((s32[]{:T(128)}, f32[1024,4,128]{0,2,1:T(8,128)S(1)}, ...), condition=%wide.region_12.13_spmd.clone, body=%wide.region_11.12_spmd.clone.sunk | while | flops 2705588224 | bytes 90759520 | solution.py:145
  246.6 2.4 fusion.107
  249.1 2.4 bitcast_add_fusion.5
  251.5 2.6 multiply_convert_fusion.2
  254.1 1.3 fusion.108
  258.2 2.4 fusion.107
  260.7 2.4 bitcast_add_fusion.5
  263.1 2.5 multiply_convert_fusion.2
  265.7 1.3 fusion.108
  269.7 2.2 all_to_all.96
  271.9 4.9 %all-to-all-start.4 = ((bf16[8,128,512]{2,1,0:T(8,128)(2,1)}), bf16[8,128,512]{2,1,0:T(8,128)(2,1)S(1)}, u32[]{:S(2)}, u32[]{:S(2)}) async-start(bf16[8,128,512]{2,1,0:T(8,128)(2,1)} %all_to_all.96), calls=%async_computation.4 | async-start | bytes 2097152 | tf_op jit(solution)/shard_map/all_to_all | solution.py:152
  277.1 1.2 copy.152
  278.3 2.4 copy.145
  280.7 18.2 %all-to-all-done.4 = bf16[8,128,512]{2,1,0:T(8,128)(2,1)S(1)} async-done(((bf16[8,128,512]{2,1,0:T(8,128)(2,1)}), bf16[8,128,512]{2,1,0:T(8,128)(2,1)S(1)}, u32[]{:S(2)}, u32[]{:S(2)}) %all-to-all-start.4) | async-done | bytes 1048608 | tf_op jit(solution)/shard_map/all_to_all | solution.py:152
  298.9 6.3 %all-to-all-start.5 = ((bf16[8,128,512]{2,1,0:T(8,128)(2,1)}), bf16[8,128,512]{2,1,0:T(8,128)(2,1)}, u32[]{:S(2)}, u32[]{:S(2)}) async-start(bf16[8,128,512]{2,1,0:T(8,128)(2,1)} %copy.145), calls=%async_computation.5 | async-start | bytes 2097152 | tf_op jit(solution)/shard_map/all_to_all | solution.py:153
  305.7 1.5 copy.146
  307.1 20.8 %all-to-all-done.5 = bf16[8,128,512]{2,1,0:T(8,128)(2,1)} async-done(((bf16[8,128,512]{2,1,0:T(8,128)(2,1)}), bf16[8,128,512]{2,1,0:T(8,128)(2,1)}, u32[]{:S(2)}, u32[]{:S(2)}) %all-to-all-start.5) | async-done | bytes 1048608 | tf_op jit(solution)/shard_map/all_to_all | solution.py:153
  327.9 6.0 %all-to-all-start.6 = ((bf16[8,128,512]{2,1,0:T(8,128)(2,1)}), bf16[8,128,512]{2,1,0:T(8,128)(2,1)S(1)}, u32[]{:S(2)}, u32[]{:S(2)}) async-start(bf16[8,128,512]{2,1,0:T(8,128)(2,1)} %copy.146), calls=%async_computation.6 | async-start | bytes 2097152 | tf_op jit(solution)/shard_map/all_to_all | solution.py:154
  335.1 33.3 %all-reduce.5.cloned.1.call-done = bf16[8,5120]{1,0:T(8,128)(2,1)} async-done(((bf16[8,5120]{1,0:T(8,128)(2,1)}), bf16[8,5120]{1,0:T(8,128)(2,1)}) %all-reduce.5.cloned.1.call-update) | async-done | bytes 81936 | tf_op jit(solution)/shard_map/psum | solution.py:122
  368.4 1.6 convert_element_type.91
  370.0 1.6 copy.125
  371.6 1.3 copy.139
  373.6 1.3 copy.140
  374.9 1.6 copy.136
  376.5 1.3 copy.141
  378.5 1.3 copy.142
  (124 shorter events, 16.5 us)
Async XLA Ops:
  7.2 220.6 %copy-start = (f32[8,5120]{1,0:T(8,128)S(1)}, f32[8,5120]{1,0:T(8,128)}, u32[]{:S(2)}) copy-start(f32[8,5120]{1,0:T(8,128)} %param.16) | copy-start | bytes 491524
  7.2 9.3 %copy-start.13 = (bf16[1,128,4096]{2,1,0:T(8,128)(2,1)S(1)}, bf16[1,128,4096]{2,1,0:T(8,128)(2,1)}, u32[]{:S(2)}) copy-start(bf16[1,128,4096]{2,1,0:T(8,128)(2,1)} %param.13) | copy-start | bytes 3145732
  10.2 29.7 %all-to-all-start = ((bf16[128,8,512]{2,0,1:T(8,128)(2,1)}), bf16[128,8,512]{2,0,1:T(8,128)(2,1)S(1)}, u32[]{:S(2)}, u32[]{:S(2)}) async-start(bf16[128,8,512]{2,0,1:T(8,128)(2,1)} %copy.116), calls=%async_computation | async-start | bytes 2097152 | tf_op jit(solution)/shard_map/all_to_all | solution.py:77
  16.5 60.6 %copy-start.19 = (s32[1,1024]{1,0:T(1,128)S(1)}, s32[1,1024]{1,0:T(1,128)}, u32[]{:S(2)}) copy-start(s32[1,1024]{1,0:T(1,128)} %param.17) | copy-start | bytes 12292
  39.9 29.5 %all-to-all-start.1 = ((bf16[128,8,512]{0,2,1:T(8,128)(2,1)}), bf16[128,8,512]{0,2,1:T(8,128)(2,1)S(1)}, u32[]{:S(2)}, u32[]{:S(2)}) async-start(bf16[128,8,512]{0,2,1:T(8,128)(2,1)} %bitcast.9), calls=%async_computation.1 | async-start | bytes 2097152 | tf_op jit(solution)/shard_map/all_to_all | solution.py:78
  69.4 6.5 %copy-start.12 = (bf16[128,8,512]{0,2,1:T(8,128)(2,1)}, bf16[128,8,512]{0,2,1:T(8,128)(2,1)S(1)}, u32[]{:S(2)}) copy-start(bf16[128,8,512]{0,2,1:T(8,128)(2,1)S(1)} %all-to-all-done.1) | copy-start | bytes 3145732
  69.4 29.7 %all-to-all-start.2 = ((bf16[128,8,512]{0,2,1:T(8,128)(2,1)}), bf16[128,8,512]{0,2,1:T(8,128)(2,1)}, u32[]{:S(2)}, u32[]{:S(2)}) async-start(bf16[128,8,512]{0,2,1:T(8,128)(2,1)} %bitcast.11), calls=%async_computation.2 | async-start | bytes 2097152 | tf_op jit(solution)/shard_map/all_to_all | solution.py:79
  75.9 151.9 %all-reduce.3.cloned.1.call-start = ((), (), s32[]{:S(2)}) async-start(), calls=%async_computation.7 | async-start | bytes 491520 | tf_op jit(solution)/shard_map/psum | solution.py:109
  77.9 50.8 %copy-start.29 = (f32[21]{0:T(128)}, f32[21]{0:T(128)S(1)}, u32[]{:S(2)}) copy-start(f32[21]{0:T(128)S(1)} %convert_reduce_fusion) | copy-start | bytes 256
  108.9 1.9 copy-start.7
  108.9 1.9 copy-start.10
  112.8 1.0 copy-start.11
  116.2 1.9 copy-start.7
  116.2 1.9 copy-start.10
  120.1 1.0 copy-start.11
  121.1 31.8 %copy-start.17 = (f32[2,512,4]{1,2,0:T(4,128)}, f32[2,512,4]{1,2,0:T(4,128)S(1)}, u32[]{:S(2)}) copy-start(f32[2,512,4]{1,2,0:T(4,128)S(1)} %get-tuple-element.403) | copy-start | bytes 49156
  130.3 30.6 %copy-start.20 = (f32[21,512]{1,0:T(8,128)}, f32[21,512]{1,0:T(8,128)S(1)}, u32[]{:S(2)}) copy-start(f32[21,512]{1,0:T(8,128)S(1)} %get-tuple-element.267) | copy-start | bytes 129028
  148.8 12.0 %copy-start.31 = (bf16[21]{0:T(256)(128)(2,1)}, bf16[21]{0:T(256)(128)(2,1)S(1)}, u32[]{:S(2)}) copy-start(bf16[21]{0:T(256)(128)(2,1)S(1)} %psum.22) | copy-start | bytes 130
  152.9 119.1 %all-to-all-start.3 = ((bf16[8,128,512]{2,1,0:T(8,128)(2,1)}), bf16[8,128,512]{2,1,0:T(8,128)(2,1)}, u32[]{:S(2)}, u32[]{:S(2)}) async-start(bf16[8,128,512]{2,1,0:T(8,128)(2,1)} %all_to_all.93), calls=%async_computation.3 | async-start | bytes 2097152 | tf_op jit(solution)/shard_map/all_to_all | solution.py:91
  227.8 1.6 copy-start.16
  227.8 2.7 copy-start.32
  227.8 2.7 copy-start.21
  227.8 2.7 copy-start.25
  229.4 5.2 %copy-start.27 = (f32[21]{0:T(128)}, f32[21]{0:T(128)S(1)}, u32[]{:S(2)}) copy-start(f32[21]{0:T(128)S(1)} %multiply_multiply_fusion) | copy-start | bytes 256
  230.6 4.0 %copy-start.22 = (s32[1024]{0:T(1024)S(1)}, s32[1024]{0:T(1024)}, u32[]{:S(2)}) copy-start(s32[1024]{0:T(1024)} %broadcast_clamp_fusion) | copy-start | bytes 12292
  239.5 2.9 copy-start.24
  239.5 5.7 %copy-start.23 = (pred[2,512]{1,0:T(4,128)(4,1)S(1)}, pred[2,512]{1,0:T(4,128)(4,1)}, u32[]{:S(2)}) copy-start(pred[2,512]{1,0:T(4,128)(4,1)} %compare_and_fusion) | copy-start | bytes 3076
  242.4 2.9 copy-start.9
  242.4 4.2 %copy-start.18 = (f32[2,512,4]{1,2,0:T(4,128)S(1)}, f32[2,512,4]{1,2,0:T(4,128)}, u32[]{:S(2)}) copy-start(f32[2,512,4]{1,2,0:T(4,128)} %copy-done.17) | copy-start | bytes 49156
  246.6 2.5 copy-start.3
  246.6 2.5 copy-start.6
  249.1 2.4 copy-start.8
  251.5 2.6 copy-start.4
  254.1 1.3 copy-start.2
  255.4 1.2 copy-start.14
  257.1 1.1 copy-start.15
  258.2 2.5 copy-start.3
  258.2 2.5 copy-start.6
  260.6 2.4 copy-start.8
  263.1 2.6 copy-start.4
  265.7 1.3 copy-start.2
  266.9 1.2 copy-start.14
  268.6 1.1 copy-start.15
  271.9 26.9 %all-to-all-start.4 = ((bf16[8,128,512]{2,1,0:T(8,128)(2,1)}), bf16[8,128,512]{2,1,0:T(8,128)(2,1)S(1)}, u32[]{:S(2)}, u32[]{:S(2)}) async-start(bf16[8,128,512]{2,1,0:T(8,128)(2,1)} %all_to_all.96), calls=%async_computation.4 | async-start | bytes 2097152 | tf_op jit(solution)/shard_map/all_to_all | solution.py:152
  277.0 28.2 %copy-start.5 = (f32[1024,4,128]{0,2,1:T(8,128)S(1)}, f32[1024,4,128]{0,2,1:T(8,128)}, u32[]{:S(2)}) copy-start(f32[1024,4,128]{0,2,1:T(8,128)} %get-tuple-element.96) | copy-start | bytes 6291460
  298.9 29.0 %all-to-all-start.5 = ((bf16[8,128,512]{2,1,0:T(8,128)(2,1)}), bf16[8,128,512]{2,1,0:T(8,128)(2,1)}, u32[]{:S(2)}, u32[]{:S(2)}) async-start(bf16[8,128,512]{2,1,0:T(8,128)(2,1)} %copy.145), calls=%async_computation.5 | async-start | bytes 2097152 | tf_op jit(solution)/shard_map/all_to_all | solution.py:153
  305.2 28.7 %copy-start.26 = (f32[21]{0:T(128)S(1)}, f32[21]{0:T(128)}, u32[]{:S(2)}) copy-start(f32[21]{0:T(128)} %add_sqrt_fusion) | copy-start | bytes 256
  305.2 28.7 %copy-start.28 = (f32[21]{0:T(128)S(1)}, f32[21]{0:T(128)}, u32[]{:S(2)}) copy-start(f32[21]{0:T(128)} %copy-done.27) | copy-start | bytes 256
  305.2 28.7 %copy-start.30 = (s32[1,21]{1,0:T(1,128)S(1)}, s32[1,21]{1,0:T(1,128)}, u32[]{:S(2)}) copy-start(s32[1,21]{1,0:T(1,128)} %param.18) | copy-start | bytes 256
  327.9 49.9 %all-to-all-start.6 = ((bf16[8,128,512]{2,1,0:T(8,128)(2,1)}), bf16[8,128,512]{2,1,0:T(8,128)(2,1)S(1)}, u32[]{:S(2)}, u32[]{:S(2)}) async-start(bf16[8,128,512]{2,1,0:T(8,128)(2,1)} %copy.146), calls=%async_computation.6 | async-start | bytes 2097152 | tf_op jit(solution)/shard_map/all_to_all | solution.py:154
  333.9 34.5 %all-reduce.5.cloned.1.call-start = ((), (), s32[]{:S(2)}) async-start(), calls=%async_computation.8 | async-start | bytes 163840 | tf_op jit(solution)/shard_map/psum | solution.py:122
  373.5 6.2 %copy-start.1 = (f32[8,5120]{1,0:T(8,128)S(1)}, f32[8,5120]{1,0:T(8,128)}, u32[]{:S(2)}) copy-start(f32[8,5120]{1,0:T(8,128)} %param.16) | copy-start | bytes 491524
Sparse Core Ops, SparseCore 0:
  153.0 74.7 all-reduce.2
  337.7 30.5 all-reduce.4
where the time goes:
time: 389 us; the launch traced here: 387 us
  waiting for transfers between devices  194 us (50%)
  local copies, waits for them, and re-layouts  60.6 us (16%)
  starting transfers between devices  43.5 us (11%)
  matrix products  40.8 us (10%)
  blocking collectives  18.5 us (5%)
  between operations  15 us (4%)
  other arithmetic  14.1 us (4%)
    psum x1, waiting for transfers between devices, on_device(): lax.psum(project_part.astype(jnp.bfloat16), 'gen').astype(jnp.float32)  66.9 us
    psum x1, waiting for transfers between devices, on_device(): lax.psum(head_part.astype(jnp.bfloat16), 'grp').astype(jnp.float32)  33.3 us
    all_to_all x1, waiting for transfers between devices, on_device(): lax.all_to_all(seq_rows[0], 'gen', split_axis=1, concat_axis=0, tiled=True)  22.1 us
    all_to_all x1, waiting for transfers between devices, on_device(): lax.all_to_all(seq_rows[1], 'gen', split_axis=1, concat_axis=0, tiled=True)  21.3 us
    all_to_all x1, waiting for transfers between devices, on_device(): lax.all_to_all(grads[1], 'gen', split_axis=0, concat_axis=1, tiled=True)  20.8 us
    psum x1, blocking collectives, on_device(): lax.psum(square_part.astype(jnp.bfloat16), 'gen').astype(jnp.float32)  18.5 us
    all_to_all x1, waiting for transfers between devices, on_device(): lax.all_to_all(grads[0], 'gen', split_axis=0, concat_axis=1, tiled=True)  18.2 us
    unnamed x56, local copies, waits for them, and re-layouts  12.6 us
  transfers between devices with their start and end apart: 9, of which 7 were waited for; matrix products, arithmetic and copies ran while one was open for 18% of the time, Pallas kernels for 0%

commit v1 on v0

v1 whole, which is shorter than its diff:
```python
import functools
import math

import jax
import jax.numpy as jnp
from jax import lax
from jax.experimental import pallas as pl
from jax.experimental.pallas import tpu as pltpu
from jax.sharding import PartitionSpec as P

HS = 128
FRAMES = 21
FR = 24
NDH = 8
NSTEPS = 1000
LANES = 128
epsilon = 1e-06
SCALE = 1.0 / math.sqrt(HS)
LOG2E = math.log2(math.e)
BF = jnp.bfloat16
F32 = jnp.float32
VMEM_LIMIT = 48 * 1024 * 1024


def params(axes=1):
    return pltpu.CompilerParams(
        vmem_limit_bytes=VMEM_LIMIT, dimension_semantics=("arbitrary",) * axes
    )


def dot_nn(a, b):
    return lax.dot_general(a, b, (((1,), (0,)), ((), ())), preferred_element_type=F32)


def dot_nt(a, b):
    return lax.dot_general(a, b, (((1,), (1,)), ((), ())), preferred_element_type=F32)


def dot_tn(a, b):
    return lax.dot_general(a, b, (((0,), (0,)), ((), ())), preferred_element_type=F32)


def rows_of(ref):
    block = ref[...]
    return block.reshape(block.shape[-3] * block.shape[-2], block.shape[-1])


def split_three(value):
    high = value.astype(BF)
    rest = value - high.astype(F32)
    middle = rest.astype(BF)
    low = (rest - middle.astype(F32)).astype(BF)
    return high, middle, low


def lanes_three(value, shape, first):
    lane = lax.broadcasted_iota(jnp.int32, shape, 1)
    out = jnp.zeros(shape, F32)
    for i, part in enumerate(split_three(value)):
        out = jnp.where(lane == first + i, part.astype(F32), out)
    return out


def ones_three(shape):
    lane = lax.broadcasted_iota(jnp.int32, shape, 1)
    return jnp.where(lane < 3, 1.0, 0.0).astype(BF)


def take_lanes(block, first, count):
    lane = lax.broadcasted_iota(jnp.int32, block.shape, 1)
    keep = (lane >= first) & (lane < first + count)
    return jnp.sum(jnp.where(keep, block, 0.0), axis=1, keepdims=True)


def row_chunk(tokens):
    return min(256, tokens)


def stats_kernel(q_ref, k_ref, mt_ref, aug_ref, r_ref):
    blocks = q_ref.shape[0]
    tokens = blocks * LANES
    chunk = row_chunk(tokens)
    per = chunk // LANES
    keys = rows_of(k_ref)

    def step(i, total_r):
        q = q_ref[pl.ds(i * per, per)].reshape(chunk, HS)
        s = dot_nt(q, keys) * (SCALE * LOG2E)
        peak = jnp.max(s, axis=1, keepdims=True)
        e = jnp.exp2(s - peak)
        total = jnp.sum(e, axis=1, keepdims=True)
        p = (e * (1.0 / total)).astype(BF)
        lse = (peak + jnp.log2(total)) * (-1.0 / (SCALE * LOG2E))
        aug_ref[0, pl.ds(pl.multiple_of(i * chunk, chunk), chunk)] = lanes_three(
            lse, (chunk, LANES), 0
        ).astype(BF)
        return total_r + dot_nn(mt_ref[i], p)

    zero = jnp.zeros((FR, tokens), F32)
    r = run_steps(tokens // chunk, step, zero)
    for d in range(blocks):
        r_ref[d, 0] = r[:, d * LANES : (d + 1) * LANES].astype(BF)


def run_steps(count, step, carry):
    if count <= 4:
        for i in range(count):
            carry = step(i, carry)
        return carry
    return lax.fori_loop(0, count, step, carry)


def pool_kernel(blocks, heads, chunk, r_ref, v_ref, meta_ref, w_ref, part_ref, pooled_ref):
    count = jnp.maximum(take_lanes(meta_ref[...], 0, 1), 1.0)
    columns = []
    for h in range(heads):
        r = jnp.concatenate([r_ref[d, h] for d in range(blocks)], axis=1)
        v = jnp.concatenate(
            [v_ref[d, :, h * HS : (h + 1) * HS] for d in range(blocks)], axis=0
        )
        columns.append(dot_nn(r, v))
    pooled = jnp.concatenate(columns, axis=1) if heads > 1 else columns[0]
    pooled = pooled / count
    pooled_ref[...] = pooled
    squares = jnp.sum(pooled * pooled, axis=1, keepdims=True)
    stats = lanes_three(squares, (FR, LANES), 0).astype(BF)
    rounded = pooled.astype(BF)
    for d in range(blocks):
        w = w_chunk(w_ref, d, chunk)
        part_ref[d, :, :chunk] = dot_nn(rounded, w).astype(BF)
        part_ref[d, :, chunk:] = stats


def w_chunk(w_ref, d, chunk):
    if len(w_ref.shape) == 3:
        return w_ref[d]
    return w_ref[:, d * chunk : (d + 1) * chunk]


def middle_kernel(blocks, chunk, width, got_ref, rows_ref, send_ref, feature_ref, root_ref):
    total = got_ref[0].astype(F32)
    for d in range(1, blocks):
        total = total + got_ref[d].astype(F32)
    projected = total[:, :chunk]
    squares = take_lanes(total[:, chunk:], 0, 3)
    root = jnp.sqrt(squares / width + epsilon)
    pre = projected / root
    gate = jax.nn.sigmoid(pre)
    feature = pre * gate
    head_rows = rows_ref[...]
    direction = head_rows * gate * (1.0 + pre * (1.0 - gate))
    score = jnp.sum(feature * head_rows, axis=1, keepdims=True)
    slope = jnp.sum(direction * pre, axis=1, keepdims=True)
    stats = (
        lanes_three(score, (FR, LANES), 0) + lanes_three(slope, (FR, LANES), 3)
    ).astype(BF)
    rounded = direction.astype(BF)
    for d in range(blocks):
        send_ref[d, :, :chunk] = rounded
        send_ref[d, :, chunk:] = stats
    feature_ref[...] = feature
    root_ref[...] = jnp.broadcast_to(root, (FR, LANES))


def spread_kernel(
    blocks,
    chunk,
    width,
    tokens,
    got_ref,
    w_ref,
    pooled_ref,
    meta_ref,
    root_ref,
    feature_ref,
    picked_ref,
    spread_ref,
    heads_ref,
):
    meta = meta_ref[...]
    count = jnp.maximum(take_lanes(meta, 0, 1), 1.0)
    weight = take_lanes(meta, 1, 1)
    root = take_lanes(root_ref[...], 0, 1)
    stats = got_ref[0, :, chunk:].astype(F32)
    for d in range(1, blocks):
        stats = stats + got_ref[d, :, chunk:].astype(F32)
    score = take_lanes(stats, 0, 3)
    slope = take_lanes(stats, 3, 3)
    grad_score = -weight * jax.nn.sigmoid(-score) / FRAMES
    total = jnp.zeros(pooled_ref.shape, F32)
    for d in range(blocks):
        total = total + dot_nt(got_ref[d, :, :chunk], w_chunk(w_ref, d, chunk))
    grad_root = -(grad_score * slope) / root
    grad_pooled = (grad_score / root) * total + (grad_root / root / width) * pooled_ref[...]
    spread_ref[:FR] = (tokens * (grad_pooled / count)).astype(BF)
    spread_ref[FR:] = jnp.zeros((LANES - FR, pooled_ref.shape[1]), BF)
    scaled = feature_ref[...] * grad_score
    picked = picked_ref[...]
    for j in range(NDH):
        heads_ref[j : j + 1, :] = jnp.sum(scaled * picked[:, j : j + 1], axis=0, keepdims=True)


def output_kernel(q_ref, k_ref, v_ref, aug_ref, o_ref):
    blocks = q_ref.shape[0]
    tokens = blocks * LANES
    chunk = row_chunk(tokens)
    per = chunk // LANES
    keys = jnp.concatenate([rows_of(k_ref), ones_three((tokens, LANES))], axis=1)
    values = rows_of(v_ref)

    def step(i, carry):
        q = q_ref[pl.ds(i * per, per)].reshape(chunk, HS)
        aug = aug_ref[0, pl.ds(pl.multiple_of(i * chunk, chunk), chunk)]
        s = dot_nt(jnp.concatenate([q, aug], axis=1), keys)
        p = jnp.exp2(s * (SCALE * LOG2E)).astype(BF)
        o = dot_nn(p, values).astype(BF)
        o_ref[pl.ds(i * per, per)] = o.reshape(per, LANES, HS)
        return carry

    run_steps(tokens // chunk, step, 0)


def back_kernel(q_ref, k_ref, v_ref, o_ref, aug_ref, m_ref, spread_ref, dqk_ref, dk_ref):
    blocks = q_ref.shape[0]
    tokens = blocks * LANES
    chunk = row_chunk(tokens)
    per = chunk // LANES
    plain = rows_of(k_ref)
    keys = jnp.concatenate([plain, ones_three((tokens, LANES))], axis=1)
    values = rows_of(v_ref)
    spread = spread_ref[...]
    dk_ref[...] = jnp.zeros(dk_ref.shape, F32)

    def step(i, carry):
        at = pl.ds(pl.multiple_of(i * chunk, chunk), chunk)
        q = q_ref[pl.ds(i * per, per)].reshape(chunk, HS)
        o = o_ref[pl.ds(i * per, per)].reshape(chunk, HS)
        s = dot_nt(jnp.concatenate([q, aug_ref[0, at]], axis=1), keys)
        p = jnp.exp2(s * (SCALE * LOG2E))
        grad = dot_nn(m_ref[at], spread)
        delta = jnp.sum(grad * o.astype(F32), axis=1, keepdims=True)
        dp = dot_nt(grad.astype(BF), values)
        ds = (p * (dp - delta)).astype(BF)
        dq = (dot_nn(ds, plain) * SCALE).astype(BF)
        dqk_ref[pl.ds(i * per, per), :LANES] = dq.reshape(per, LANES, HS)
        dk_ref[...] += dot_tn(ds, q)
        return carry

    run_steps(tokens // chunk, step, 0)
    dk = (dk_ref[...] * SCALE).astype(BF)
    dqk_ref[:, LANES:] = dk.reshape(blocks, LANES, HS)


def value_kernel(heads, r_ref, spread_ref, dv_ref):
    for h in range(heads):
        at = slice(h * HS, (h + 1) * HS)
        dv_ref[:, at] = dot_tn(r_ref[0, h], spread_ref[0, :, at]).astype(BF)


def exchange(array):
    return lax.all_to_all(array, "gen", split_axis=0, concat_axis=0, tiled=True)


def on_device(
    query_in, key_in, value_in, teacher_w, disc_heads, frame_of_token, head_of_frame, timestep
):
    n = lax.axis_size("gen")
    grp = lax.axis_size("grp")
    me = lax.axis_index("gen")
    tok = query_in.shape[1]
    width = query_in.shape[2]
    tokens = tok * n
    heads = width // HS // n
    lw = heads * HS
    dh = teacher_w.shape[1]
    columns = dh // n
    chunk = -(-columns // LANES) * LANES
    rows = row_chunk(tokens)

    def to_blocks(array):
        return jnp.transpose(array.reshape(tok, n, lw), (1, 0, 2))

    qk = exchange(jnp.concatenate([to_blocks(query_in[0]), to_blocks(key_in[0])], axis=1))
    v = exchange(to_blocks(value_in[0]))

    frames = frame_of_token[0]
    member = (frames[:, None] == lax.broadcasted_iota(jnp.int32, (tokens, LANES), 1)).astype(BF)
    member_t = (
        frames[None, :] == lax.broadcasted_iota(jnp.int32, (FR, tokens), 0)
    )
    counts = jnp.sum(member_t.astype(F32), axis=1)
    member_t = jnp.transpose(
        member_t.astype(BF).reshape(FR, tokens // rows, rows), (1, 0, 2)
    )
    weight = (timestep[0].astype(F32) + 1.0) / NSTEPS
    lane = lax.broadcasted_iota(jnp.int32, (FR, LANES), 1)
    meta = jnp.where(lane == 0, counts[:, None], weight)
    head_ids = jnp.concatenate([head_of_frame[0], jnp.full((FR - FRAMES,), NDH, jnp.int32)])
    picked = (
        head_ids[:, None] == lax.broadcasted_iota(jnp.int32, (FR, NDH), 1)
    ).astype(F32)
    my_heads = lax.dynamic_slice_in_dim(disc_heads, me * columns, columns, axis=1)
    my_heads = jnp.pad(my_heads, ((0, 0), (0, chunk - columns)))
    head_rows = jnp.sum(picked[:, :, None] * my_heads[None], axis=1)
    if chunk == columns:
        w = teacher_w
    else:
        w = jnp.transpose(teacher_w.reshape(lw, n, columns), (1, 0, 2))
        w = jnp.pad(w, ((0, 0), (0, 0), (0, chunk - columns)))

    head_block = pl.BlockSpec((n, LANES, HS), lambda h: (0, 0, h))
    second_block = pl.BlockSpec((n, LANES, HS), lambda h: (0, 1, h))
    aug_block = pl.BlockSpec((1, tokens, LANES), lambda h: (h, 0, 0))
    square = 2 * tokens * tokens * HS

    with jax.named_scope("softmax_stats"):
        aug, r = pl.pallas_call(
            stats_kernel,
            grid=(heads,),
            in_specs=[
                head_block,
                second_block,
                pl.BlockSpec((tokens // rows, FR, rows), lambda h: (0, 0, 0)),
            ],
            out_specs=[
                aug_block,
                pl.BlockSpec((n, 1, FR, LANES), lambda h: (0, h, 0, 0)),
            ],
            out_shape=[
                jax.ShapeDtypeStruct((heads, tokens, LANES), BF),
                jax.ShapeDtypeStruct((n, heads, FR, LANES), BF),
            ],
            compiler_params=params(),
            cost_estimate=pl.CostEstimate(
                flops=heads * square, bytes_accessed=4 << 20, transcendentals=heads * tokens**2
            ),
        )(qk, qk, member_t)

    with jax.named_scope("pool_project"):
        part, pooled = pl.pallas_call(
            functools.partial(pool_kernel, n, heads, chunk),
            out_shape=[
                jax.ShapeDtypeStruct((n, FR, chunk + LANES), BF),
                jax.ShapeDtypeStruct((FR, lw), F32),
            ],
            compiler_params=params(0),
        )(r, v, meta, w)

    got = exchange(part)

    with jax.named_scope("attention_output"):
        mixed = pl.pallas_call(
            output_kernel,
            grid=(heads,),
            in_specs=[head_block, second_block, head_block, aug_block],
            out_specs=head_block,
            out_shape=jax.ShapeDtypeStruct((n, LANES, lw), BF),
            compiler_params=params(),
            cost_estimate=pl.CostEstimate(
                flops=2 * heads * square, bytes_accessed=5 << 20, transcendentals=heads * tokens**2
            ),
        )(qk, qk, v, aug)

    with jax.named_scope("discriminator"):
        send, feature, root = pl.pallas_call(
            functools.partial(middle_kernel, n, chunk, width),
            out_shape=[
                jax.ShapeDtypeStruct((n, FR, chunk + LANES), BF),
                jax.ShapeDtypeStruct((FR, chunk), F32),
                jax.ShapeDtypeStruct((FR, LANES), F32),
            ],
            compiler_params=params(0),
        )(got, head_rows)

    got_back = exchange(send)

    with jax.named_scope("pooled_gradient"):
        spread, head_part = pl.pallas_call(
            functools.partial(spread_kernel, n, chunk, width, tokens),
            out_shape=[
                jax.ShapeDtypeStruct((LANES, lw), BF),
                jax.ShapeDtypeStruct((NDH, chunk), F32),
            ],
            compiler_params=params(0),
        )(got_back, w, pooled, meta, root, feature, picked)

    latents = exchange(mixed)

    with jax.named_scope("attention_back"):
        dqk = pl.pallas_call(
            back_kernel,
            grid=(heads,),
            in_specs=[
                head_block,
                second_block,
                head_block,
                head_block,
                aug_block,
                pl.BlockSpec((tokens, LANES), lambda h: (0, 0)),
                pl.BlockSpec((LANES, HS), lambda h: (0, h)),
            ],
            out_specs=pl.BlockSpec((n, 2 * LANES, HS), lambda h: (0, 0, h)),
            out_shape=jax.ShapeDtypeStruct((n, 2 * LANES, lw), BF),
            scratch_shapes=[pltpu.VMEM((tokens, HS), F32)],
            compiler_params=params(),
            cost_estimate=pl.CostEstimate(
                flops=4 * heads * square, bytes_accessed=8 << 20, transcendentals=heads * tokens**2
            ),
        )(qk, qk, v, mixed, aug, member, spread)

    step = 1
    while step < grp:
        head_part = head_part + lax.ppermute(
            head_part, "grp", [(i, i ^ step) for i in range(grp)]
        )
        step *= 2
    high = head_part.astype(BF)
    low = (head_part - high.astype(F32)).astype(BF)
    pieces = jnp.concatenate(
        [
            r.reshape(n, heads * FR, LANES),
            jnp.broadcast_to(
                jnp.transpose(spread[:FR].reshape(FR, heads, HS), (1, 0, 2)).reshape(
                    1, heads * FR, HS
                ),
                (n, heads * FR, HS),
            ),
            jnp.broadcast_to(
                jnp.concatenate([high, low], axis=0).reshape(1, -1, LANES),
                (n, 2 * NDH * chunk // LANES, LANES),
            ),
        ],
        axis=1,
    )
    pieces = exchange(pieces)
    all_r = pieces[:, : heads * FR].reshape(n, heads, FR, LANES)
    all_spread = jnp.transpose(
        pieces[:, heads * FR : 2 * heads * FR].reshape(n, heads, FR, HS), (0, 2, 1, 3)
    ).reshape(n, FR, lw)
    gathered = pieces[:, 2 * heads * FR :].reshape(n, 2, NDH, chunk).astype(F32)
    gathered = (gathered[:, 0] + gathered[:, 1])[:, :, :columns]
    grad_heads = jnp.transpose(gathered, (1, 0, 2)).reshape(NDH, dh)

    with jax.named_scope("value_gradient"):
        out_value = pl.pallas_call(
            functools.partial(value_kernel, heads),
            grid=(n,),
            in_specs=[
                pl.BlockSpec((1, heads, FR, LANES), lambda d: (d, 0, 0, 0)),
                pl.BlockSpec((1, FR, lw), lambda d: (d, 0, 0)),
            ],
            out_specs=pl.BlockSpec((tok, lw), lambda d: (0, d)),
            out_shape=jax.ShapeDtypeStruct((tok, width), BF),
            compiler_params=params(),
        )(all_r, all_spread)

    back = exchange(dqk)

    def to_tokens(blocks):
        return jnp.transpose(blocks, (1, 0, 2)).reshape(1, tok, width)

    return (
        to_tokens(latents),
        to_tokens(back[:, :LANES]),
        to_tokens(back[:, LANES:]),
        out_value[None],
        grad_heads,
    )


def solution(mesh):
    return jax.shard_map(
        on_device,
        mesh=mesh,
        in_specs=(
            P("grp", "gen", None),
            P("grp", "gen", None),
            P("grp", "gen", None),
            P("gen", None),
            P(),
            P("grp", None),
            P("grp", None),
            P("grp"),
        ),
        out_specs=(
            P("grp", "gen", None),
            P("grp", "gen", None),
            P("grp", "gen", None),
            P("grp", "gen", None),
            P(),
        ),
        check_vma=False,
    )
```

time: 389 us -> 237 us (0.61)
  waiting for transfers between devices: 194 us -> 112 us
  Pallas kernels: 0 us -> 41.7 us
  matrix products: 40.8 us -> 0 us
  local copies, waits for them, and re-layouts: 60.6 us -> 28.8 us
  blocking collectives: 18.5 us -> 0 us
  between operations: 15 us -> 1.62 us
  other arithmetic: 14.1 us -> 6.04 us
    psum x2 -> x0, waiting for transfers between devices: 100 us -> none  [the longest x1 66.9 us: on_device(): lax.psum(project_part.astype(jnp.bfloat16), 'gen').astype(jnp.float32)]
    pallas_call x0 -> x7, Pallas kernels: none -> 41.7 us  [the longest x1 14.5 us: on_device(): pl.pallas_call(back_kernel, grid=(heads,), in_specs=[head_block, second_b...]
    dot_general x19 -> x0, matrix products: 40.8 us -> none  [the longest x2 5.11 us: backward_rows(): jnp.einsum('rhd,thd->hrt', grad_rows, value_three, preferred_element_type...]
    all_to_all x11 -> x0, local copies, waits for them, and re-layouts: 18.9 us -> none  [the longest x2 4.02 us: on_device(): lax.all_to_all(grads[1], 'gen', split_axis=0, concat_axis=1, tiled=True)]
    psum x1 -> x0, blocking collectives: 18.5 us -> none  [on_device(): lax.psum(square_part.astype(jnp.bfloat16), 'gen').astype(jnp.float32)]
    while x45 -> x0, local copies, waits for them, and re-layouts: 15.7 us -> none  [the longest x5 11.6 us: on_device(): lax.map(forward_block, head_query.reshape(block_count, row_block, heads_d...]
    all_to_all x7, waiting for transfers between devices: 93.5 us -> 108 us  [exchange(): return lax.all_to_all(array, 'gen', split_axis=0, concat_axis=0, tiled=True)]
    gather x2 -> x0, local copies, waits for them, and re-layouts: 7.79 us -> none  [on_device(): jnp.take(spread, frames, axis=0)]
  transfers between devices with their start and end apart: 9 -> 9, of which waited for: 7 -> 7; matrix products, arithmetic and copies ran while one was open for 18% -> 5% of each run, Pallas kernels for 0% -> 16%
where the time goes in v1:
time: 237 us; the launch traced here: 233 us
  waiting for transfers between devices  112 us (47%)
  starting transfers between devices  43.1 us (18%)
  Pallas kernels  41.7 us (18%)
  local copies, waits for them, and re-layouts  28.8 us (12%)
  other arithmetic  6.04 us (3%)
    all_to_all x7, waiting for transfers between devices, exchange(): return lax.all_to_all(array, 'gen', split_axis=0, concat_axis=0, tiled=True)  108 us
    all_to_all x7, starting transfers between devices, exchange(): return lax.all_to_all(array, 'gen', split_axis=0, concat_axis=0, tiled=True)  41.5 us
    unnamed x47, local copies, waits for them, and re-layouts  19.6 us
    pallas_call x1, Pallas kernels, on_device(): pl.pallas_call(back_kernel, grid=(heads,), in_specs=[head_block, second_b...  14.5 us
    pallas_call x1, Pallas kernels, on_device(): pl.pallas_call(stats_kernel, grid=(heads,), in_specs=[head_block, second_...  9.92 us
    pallas_call x1, Pallas kernels, on_device(): pl.pallas_call(output_kernel, grid=(heads,), in_specs=[head_block, second...  5.92 us
    transpose x4, local copies, waits for them, and re-layouts, to_tokens(): return jnp.transpose(blocks, (1, 0, 2)).reshape(1, tok, width)  5.48 us
  transfers between devices with their start and end apart: 9, of which 7 were waited for; matrix products, arithmetic and copies ran while one was open for 5% of the time, Pallas kernels for 16%

profile of v1, /device:TPU:8, one launch (start us, length us, event | category | flops | bytes accessed | tf_op | source)
XLA Modules:
  0.0 232.8 jit_solution(14562026879314902966)
XLA Ops:
  0.6 0.0 copy-start
  0.7 1.7 copy.29
  2.4 0.5 copy.30
  2.9 0.7 copy.31
  3.6 0.5 copy.32
  4.1 1.6 pad_maximum_fusion
  5.7 6.3 %all-to-all-start = ((bf16[8,256,512]{2,1,0:T(8,128)(2,1)}), bf16[8,256,512]{2,1,0:T(8,128)(2,1)S(1)}, u32[]{:S(2)}, u32[]{:S(2)}) async-start(bf16[8,256,512]{2,1,0:T(8,128)(2,1)} %pad_maximum_fusion), calls=%async_computation | async-start | bytes 4194304 | tf_op jit(solution)/shard_map/all_to_all | solution.py:261
  12.0 1.6 copy.33
  13.6 0.0 copy-start.18
  13.6 1.3 copy.34
  14.9 42.8 %all-to-all-done.q_ref.k_ref = bf16[8,256,512]{2,1,0:T(8,128)(2,1)S(1)} async-done(((bf16[8,256,512]{2,1,0:T(8,128)(2,1)}), bf16[8,256,512]{2,1,0:T(8,128)(2,1)S(1)}, u32[]{:S(2)}, u32[]{:S(2)}) %all-to-all-start) | async-done | bytes 2097184 | tf_op jit(solution)/shard_map/all_to_all | solution.py:261
  57.8 6.1 %all-to-all-start.1 = ((bf16[8,128,512]{2,1,0:T(8,128)(2,1)}), bf16[8,128,512]{2,1,0:T(8,128)(2,1)S(1)}, u32[]{:S(2)}, u32[]{:S(2)}) async-start(bf16[8,128,512]{2,1,0:T(8,128)(2,1)} %bitcast.43), calls=%async_computation.1 | async-start | bytes 2097152 | tf_op jit(solution)/shard_map/all_to_all | solution.py:261
  64.5 0.5 broadcast.25
  65.0 0.7 reduce.3
  65.7 0.1 convert_reduce_fusion
  65.9 0.1 broadcast_select_fusion.meta_ref
  66.0 9.9 %softmax_stats.1 = (bf16[4,1024,128]{2,1,0:T(8,128)(2,1)S(1)}, bf16[8,4,24,128]{3,2,1,0:T(8,128)(2,1)S(1)}) custom-call(bf16[8,256,512]{2,1,0:T(8,128)(2,1)S(1)} %all-to-all-done.q_ref.k_ref, bf16[8,256,512]{2,1,0:T(8,128)(2,1)S(1)} %all-to-all-done.q_ref.k_ref, bf16[4,24,256]{2,1,0:T(8,128)(2,1)S(1)} %fusion.1.mt_ref), custom_call_target="tpu_custom_call" | custom-call | flops 1073741824 | bytes 4194304 | tf_op jit(solution)/shard_map/softmax_stats/pallas_call | solution.py:317
  75.9 0.0 copy-start.12
  75.9 1.0 copy-done.12
  76.9 10.6 %all-to-all-done.1.v_ref = bf16[8,128,512]{2,1,0:T(8,128)(2,1)S(1)} async-done(((bf16[8,128,512]{2,1,0:T(8,128)(2,1)}), bf16[8,128,512]{2,1,0:T(8,128)(2,1)S(1)}, u32[]{:S(2)}, u32[]{:S(2)}) %all-to-all-start.1) | async-done | bytes 1048608 | tf_op jit(solution)/shard_map/all_to_all | solution.py:261
  87.4 3.7 %pool_project.1 = (bf16[8,24,768]{2,1,0:T(8,128)(2,1)S(1)}, f32[24,512]{1,0:T(8,128)S(1)}) custom-call(bf16[8,4,24,128]{3,2,1,0:T(8,128)(2,1)S(1)} %get-tuple-element.15.r_ref, bf16[8,128,512]{2,1,0:T(8,128)(2,1)S(1)} %all-to-all-done.1.v_ref, f32[24,128]{1,0:T(8,128)S(1)} %broadcast_select_fusion.meta_ref, bf16[512,5120]{1,0:T(8,128)(2,1)} %w_ref.3), custom_call_target="tpu_custom_call" | custom-call | tf_op jit(solution)/shard_map/pool_project/pallas_call | solution.py:340
  91.2 0.0 copy-start.5
  91.2 0.7 copy-done.5
  91.9 0.6 copy-done.10
  92.5 6.3 %all-to-all-start.3 = ((bf16[8,24,768]{2,1,0:T(8,128)(2,1)}), bf16[8,24,768]{2,1,0:T(8,128)(2,1)}, u32[]{:S(2)}, u32[]{:S(2)}) async-start(bf16[8,24,768]{2,1,0:T(8,128)(2,1)} %copy-done.5), calls=%async_computation.3 | async-start | bytes 589824 | tf_op jit(solution)/shard_map/all_to_all | solution.py:261
  98.9 0.1 fusion.2.picked_ref
  98.9 0.8 multiply_reduce_fusion.rows_ref
  99.8 7.7 %all-to-all-done.3.got_ref = bf16[8,24,768]{2,1,0:T(8,128)(2,1)} async-done(((bf16[8,24,768]{2,1,0:T(8,128)(2,1)}), bf16[8,24,768]{2,1,0:T(8,128)(2,1)}, u32[]{:S(2)}, u32[]{:S(2)}) %all-to-all-start.3) | async-done | bytes 294944 | tf_op jit(solution)/shard_map/all_to_all | solution.py:261
  107.4 0.8 copy-done.7
  108.3 1.2 discriminator.1
  109.5 0.7 copy-done.6
  110.2 0.6 copy-done.8
  110.8 4.9 %all-to-all-start.4 = ((bf16[8,24,768]{2,1,0:T(8,128)(2,1)}), bf16[8,24,768]{2,1,0:T(8,128)(2,1)}, u32[]{:S(2)}, u32[]{:S(2)}) async-start(bf16[8,24,768]{2,1,0:T(8,128)(2,1)} %copy-done.6), calls=%async_computation.4 | async-start | bytes 589824 | tf_op jit(solution)/shard_map/all_to_all | solution.py:261
  115.7 1.2 copy-done.13
  117.0 5.9 %attention_output.1.o_ref = bf16[8,128,512]{2,1,0:T(8,128)(2,1)S(1)} custom-call(bf16[8,256,512]{2,1,0:T(8,128)(2,1)S(1)} %all-to-all-done.q_ref.k_ref, bf16[8,256,512]{2,1,0:T(8,128)(2,1)S(1)} %all-to-all-done.q_ref.k_ref, bf16[8,128,512]{2,1,0:T(8,128)(2,1)S(1)} %all-to-all-done.1.v_ref, bf16[4,1024,128]{2,1,0:T(8,128)(2,1)S(1)} %copy-done.13), custom_call_target="tpu_custom_call" | custom-call | flops 2147483648 | bytes 5242880 | tf_op jit(solution)/shard_map/attention_output/pallas_call | solution.py:352
  122.9 1.0 copy-done.3
  123.9 6.2 %all-to-all-start.2 = ((bf16[8,128,512]{2,1,0:T(8,128)(2,1)}), bf16[8,128,512]{2,1,0:T(8,128)(2,1)}, u32[]{:S(2)}, u32[]{:S(2)}) async-start(bf16[8,128,512]{2,1,0:T(8,128)(2,1)} %copy-done.3), calls=%async_computation.2 | async-start | bytes 2097152 | tf_op jit(solution)/shard_map/all_to_all | solution.py:261
  130.1 2.5 %copy-done.1 = bf16[512,5120]{1,0:T(8,128)(2,1)S(1)} copy-done((bf16[512,5120]{1,0:T(8,128)(2,1)S(1)}, bf16[512,5120]{1,0:T(8,128)(2,1)}, u32[]{:S(2)}) %copy-start.1) | copy-done | bytes 5242904
  132.5 2.7 %pooled_gradient.1 = (bf16[128,512]{1,0:T(8,128)(2,1)S(1)}, f32[8,640]{1,0:T(8,128)S(1)}) custom-call(bf16[8,24,768]{2,1,0:T(8,128)(2,1)} %all-to-all-done.4.got_ref, bf16[512,5120]{1,0:T(8,128)(2,1)S(1)} %copy-done.1, f32[24,512]{1,0:T(8,128)S(1)} %copy-done.11, f32[24,128]{1,0:T(8,128)S(1)} %broadcast_select_fusion.meta_ref, ...), custom_call_target="tpu_custom_call" | custom-call | tf_op jit(solution)/shard_map/pooled_gradient/pallas_call | solution.py:378
  135.2 0.1 collective-permute-start
  135.3 1.2 collective-permute-done
  136.5 1.5 collective-permute-start.1
  138.0 2.3 collective-permute-done.1
  140.4 0.8 pad_maximum_fusion.1
  141.3 11.3 %all-to-all-done.2 = bf16[8,128,512]{2,1,0:T(8,128)(2,1)} async-done(((bf16[8,128,512]{2,1,0:T(8,128)(2,1)}), bf16[8,128,512]{2,1,0:T(8,128)(2,1)}, u32[]{:S(2)}, u32[]{:S(2)}) %all-to-all-start.2) | async-done | bytes 1048608 | tf_op jit(solution)/shard_map/all_to_all | solution.py:261
  152.6 5.7 %all-to-all-start.6 = ((bf16[8,272,128]{2,1,0:T(8,128)(2,1)}), bf16[8,272,128]{2,1,0:T(8,128)(2,1)S(1)}, u32[]{:S(2)}, u32[]{:S(2)}) async-start(bf16[8,272,128]{2,1,0:T(8,128)(2,1)} %pad_maximum_fusion.1), calls=%async_computation.6 | async-start | bytes 1114112 | tf_op jit(solution)/shard_map/all_to_all | solution.py:261
  158.2 0.2 fusion.m_ref
  158.5 1.2 copy-done.14
  159.7 14.5 %attention_back.1 = bf16[8,256,512]{2,1,0:T(8,128)(2,1)} custom-call(bf16[8,256,512]{2,1,0:T(8,128)(2,1)} %copy-done.2, bf16[8,256,512]{2,1,0:T(8,128)(2,1)} %copy-done.2, bf16[8,128,512]{2,1,0:T(8,128)(2,1)S(1)} %all-to-all-done.1.v_ref, bf16[8,128,512]{2,1,0:T(8,128)(2,1)S(1)} %copy-done.4, bf16[4,1024,128]{2,1,0:T(8,128)(2,1)S(1)} %copy-done.14, ...), custom_call_target="tpu_custom_call" | custom-call | flops 4294967296 | bytes 8388608 | tf_op jit(solution)/shard_map/attention_back/pallas_call | solution.py:390
  174.2 0.8 copy-done.16
  175.0 6.0 %all-to-all-start.5 = ((bf16[8,256,512]{2,1,0:T(8,128)(2,1)}), bf16[8,256,512]{2,1,0:T(8,128)(2,1)S(1)}, u32[]{:S(2)}, u32[]{:S(2)}) async-start(bf16[8,256,512]{2,1,0:T(8,128)(2,1)} %attention_back.1), calls=%async_computation.5 | async-start | bytes 4194304 | tf_op jit(solution)/shard_map/all_to_all | solution.py:261
  181.1 1.6 copy.35
  182.7 1.3 copy.40
  184.0 1.0 fusion.3
  185.1 0.9 slice_convert_fusion
  186.0 0.1 reshape.89
  186.1 3.7 %value_gradient.1 = bf16[128,4096]{1,0:T(8,128)(2,1)} custom-call(bf16[8,4,24,128]{3,2,1,0:T(8,128)(2,1)S(1)} %bitcast.42, bf16[8,24,512]{2,1,0:T(8,128)(2,1)S(1)} %bitcast.41), custom_call_target="tpu_custom_call" | custom-call | tf_op jit(solution)/shard_map/value_gradient/pallas_call | solution.py:445
  189.8 0.7 slice_add_fusion
  190.5 35.8 %all-to-all-done.5 = bf16[8,256,512]{2,1,0:T(8,128)(2,1)S(1)} async-done(((bf16[8,256,512]{2,1,0:T(8,128)(2,1)}), bf16[8,256,512]{2,1,0:T(8,128)(2,1)S(1)}, u32[]{:S(2)}, u32[]{:S(2)}) %all-to-all-start.5) | async-done | bytes 2097184 | tf_op jit(solution)/shard_map/all_to_all | solution.py:261
  226.3 1.5 slice_bitcast_fusion
  227.8 1.7 copy.37
  229.5 1.3 copy.42
  230.8 0.7 copy.36
  231.5 1.3 copy.41
  (40 shorter events, 0.2 us)
Async XLA Ops:
  0.6 98.2 %copy-start = (f32[8,5120]{1,0:T(8,128)S(1)}, f32[8,5120]{1,0:T(8,128)}, u32[]{:S(2)}) copy-start(f32[8,5120]{1,0:T(8,128)} %param.12) | copy-start | bytes 491524
  0.6 2.3 copy-start.17
  5.7 52.1 %all-to-all-start = ((bf16[8,256,512]{2,1,0:T(8,128)(2,1)}), bf16[8,256,512]{2,1,0:T(8,128)(2,1)S(1)}, u32[]{:S(2)}, u32[]{:S(2)}) async-start(bf16[8,256,512]{2,1,0:T(8,128)(2,1)} %pad_maximum_fusion), calls=%async_computation | async-start | bytes 4194304 | tf_op jit(solution)/shard_map/all_to_all | solution.py:261
  13.6 51.4 %copy-start.18 = (s32[1,1024]{1,0:T(1,128)S(1)}, s32[1,1024]{1,0:T(1,128)}, u32[]{:S(2)}) copy-start(s32[1,1024]{1,0:T(1,128)} %param.13) | copy-start | bytes 12292
  57.8 58.0 %copy-start.2 = (bf16[8,256,512]{2,1,0:T(8,128)(2,1)}, bf16[8,256,512]{2,1,0:T(8,128)(2,1)S(1)}, u32[]{:S(2)}) copy-start(bf16[8,256,512]{2,1,0:T(8,128)(2,1)S(1)} %all-to-all-done.q_ref.k_ref) | copy-start | bytes 6291460
  57.8 29.7 %all-to-all-start.1 = ((bf16[8,128,512]{2,1,0:T(8,128)(2,1)}), bf16[8,128,512]{2,1,0:T(8,128)(2,1)S(1)}, u32[]{:S(2)}, u32[]{:S(2)}) async-start(bf16[8,128,512]{2,1,0:T(8,128)(2,1)} %bitcast.43), calls=%async_computation.1 | async-start | bytes 2097152 | tf_op jit(solution)/shard_map/all_to_all | solution.py:261
  75.9 1.0 copy-start.12
  87.4 11.4 %copy-start.19 = (s32[1,21]{1,0:T(1,128)S(1)}, s32[1,21]{1,0:T(1,128)}, u32[]{:S(2)}) copy-start(s32[1,21]{1,0:T(1,128)} %param.14) | copy-start | bytes 256
  91.2 0.7 copy-start.5
  91.9 0.6 copy-start.10
  92.5 14.9 %all-to-all-start.3 = ((bf16[8,24,768]{2,1,0:T(8,128)(2,1)}), bf16[8,24,768]{2,1,0:T(8,128)(2,1)}, u32[]{:S(2)}, u32[]{:S(2)}) async-start(bf16[8,24,768]{2,1,0:T(8,128)(2,1)} %copy-done.5), calls=%async_computation.3 | async-start | bytes 589824 | tf_op jit(solution)/shard_map/all_to_all | solution.py:261
  107.4 0.8 copy-start.7
  109.4 0.7 copy-start.6
  110.2 0.6 copy-start.8
  110.8 13.1 %all-to-all-start.4 = ((bf16[8,24,768]{2,1,0:T(8,128)(2,1)}), bf16[8,24,768]{2,1,0:T(8,128)(2,1)}, u32[]{:S(2)}, u32[]{:S(2)}) async-start(bf16[8,24,768]{2,1,0:T(8,128)(2,1)} %copy-done.6), calls=%async_computation.4 | async-start | bytes 589824 | tf_op jit(solution)/shard_map/all_to_all | solution.py:261
  115.7 1.2 copy-start.13
  122.9 1.0 copy-start.3
  123.9 6.2 %copy-start.9 = (f32[24,640]{1,0:T(8,128)S(1)}, f32[24,640]{1,0:T(8,128)}, u32[]{:S(2)}) copy-start(f32[24,640]{1,0:T(8,128)} %copy-done.8) | copy-start | bytes 184324
  123.9 6.2 %copy-start.11 = (f32[24,512]{1,0:T(8,128)S(1)}, f32[24,512]{1,0:T(8,128)}, u32[]{:S(2)}) copy-start(f32[24,512]{1,0:T(8,128)} %copy-done.10) | copy-start | bytes 147460
  123.9 28.7 %all-to-all-start.2 = ((bf16[8,128,512]{2,1,0:T(8,128)(2,1)}), bf16[8,128,512]{2,1,0:T(8,128)(2,1)}, u32[]{:S(2)}, u32[]{:S(2)}) async-start(bf16[8,128,512]{2,1,0:T(8,128)(2,1)} %copy-done.3), calls=%async_computation.2 | async-start | bytes 2097152 | tf_op jit(solution)/shard_map/all_to_all | solution.py:261
  130.0 2.5 %copy-start.1 = (bf16[512,5120]{1,0:T(8,128)(2,1)S(1)}, bf16[512,5120]{1,0:T(8,128)(2,1)}, u32[]{:S(2)}) copy-start(bf16[512,5120]{1,0:T(8,128)(2,1)} %w_ref.3) | copy-start | bytes 15728644
  135.2 23.2 %copy-start.4 = (bf16[8,128,512]{2,1,0:T(8,128)(2,1)S(1)}, bf16[8,128,512]{2,1,0:T(8,128)(2,1)}, u32[]{:S(2)}) copy-start(bf16[8,128,512]{2,1,0:T(8,128)(2,1)} %copy-done.3) | copy-start | bytes 3145732
  135.2 1.3 collective-permute-start
  136.5 3.8 %collective-permute-start.1 = (f32[8,640]{1,0:T(8,128)S(1)}, f32[8,640]{1,0:T(8,128)S(1)}, u32[]{:S(2)}, u32[]{:S(2)}) collective-permute-start(f32[8,640]{1,0:T(8,128)S(1)} %add.23), channel_id=1, source_target_pairs={{0,2},{1,3},{2,0},{3,1},{4,6},{5,7},{6,4},{7,5},{8,10},{9,11},{10,... | collective-permute-start | bytes 61448 | tf_op jit(solution)/shard_map/ppermute | solution.py:413
  152.6 21.7 %all-to-all-start.6 = ((bf16[8,272,128]{2,1,0:T(8,128)(2,1)}), bf16[8,272,128]{2,1,0:T(8,128)(2,1)S(1)}, u32[]{:S(2)}, u32[]{:S(2)}) async-start(bf16[8,272,128]{2,1,0:T(8,128)(2,1)} %pad_maximum_fusion.1), calls=%async_computation.6 | async-start | bytes 1114112 | tf_op jit(solution)/shard_map/all_to_all | solution.py:261
  158.5 1.2 copy-start.14
  174.2 0.8 copy-start.16
  175.0 51.3 %all-to-all-start.5 = ((bf16[8,256,512]{2,1,0:T(8,128)(2,1)}), bf16[8,256,512]{2,1,0:T(8,128)(2,1)S(1)}, u32[]{:S(2)}, u32[]{:S(2)}) async-start(bf16[8,256,512]{2,1,0:T(8,128)(2,1)} %attention_back.1), calls=%async_computation.5 | async-start | bytes 4194304 | tf_op jit(solution)/shard_map/all_to_all | solution.py:261
  227.8 3.0 %copy-start.15 = (bf16[128,8,512]{2,0,1:T(8,128)(2,1)S(1)}, bf16[128,8,512]{2,0,1:T(8,128)(2,1)}, u32[]{:S(2)}) copy-start(bf16[128,8,512]{2,0,1:T(8,128)(2,1)} %get-tuple-element.34) | copy-start | bytes 3145732

commit v2 on v1

v2 whole, which is shorter than its diff:
```python
import functools
import math

import jax
import jax.numpy as jnp
from jax import lax
from jax.experimental import pallas as pl
from jax.experimental.pallas import tpu as pltpu
from jax.sharding import PartitionSpec as P

HS = 128
FRAMES = 21
FR = 24
RR = 32
NDH = 8
NSTEPS = 1000
LANES = 128
epsilon = 1e-06
SCALE = 1.0 / math.sqrt(HS)
LOG2E = math.log2(math.e)
BF = jnp.bfloat16
F32 = jnp.float32


def params(tokens, axes=1):
    return pltpu.CompilerParams(
        vmem_limit_bytes=min(48, 16 * -(-tokens // 1024)) * 1024 * 1024,
        dimension_semantics=("arbitrary",) * axes,
    )


def hbm(array):
    return pltpu.with_memory_space_constraint(array, pltpu.HBM)


def after(value, *earlier):
    return lax.optimization_barrier((value,) + earlier)[0]


def dot_nn(a, b):
    return lax.dot_general(a, b, (((1,), (0,)), ((), ())), preferred_element_type=F32)


def dot_nt(a, b):
    return lax.dot_general(a, b, (((1,), (1,)), ((), ())), preferred_element_type=F32)


def dot_tn(a, b):
    return lax.dot_general(a, b, (((0,), (0,)), ((), ())), preferred_element_type=F32)


def rows_of(ref):
    block = ref[...]
    return block.reshape(block.shape[-3] * block.shape[-2], block.shape[-1])


def split_three(value):
    high = value.astype(BF)
    rest = value - high.astype(F32)
    middle = rest.astype(BF)
    low = (rest - middle.astype(F32)).astype(BF)
    return high, middle, low


def lanes_three(value, shape, first):
    lane = lax.broadcasted_iota(jnp.int32, shape, 1)
    out = jnp.zeros(shape, F32)
    for i, part in enumerate(split_three(value)):
        out = jnp.where(lane == first + i, part.astype(F32), out)
    return out


def ones_three(shape):
    lane = lax.broadcasted_iota(jnp.int32, shape, 1)
    return jnp.where(lane < 3, 1.0, 0.0).astype(BF)


def take_lanes(block, first, count):
    lane = lax.broadcasted_iota(jnp.int32, block.shape, 1)
    keep = (lane >= first) & (lane < first + count)
    return jnp.sum(jnp.where(keep, block, 0.0), axis=1, keepdims=True)


def row_chunk(tokens):
    return min(256, tokens)


def run_steps(count, step, carry):
    if count <= 4:
        for i in range(count):
            carry = step(i, carry)
        return carry
    return lax.fori_loop(0, count, step, carry)


def chunk_rows(i, chunk):
    return pl.ds(pl.multiple_of(i * chunk, chunk), chunk)


def stats_kernel(blocks, *refs):
    qk_refs, (mt_ref, aug_ref, r_ref, q_ref, k_ref) = refs[:blocks], refs[blocks:]
    tokens = blocks * LANES
    chunk = row_chunk(tokens)
    for s in range(blocks):
        at = slice(s * LANES, (s + 1) * LANES)
        q_ref[0, at] = qk_refs[s][0]
        k_ref[0, at] = qk_refs[s][1]
    keys = k_ref[0]

    def step(i, total_r):
        at = chunk_rows(i, chunk)
        s = dot_nt(q_ref[0, at], keys) * (SCALE * LOG2E)
        peak = jnp.max(s, axis=1, keepdims=True)
        e = jnp.exp2(s - peak)
        total = jnp.sum(e, axis=1, keepdims=True)
        p = (e * (1.0 / total)).astype(BF)
        lse = (peak + jnp.log2(total)) * (-1.0 / (SCALE * LOG2E))
        aug_ref[0, at] = lanes_three(lse, (chunk, LANES), 0).astype(BF)
        return total_r + dot_nn(mt_ref[i], p)

    r = run_steps(tokens // chunk, step, jnp.zeros((RR, tokens), F32))
    for s in range(blocks):
        r_ref[s, 0] = r[:, s * LANES : (s + 1) * LANES].astype(BF)


def pool_kernel(blocks, heads, chunk, *refs):
    v_refs, (r_ref, meta_ref, w_hbm, part_ref, pooled_ref, w_ref, sems) = (
        refs[:blocks],
        refs[blocks:],
    )
    copies = start_weights(w_hbm, w_ref, sems, blocks, chunk)
    count = jnp.maximum(take_lanes(meta_ref[...], 0, 1), 1.0)
    columns = []
    for h in range(heads):
        r = jnp.concatenate([r_ref[s, h] for s in range(blocks)], axis=1)
        v = jnp.concatenate(
            [v_refs[s][:, h * HS : (h + 1) * HS] for s in range(blocks)], axis=0
        )
        columns.append(dot_nn(r, v)[:FR])
    pooled = jnp.concatenate(columns, axis=1) if heads > 1 else columns[0]
    pooled = pooled / count
    pooled_ref[...] = pooled
    squares = jnp.sum(pooled * pooled, axis=1, keepdims=True)
    stats = lanes_three(squares, (FR, LANES), 0).astype(BF)
    rounded = pooled.astype(BF)
    for d in range(blocks):
        copies[d].wait()
        part_ref[d, :, :chunk] = dot_nn(rounded, w_ref[d]).astype(BF)
        part_ref[d, :, chunk:] = stats


def start_weights(w_hbm, w_ref, sems, blocks, chunk):
    copies = []
    for d in range(blocks):
        if len(w_hbm.shape) == 3:
            source = w_hbm.at[d]
        else:
            source = w_hbm.at[:, d * chunk : (d + 1) * chunk]
        copies.append(pltpu.make_async_copy(source, w_ref.at[d], sems.at[d]))
        copies[d].start()
    return copies


def middle_kernel(blocks, chunk, width, got_ref, rows_ref, send_ref, feature_ref, root_ref):
    total = got_ref[0].astype(F32)
    for d in range(1, blocks):
        total = total + got_ref[d].astype(F32)
    projected = total[:, :chunk]
    squares = take_lanes(total[:, chunk:], 0, 3)
    root = jnp.sqrt(squares / width + epsilon)
    pre = projected / root
    gate = jax.nn.sigmoid(pre)
    feature = pre * gate
    head_rows = rows_ref[...]
    direction = head_rows * gate * (1.0 + pre * (1.0 - gate))
    score = jnp.sum(feature * head_rows, axis=1, keepdims=True)
    slope = jnp.sum(direction * pre, axis=1, keepdims=True)
    stats = (
        lanes_three(score, (FR, LANES), 0) + lanes_three(slope, (FR, LANES), 3)
    ).astype(BF)
    rounded = direction.astype(BF)
    for d in range(blocks):
        send_ref[d, :, :chunk] = rounded
        send_ref[d, :, chunk:] = stats
    feature_ref[...] = feature
    root_ref[...] = jnp.broadcast_to(root, (FR, LANES))


def spread_kernel(
    blocks,
    chunk,
    width,
    tokens,
    got_ref,
    w_hbm,
    pooled_ref,
    meta_ref,
    root_ref,
    feature_ref,
    picked_ref,
    spread_ref,
    heads_ref,
    w_ref,
    sems,
):
    copies = start_weights(w_hbm, w_ref, sems, blocks, chunk)
    meta = meta_ref[...]
    count = jnp.maximum(take_lanes(meta, 0, 1), 1.0)
    weight = take_lanes(meta, 1, 1)
    root = take_lanes(root_ref[...], 0, 1)
    stats = got_ref[0, :, chunk:].astype(F32)
    for d in range(1, blocks):
        stats = stats + got_ref[d, :, chunk:].astype(F32)
    score = take_lanes(stats, 0, 3)
    slope = take_lanes(stats, 3, 3)
    grad_score = -weight * jax.nn.sigmoid(-score) / FRAMES
    total = jnp.zeros(pooled_ref.shape, F32)
    for d in range(blocks):
        copies[d].wait()
        total = total + dot_nt(got_ref[d, :, :chunk], w_ref[d])
    grad_root = -(grad_score * slope) / root
    grad_pooled = (grad_score / root) * total + (grad_root / root / width) * pooled_ref[...]
    spread_ref[:FR] = (tokens * (grad_pooled / count)).astype(BF)
    spread_ref[FR:] = jnp.zeros((LANES - FR, pooled_ref.shape[1]), BF)
    scaled = feature_ref[...] * grad_score
    picked = picked_ref[...]
    for j in range(NDH):
        heads_ref[j : j + 1, :] = jnp.sum(scaled * picked[:, j : j + 1], axis=0, keepdims=True)


def output_kernel(blocks, *refs):
    v_refs, (q_ref, k_ref, aug_ref, r_ref) = refs[:blocks], refs[blocks : blocks + 4]
    send_refs, (v_ref, o_ref) = refs[blocks + 4 : -2], refs[-2:]
    tokens = blocks * LANES
    chunk = row_chunk(tokens)
    for s in range(blocks):
        v_ref[0, s * LANES : (s + 1) * LANES] = v_refs[s][...]
    keys = jnp.concatenate([k_ref[0], ones_three((tokens, LANES))], axis=1)
    values = v_ref[0]

    def step(i, carry):
        at = chunk_rows(i, chunk)
        s = dot_nt(jnp.concatenate([q_ref[0, at], aug_ref[0, at]], axis=1), keys)
        p = jnp.exp2(s * (SCALE * LOG2E)).astype(BF)
        o_ref[0, at] = dot_nn(p, values).astype(BF)
        return carry

    run_steps(tokens // chunk, step, 0)
    for s in range(blocks):
        send_refs[s][:LANES] = o_ref[0, s * LANES : (s + 1) * LANES]
        send_refs[s][LANES:] = r_ref[s, 0]


def back_kernel(
    blocks, apart, q_ref, k_ref, v_ref, o_ref, aug_ref, m_ref, spread_ref, extra_ref, *refs
):
    out_refs, dk_ref, dq_ref = refs[:-2], refs[-2], refs[-1]
    tokens = blocks * LANES
    chunk = row_chunk(tokens)
    plain = k_ref[0]
    keys = jnp.concatenate([plain, ones_three((tokens, LANES))], axis=1)
    values = v_ref[0]
    spread = spread_ref[...]
    dk_ref[...] = jnp.zeros(dk_ref.shape, F32)

    def step(i, carry):
        at = chunk_rows(i, chunk)
        q = q_ref[0, at]
        s = dot_nt(jnp.concatenate([q, aug_ref[0, at]], axis=1), keys)
        p = jnp.exp2(s * (SCALE * LOG2E))
        grad = dot_nn(m_ref[at], spread)
        delta = jnp.sum(grad * o_ref[0, at].astype(F32), axis=1, keepdims=True)
        dp = dot_nt(grad.astype(BF), values)
        ds = (p * (dp - delta)).astype(BF)
        dq_ref[at] = (dot_nn(ds, plain) * SCALE).astype(BF)
        dk_ref[...] += dot_tn(ds, q)
        return carry

    run_steps(tokens // chunk, step, 0)
    dk = (dk_ref[...] * SCALE).astype(BF)
    me = lax.axis_index("gen")
    for s in range(blocks):
        at = slice(s * LANES, (s + 1) * LANES)
        out_ref = out_refs[s] if apart else out_refs[0].at[me ^ s]
        out_ref[:LANES] = dq_ref[at]
        out_ref[LANES : 2 * LANES] = dk[at]
        out_ref[2 * LANES : 2 * LANES + RR] = spread[:RR]
        if apart:
            out_ref[2 * LANES + RR :] = extra_ref[...]


def received(blocks, near_refs, far_refs, s):
    near = len(near_refs)
    if s < near:
        return [near_refs[s]]
    return [far_refs[i + s - near] for i in range(0, len(far_refs), blocks - near)]


def latent_kernel(blocks, lw, *refs):
    near = blocks - blocks // 2
    me = lax.axis_index("gen")
    for s in range(blocks):
        first = 0
        for ref in received(blocks, refs[:near], refs[near:-1], s):
            at = pl.ds(pl.multiple_of((me ^ s) * lw + first, LANES), ref.shape[1])
            refs[-1][:, at] = ref[:LANES]
            first += ref.shape[1]


def finish_kernel(blocks, lw, chunk, near, far, split, *refs):
    near_refs, far_refs = refs[:near], refs[near : near + far]
    late_refs, early_refs = refs[near + far :][:blocks], refs[near + far + blocks : -4]
    dq_ref, dk_ref, dv_ref, heads_ref = refs[-4:]
    me = lax.axis_index("gen")
    first = split * HS
    last = lw - first
    for s in range(blocks):
        d = me ^ s
        late = late_refs[s]
        at = pl.ds(pl.multiple_of(d * lw + first, LANES), last)
        dq_ref[:, at] = late[:LANES]
        dk_ref[:, at] = late[LANES : 2 * LANES]
        spreads = [late[2 * LANES : 2 * LANES + RR]]
        if split:
            at = pl.ds(pl.multiple_of(d * lw, LANES), first)
            early = early_refs[0].at[d]
            dq_ref[:, at] = early[:LANES]
            dk_ref[:, at] = early[LANES : 2 * LANES]
            spreads = [early[2 * LANES : 2 * LANES + RR]] + spreads
        rows = [ref[LANES:] for ref in received(blocks, near_refs, far_refs, s)]
        rows = jnp.concatenate(rows, axis=1) if len(rows) > 1 else rows[0]
        spread = jnp.concatenate(spreads, axis=1) if split else spreads[0]
        parts = [
            dot_tn(rows[:, h : h + HS], spread[:, h : h + HS]).astype(BF)
            for h in range(0, lw, HS)
        ]
        at = pl.ds(pl.multiple_of(d * lw, LANES), lw)
        dv_ref[:, at] = jnp.concatenate(parts, axis=1) if len(parts) > 1 else parts[0]
        per = last // LANES
        for piece in range(chunk // LANES):
            row = 2 * LANES + RR + piece // per * 2 * NDH
            lane = piece % per * LANES
            both = late[row : row + 2 * NDH, lane : lane + LANES].astype(F32)
            at = pl.ds(pl.multiple_of(d * chunk + piece * LANES, LANES), LANES)
            heads_ref[:, at] = both[:NDH] + both[NDH:]


def exchange(array):
    return lax.all_to_all(array, "gen", split_axis=0, concat_axis=0, tiled=True)


def on_device(
    query_in, key_in, value_in, teacher_w, disc_heads, frame_of_token, head_of_frame, timestep
):
    n = lax.axis_size("gen")
    grp = lax.axis_size("grp")
    me = lax.axis_index("gen")
    tok = query_in.shape[1]
    width = query_in.shape[2]
    tokens = tok * n
    heads = width // HS // n
    lw = heads * HS
    dh = teacher_w.shape[1]
    columns = dh // n
    chunk = -(-columns // LANES) * LANES
    rows = row_chunk(tokens)

    far, near = list(range(n // 2, n)), list(range(1, n // 2))
    half = len(far)

    def columns_for(array, s):
        return lax.dynamic_slice_in_dim(array, (me ^ s) * lw, lw, axis=1)

    def send(array, s):
        return lax.ppermute(array, "gen", [(i, i ^ s) for i in range(n)])

    def query_key(s):
        return jnp.stack([columns_for(query_in[0], s), columns_for(key_in[0], s)])

    qk, v = {0: query_key(0)}, {0: columns_for(value_in[0], 0)}
    blocks = {s: query_key(s) for s in far}
    for s in far:
        qk[s] = send(blocks[s], s)
    most = [qk[s] for s in far[: half - 1]]
    every = [qk[s] for s in far]
    for s in near:
        behind = [qk[s - 1]] if s > 1 else list(blocks.values())
        qk[s] = send(after(query_key(s), *behind), s)
    for s in near:
        behind = v[s - 1] if s > 1 else qk[s]
        v[s] = send(after(columns_for(value_in[0], s), behind), s)
    for i, s in enumerate(far):
        v[s] = send(after(columns_for(value_in[0], s), *(most if i < 2 else every)), s)
    qk, v = [qk[s] for s in range(n)], [v[s] for s in range(n)]

    frames = frame_of_token[0]
    frames = jnp.take(frames.reshape(n, tok), me ^ jnp.arange(n), axis=0).reshape(tokens)
    member = (frames[:, None] == lax.broadcasted_iota(jnp.int32, (tokens, LANES), 1)).astype(BF)
    member_t = (
        frames[None, :] == lax.broadcasted_iota(jnp.int32, (RR, tokens), 0)
    )
    counts = jnp.sum(member_t.astype(F32), axis=1)[:FR]
    member_t = jnp.transpose(
        member_t.astype(BF).reshape(RR, tokens // rows, rows), (1, 0, 2)
    )
    weight = (timestep[0].astype(F32) + 1.0) / NSTEPS
    lane = lax.broadcasted_iota(jnp.int32, (FR, LANES), 1)
    meta = jnp.where(lane == 0, counts[:, None], weight)
    head_ids = jnp.concatenate([head_of_frame[0], jnp.full((FR - FRAMES,), NDH, jnp.int32)])
    picked = (
        head_ids[:, None] == lax.broadcasted_iota(jnp.int32, (FR, NDH), 1)
    ).astype(F32)
    my_heads = lax.dynamic_slice_in_dim(disc_heads, me * columns, columns, axis=1)
    my_heads = jnp.pad(my_heads, ((0, 0), (0, chunk - columns)))
    head_rows = jnp.sum(picked[:, :, None] * my_heads[None], axis=1)
    if chunk == columns:
        w = teacher_w
    else:
        w = jnp.transpose(teacher_w.reshape(lw, n, columns), (1, 0, 2))
        w = jnp.pad(w, ((0, 0), (0, 0), (0, chunk - columns)))

    head_block = pl.BlockSpec((1, tokens, HS), lambda h: (h, 0, 0))
    head_shape = pltpu.HBM((heads, tokens, HS), BF)
    r_block = pl.BlockSpec((n, 1, RR, LANES), lambda h: (0, h, 0, 0))
    square = 2 * tokens * tokens * HS
    in_vmem = pl.BlockSpec(memory_space=pltpu.VMEM)
    anywhere = pl.BlockSpec(memory_space=pl.ANY)
    weights_scratch = [pltpu.VMEM((n, lw, chunk), BF), pltpu.SemaphoreType.DMA((n,))]

    with jax.named_scope("softmax_stats"):
        aug, r, q_rows, k_rows = pl.pallas_call(
            functools.partial(stats_kernel, n),
            grid=(heads,),
            in_specs=[pl.BlockSpec((2, LANES, HS), lambda h: (0, 0, h))] * n
            + [pl.BlockSpec((tokens // rows, RR, rows), lambda h: (0, 0, 0))],
            out_specs=[head_block, r_block, head_block, head_block],
            out_shape=[
                head_shape,
                pltpu.HBM((n, heads, RR, LANES), BF),
                head_shape,
                head_shape,
            ],
            compiler_params=params(tokens),
            cost_estimate=pl.CostEstimate(
                flops=heads * square, bytes_accessed=4 << 20, transcendentals=heads * tokens**2
            ),
        )(*map(hbm, qk), member_t)

    with jax.named_scope("pool_project"):
        part, pooled = pl.pallas_call(
            functools.partial(pool_kernel, n, heads, chunk),
            in_specs=[in_vmem] * (n + 2) + [anywhere],
            scratch_shapes=weights_scratch,
            out_shape=[
                jax.ShapeDtypeStruct((n, FR, chunk + LANES), BF),
                jax.ShapeDtypeStruct((FR, lw), F32),
            ],
            compiler_params=params(tokens, 0),
        )(*v, r, meta, hbm(w))

    got = exchange(part)

    split = heads // 2
    parts = [(0, split), (split, heads)] if split else [(0, heads)]

    def output(first, last, behind):
        at = pl.BlockSpec((1, tokens, HS), lambda h: (h + first, 0, 0))
        own = pltpu.HBM((last - first, tokens, HS), BF)
        with jax.named_scope("attention_output"):
            *made, v_rows, o_rows = pl.pallas_call(
                functools.partial(output_kernel, n),
                grid=(last - first,),
                in_specs=[pl.BlockSpec((LANES, HS), lambda h: (0, h + first))] * n
                + [at] * 3
                + [pl.BlockSpec((n, 1, RR, LANES), lambda h: (0, h + first, 0, 0))],
                out_specs=[pl.BlockSpec((LANES + RR, HS), lambda h: (0, h))] * n
                + [head_block, head_block],
                out_shape=[pltpu.HBM((LANES + RR, (last - first) * HS), BF)] * n + [own, own],
                compiler_params=params(tokens),
                cost_estimate=pl.CostEstimate(
                    flops=2 * (last - first) * square,
                    bytes_accessed=(last - first) << 20,
                    transcendentals=(last - first) * tokens**2,
                ),
            )(*map(hbm, v), *map(hbm, (q_rows, k_rows, aug, after(r, behind))))
        return made, v_rows, o_rows

    outputs = [output(*parts[0], part)]
    got = after(got, outputs[0][2])
    mixed = [[send(outputs[0][0][s], s) for s in far]]

    with jax.named_scope("discriminator"):
        direction, feature, root = pl.pallas_call(
            functools.partial(middle_kernel, n, chunk, width),
            out_shape=[
                jax.ShapeDtypeStruct((n, FR, chunk + LANES), BF),
                jax.ShapeDtypeStruct((FR, chunk), F32),
                jax.ShapeDtypeStruct((FR, LANES), F32),
            ],
            compiler_params=params(tokens, 0),
        )(got, head_rows)

    got_back = exchange(after(direction, *mixed[0][:2]))
    got_back = after(got_back, *mixed[0][2:])
    if split:
        outputs.append(output(*parts[1], direction))
        got_back = after(got_back, outputs[1][2])
        mixed.append([send(outputs[1][0][s], s) for s in far])
    mixed_near = []
    for s in range(n - half):
        block = jnp.concatenate([made[0][s] for made in outputs], axis=1) if split else outputs[0][0][s]
        mixed_near.append(send(block, s) if s else block)

    with jax.named_scope("pooled_gradient"):
        spread, head_part = pl.pallas_call(
            functools.partial(spread_kernel, n, chunk, width, tokens),
            in_specs=[in_vmem, anywhere] + [in_vmem] * 5,
            scratch_shapes=weights_scratch,
            out_shape=[
                jax.ShapeDtypeStruct((LANES, lw), BF),
                jax.ShapeDtypeStruct((NDH, chunk), F32),
            ],
            compiler_params=params(tokens, 0),
        )(got_back, hbm(w), pooled, meta, root, feature, picked)

    def back(i, apart, extra):
        first, last = parts[i]
        part = (last - first) * HS
        if apart:
            block = (2 * LANES + RR + extra.shape[0], HS)
        else:
            block = (n, 2 * LANES + RR, HS)
        shape = block[:-1] + (part,)
        count = n if apart else 1
        at = pl.BlockSpec((1, tokens, HS), lambda h: (h + first, 0, 0))
        with jax.named_scope("attention_back"):
            return pl.pallas_call(
                functools.partial(back_kernel, n, apart),
                grid=(last - first,),
                in_specs=[at, at, head_block, head_block, at]
                + [
                    pl.BlockSpec((tokens, LANES), lambda h: (0, 0)),
                    pl.BlockSpec((LANES, HS), lambda h: (0, h + first)),
                    pl.BlockSpec((extra.shape[0], HS), lambda h: (0, h)),
                ],
                out_specs=[pl.BlockSpec(block, lambda h: (0,) * (len(block) - 1) + (h,))] * count,
                out_shape=[pltpu.HBM(shape, BF)] * count,
                scratch_shapes=[pltpu.VMEM((tokens, HS), F32), pltpu.VMEM((tokens, HS), BF)],
                compiler_params=params(tokens),
                cost_estimate=pl.CostEstimate(
                    flops=4 * (last - first) * square,
                    bytes_accessed=(last - first) * (2 << 20),
                    transcendentals=(last - first) * tokens**2,
                ),
            )(*map(hbm, (q_rows, k_rows) + outputs[i][1:] + (aug,)), member, spread, extra)

    early = []
    if split:
        made = back(0, False, jnp.zeros((2 * NDH, split * HS), BF))[0]
        spread, head_part, made = lax.optimization_barrier((spread, head_part, made))
        made = after(made, *(block for blocks in mixed for block in blocks), *mixed_near[1:])
        early = [exchange(made)]

    step = 1
    while step < grp:
        head_part = head_part + lax.ppermute(
            head_part, "grp", [(i, i ^ step) for i in range(grp)]
        )
        step *= 2
    high = head_part.astype(BF)
    low = (head_part - high.astype(F32)).astype(BF)
    late_width = lw - split * HS
    groups = -(-chunk // late_width)
    extra = jnp.concatenate([high, low], axis=0)
    extra = jnp.pad(extra, ((0, 0), (0, groups * late_width - chunk)))
    extra = jnp.transpose(extra.reshape(2 * NDH, groups, late_width), (1, 0, 2))
    made = back(len(parts) - 1, True, extra.reshape(groups * 2 * NDH, late_width))
    late = [made[0]] + [send(made[s], s) for s in range(1, n)]

    whole = jax.ShapeDtypeStruct((tok, width), BF)
    mixed = mixed_near + [block for blocks in mixed for block in blocks]
    with jax.named_scope("latents"):
        latents = pl.pallas_call(
            functools.partial(latent_kernel, n, lw),
            out_shape=whole,
            compiler_params=params(tokens, 0),
        )(*map(hbm, mixed))
    with jax.named_scope("finish"):
        late[0] = after(late[0], latents)
        out_query, out_key, out_value, grad_heads = pl.pallas_call(
            functools.partial(
                finish_kernel, n, lw, chunk, n - half, len(mixed) - (n - half), split
            ),
            out_shape=[whole] * 3 + [jax.ShapeDtypeStruct((NDH, n * chunk), F32)],
            compiler_params=params(tokens, 0),
        )(*map(hbm, mixed + late + early))
    if chunk != columns:
        grad_heads = grad_heads.reshape(NDH, n, chunk)[:, :, :columns].reshape(NDH, dh)

    return (latents[None], out_query[None], out_key[None], out_value[None], grad_heads)


def solution(mesh):
    return jax.shard_map(
        on_device,
        mesh=mesh,
        in_specs=(
            P("grp", "gen", None),
            P("grp", "gen", None),
            P("grp", "gen", None),
            P("gen", None),
            P(),
            P("grp", None),
            P("grp", None),
            P("grp"),
        ),
        out_specs=(
            P("grp", "gen", None),
            P("grp", "gen", None),
            P("grp", "gen", None),
            P("grp", "gen", None),
            P(),
        ),
        check_vma=False,
    )
```

time: 237 us -> 206 us (0.87); the launches traced: 233 us -> 205 us
  waiting for transfers between devices: 112 us -> 62 us
  starting transfers between devices: 43.1 us -> 75.6 us
  local copies, waits for them, and re-layouts: 28.8 us -> 7.47 us
  Pallas kernels: 41.7 us -> 53.4 us
    all_to_all x7 -> x3, waiting for transfers between devices: 108 us -> 0.01 us  [exchange(): return lax.all_to_all(array, 'gen', split_axis=0, concat_axis=0, tiled=True)]
    ppermute x0 -> x32, waiting for transfers between devices: none -> 58.5 us  [send(): return lax.ppermute(array, 'gen', [(i, i ^ s) for i in range(n)])]
    ppermute x0 -> x32, starting transfers between devices: none -> 54.5 us  [send(): return lax.ppermute(array, 'gen', [(i, i ^ s) for i in range(n)])]
    all_to_all x7 -> x3, starting transfers between devices: 41.5 us -> 19.6 us  [exchange(): return lax.all_to_all(array, 'gen', split_axis=0, concat_axis=0, tiled=True)]
    unnamed x47 -> x91, local copies, waits for them, and re-layouts: 19.6 us -> 4.29 us
    pallas_call x5 -> x8, Pallas kernels: 37.8 us -> 49.3 us  [the longest x2 17 us: back(): pl.pallas_call(functools.partial(back_kernel, n, apart), grid=(last - fir...]
    transpose x4 -> x1, local copies, waits for them, and re-layouts: 5.48 us -> 0.01 us  [on_device(): extra = jnp.transpose(extra.reshape(2 * NDH, groups, late_width), (1, 0, 2))]
    dynamic_slice x0 -> x2, local copies, waits for them, and re-layouts: none -> 2.58 us  [columns_for(): return lax.dynamic_slice_in_dim(array, (me ^ s) * lw, lw, axis=1)]
  transfers between devices with their start and end apart: 9 -> 37, of which waited for: 7 -> 17; matrix products, arithmetic and copies ran while one was open for 5% -> 3% of each run, Pallas kernels for 16% -> 22%
where the time goes in v2:
time: 206 us; the launch traced here: 205 us
  starting transfers between devices  75.6 us (37%)
  waiting for transfers between devices  62 us (30%)
  Pallas kernels  53.4 us (26%)
  local copies, waits for them, and re-layouts  7.47 us (4%)
  other arithmetic  4.49 us (2%)
  between operations  2.1 us (1%)
    ppermute x32, waiting for transfers between devices, send(): return lax.ppermute(array, 'gen', [(i, i ^ s) for i in range(n)])  58.5 us
    ppermute x32, starting transfers between devices, send(): return lax.ppermute(array, 'gen', [(i, i ^ s) for i in range(n)])  54.5 us
    all_to_all x3, starting transfers between devices, exchange(): return lax.all_to_all(array, 'gen', split_axis=0, concat_axis=0, tiled=True)  19.6 us
    pallas_call x2, Pallas kernels, back(): pl.pallas_call(functools.partial(back_kernel, n, apart), grid=(last - fir...  17 us
    pallas_call x1, Pallas kernels, on_device(): pl.pallas_call(functools.partial(stats_kernel, n), grid=(heads,), in_spec...  11.7 us
    pallas_call x2, Pallas kernels, output(): pl.pallas_call(functools.partial(output_kernel, n), grid=(last - first,),...  9.89 us
    pallas_call x1, Pallas kernels, on_device(): pl.pallas_call(functools.partial(finish_kernel, n, lw, chunk, n - half, l...  4.42 us
    unnamed x91, local copies, waits for them, and re-layouts  4.29 us
  transfers between devices with their start and end apart: 37, of which 17 were waited for; matrix products, arithmetic and copies ran while one was open for 3% of the time, Pallas kernels for 22%

profile of v2, /device:TPU:8, one launch (start us, length us, event | category | flops | bytes accessed | tf_op | source)
XLA Modules:
  0.0 205.0 jit_solution(1994619673583199430)
XLA Ops:
  0.7 1.8 constant_dynamic-slice_fusion.1
  2.5 2.6 %collective-permute-start.9 = (bf16[2,128,512]{2,1,0:T(8,128)(2,1)S(1)}, bf16[2,128,512]{2,1,0:T(8,128)(2,1)}, u32[]{:S(2)}, u32[]{:S(2)}) collective-permute-start(bf16[2,128,512]{2,1,0:T(8,128)(2,1)S(1)} %pad_maximum_fusion.4), channel_id=1, source_target_pairs={{0,28},{4,24},{8,20},{12,16},{16,12},{20,8},{24,4},{28,0},{1,29},{... | collective-permute-start | bytes 786440 | tf_op jit(solution)/shard_map/ppermute | solution.py:375
  5.7 4.4 %collective-permute-start.5 = (bf16[2,128,512]{2,1,0:T(8,128)(2,1)S(1)}, bf16[2,128,512]{2,1,0:T(8,128)(2,1)}, u32[]{:S(2)}, u32[]{:S(2)}) collective-permute-start(bf16[2,128,512]{2,1,0:T(8,128)(2,1)S(1)} %pad_maximum_fusion.2), channel_id=1, source_target_pairs={{0,20},{4,16},{8,28},{12,24},{16,4},{20,0},{24,12},{28,8},{1,21},{... | collective-permute-start | bytes 786440 | tf_op jit(solution)/shard_map/ppermute | solution.py:375
  10.2 1.6 collective-permute-start
  12.6 5.1 %collective-permute-done.refs_1_ = bf16[2,128,512]{2,1,0:T(8,128)(2,1)} collective-permute-done((bf16[2,128,512]{2,1,0:T(8,128)(2,1)S(1)}, bf16[2,128,512]{2,1,0:T(8,128)(2,1)}, u32[]{:S(2)}, u32[]{:S(2)}) %collective-permute-start) | collective-permute-done | bytes 262176 | tf_op jit(solution)/shard_map/ppermute | solution.py:375
  17.7 2.1 %collective-permute-start.12 = (bf16[2,128,512]{2,1,0:T(8,128)(2,1)S(1)}, bf16[2,128,512]{2,1,0:T(8,128)(2,1)S(1)}, u32[]{:S(2)}, u32[]{:S(2)}) collective-permute-start(bf16[2,128,512]{2,1,0:T(8,128)(2,1)S(1)} %pad_maximum_fusion.6), channel_id=1, source_target_pairs={{0,8},{4,12},{8,0},{12,4},{16,24},{20,28},{24,16},{28,20},{1,9},{5... | collective-permute-start | bytes 786440 | tf_op jit(solution)/shard_map/ppermute | solution.py:375
  19.7 0.8 dynamic-slice_bitcast_fusion
  20.5 1.4 collective-permute-start.1
  22.1 8.4 %collective-permute-done.12.refs_2_ = bf16[2,128,512]{2,1,0:T(8,128)(2,1)S(1)} collective-permute-done((bf16[2,128,512]{2,1,0:T(8,128)(2,1)S(1)}, bf16[2,128,512]{2,1,0:T(8,128)(2,1)S(1)}, u32[]{:S(2)}, u32[]{:S(2)}) %collective-permute-start.12) | collective-permute-done | bytes 262176 | tf_op jit(solution)/shard_map/ppermute | solution.py:375
  30.5 0.7 collective-permute-done.1.refs_1_
  32.1 2.9 %collective-permute-start.2 = (bf16[128,512]{1,0:T(8,128)(2,1)S(1)}, bf16[128,512]{1,0:T(8,128)(2,1)S(1)}, u32[]{:S(2)}, u32[]{:S(2)}) collective-permute-start(bf16[128,512]{1,0:T(8,128)(2,1)S(1)} %get-tuple-element.71), channel_id=1, source_target_pairs={{0,8},{4,12},{8,0},{12,4},{16,24},{20,28},{24,16},{28,20},{1,9},{5... | collective-permute-start | bytes 393224 | tf_op jit(solution)/shard_map/ppermute | solution.py:375
  35.0 5.7 %collective-permute-done.6.refs_6_ = bf16[2,128,512]{2,1,0:T(8,128)(2,1)} collective-permute-done((bf16[2,128,512]{2,1,0:T(8,128)(2,1)S(1)}, bf16[2,128,512]{2,1,0:T(8,128)(2,1)}, u32[]{:S(2)}, u32[]{:S(2)}) %collective-permute-start.6) | collective-permute-done | bytes 262176 | tf_op jit(solution)/shard_map/ppermute | solution.py:375
  40.7 4.9 %collective-permute-done.5.refs_5_ = bf16[2,128,512]{2,1,0:T(8,128)(2,1)} collective-permute-done((bf16[2,128,512]{2,1,0:T(8,128)(2,1)S(1)}, bf16[2,128,512]{2,1,0:T(8,128)(2,1)}, u32[]{:S(2)}, u32[]{:S(2)}) %collective-permute-start.5) | collective-permute-done | bytes 262176 | tf_op jit(solution)/shard_map/ppermute | solution.py:375
  45.6 4.6 %collective-permute-done.4.refs_4_ = bf16[2,128,512]{2,1,0:T(8,128)(2,1)S(1)} collective-permute-done((bf16[2,128,512]{2,1,0:T(8,128)(2,1)S(1)}, bf16[2,128,512]{2,1,0:T(8,128)(2,1)S(1)}, u32[]{:S(2)}, u32[]{:S(2)}) %collective-permute-start.4) | collective-permute-done | bytes 262176 | tf_op jit(solution)/shard_map/ppermute | solution.py:375
  50.5 1.6 collective-permute-start.10
  52.1 6.3 %collective-permute-start.8 = (bf16[128,512]{1,0:T(8,128)(2,1)S(1)}, bf16[128,512]{1,0:T(8,128)(2,1)S(1)}, u32[]{:S(2)}, u32[]{:S(2)}) collective-permute-start(bf16[128,512]{1,0:T(8,128)(2,1)S(1)} %get-tuple-element.74), channel_id=1, source_target_pairs={{0,20},{4,16},{8,28},{12,24},{16,4},{20,0},{24,12},{28,8},{1,21},{... | collective-permute-start | bytes 393224 | tf_op jit(solution)/shard_map/ppermute | solution.py:375
  58.4 1.8 collective-permute-start.3
  60.2 0.7 pad_maximum_fusion.5.refs_0_
  60.9 11.7 %softmax_stats.1 = (bf16[4,1024,128]{2,1,0:T(8,128)(2,1)}, bf16[8,4,32,128]{3,2,1,0:T(8,128)(2,1)}, bf16[4,1024,128]{2,1,0:T(8,128)(2,1)}, bf16[4,1024,128]{2,1,0:T(8,128)(2,1)}) custom-call(bf16[2,128,512]{2,1,0:T(8,128)(2,1)} %pad_maximum_fusion.5.refs_0_, bf16[2,128,512]{2,1,0:T(8,128)(2,1)} %collective-permute-done.refs_1_, ...), custom_call_target="tpu_custom_call" | custom-call | flops 1073741824 | bytes 4194304 | tf_op jit(solution)/shard_map/softmax_stats/pallas_call | solution.py:431
  72.7 1.1 copy-done.1
  73.8 3.9 %pool_project.1 = (bf16[8,24,768]{2,1,0:T(8,128)(2,1)}, f32[24,512]{1,0:T(8,128)S(1)}) custom-call(bf16[128,512]{1,0:T(8,128)(2,1)S(1)} %get-tuple-element.155.refs_0_, bf16[128,512]{1,0:T(8,128)(2,1)S(1)} %collective-permute-done.1.refs_1_, bf16[128,512]{1,0:T(8,128)(2,1)S(1)} %collective-permute-done.2.refs_2_, ...), custom_call_target="tpu_custom_call" | custom-call | tf_op jit(solution)/shard_map/pool_project/pallas_call | solution.py:450
  77.8 6.9 %all-to-all-start = ((bf16[8,24,768]{2,1,0:T(8,128)(2,1)}), bf16[8,24,768]{2,1,0:T(8,128)(2,1)S(1)}, u32[]{:S(2)}, u32[]{:S(2)}) async-start(bf16[8,24,768]{2,1,0:T(8,128)(2,1)} %get-tuple-element.83), calls=%async_computation | async-start | bytes 589824 | tf_op jit(solution)/shard_map/all_to_all | solution.py:349
  84.7 4.9 %attention_output.2 = (bf16[160,256]{1,0:T(8,128)(2,1)}, bf16[160,256]{1,0:T(8,128)(2,1)}, bf16[160,256]{1,0:T(8,128)(2,1)}, bf16[160,256]{1,0:T(8,128)(2,1)}, b...) custom-call(bf16[128,512]{1,0:T(8,128)(2,1)} %copy-done.2, ...), custom_call_target="tpu_custom_call" | custom-call | flops 1073741824 | bytes 2097152 | tf_op jit(solution)/shard_map/attention_output/pallas_call | solution.py:470
  89.7 2.4 %collective-permute-start.17 = (bf16[160,256]{1,0:T(8,128)(2,1)}, bf16[160,256]{1,0:T(8,128)(2,1)S(1)}, u32[]{:S(2)}, u32[]{:S(2)}) collective-permute-start(bf16[160,256]{1,0:T(8,128)(2,1)} %get-tuple-element.97), channel_id=1, source_target_pairs={{0,16},{4,20},{8,24},{12,28},{16,0},{20,4},{24,8},{28,12},{1,17},{... | collective-permute-start | bytes 245768 | tf_op jit(solution)/shard_map/ppermute | solution.py:375
  92.1 1.5 collective-permute-start.18
  93.8 1.0 discriminator.1
  94.7 1.7 collective-permute-done.17.refs_4_
  96.4 2.2 %collective-permute-done.18.refs_5_ = bf16[160,256]{1,0:T(8,128)(2,1)S(1)} collective-permute-done((bf16[160,256]{1,0:T(8,128)(2,1)}, bf16[160,256]{1,0:T(8,128)(2,1)S(1)}, u32[]{:S(2)}, u32[]{:S(2)}) %collective-permute-start.18) | collective-permute-done | bytes 81952 | tf_op jit(solution)/shard_map/ppermute | solution.py:375
  98.6 5.5 %all-to-all-start.1 = ((bf16[8,24,768]{2,1,0:T(8,128)(2,1)}), bf16[8,24,768]{2,1,0:T(8,128)(2,1)S(1)}, u32[]{:S(2)}, u32[]{:S(2)}) async-start(bf16[8,24,768]{2,1,0:T(8,128)(2,1)} %get-tuple-element.107), calls=%async_computation.1 | async-start | bytes 589824 | tf_op jit(solution)/shard_map/all_to_all | solution.py:349
  104.4 1.5 collective-permute-start.19
  105.9 1.5 collective-permute-start.20
  107.5 5.0 %attention_output.3 = (bf16[160,256]{1,0:T(8,128)(2,1)}, bf16[160,256]{1,0:T(8,128)(2,1)}, bf16[160,256]{1,0:T(8,128)(2,1)}, bf16[160,256]{1,0:T(8,128)(2,1)}, b...) custom-call(bf16[128,512]{1,0:T(8,128)(2,1)} %copy-done.2, ...), custom_call_target="tpu_custom_call" | custom-call | flops 1073741824 | bytes 2097152 | tf_op jit(solution)/shard_map/attention_output/pallas_call | solution.py:470
  112.5 0.9 pad_maximum_fusion.10
  113.4 2.0 collective-permute-start.16
  115.4 2.3 %collective-permute-start.21 = (bf16[160,256]{1,0:T(8,128)(2,1)}, bf16[160,256]{1,0:T(8,128)(2,1)S(1)}, u32[]{:S(2)}, u32[]{:S(2)}) collective-permute-start(bf16[160,256]{1,0:T(8,128)(2,1)} %get-tuple-element.101), channel_id=1, source_target_pairs={{0,16},{4,20},{8,24},{12,28},{16,0},{20,4},{24,8},{28,12},{1,17},{... | collective-permute-start | bytes 245768 | tf_op jit(solution)/shard_map/ppermute | solution.py:375
  117.7 1.9 collective-permute-start.22
  119.6 0.9 pad_maximum_fusion.9
  120.5 0.9 pad_maximum_fusion.8
  121.5 1.0 collective-permute-start.15
  123.0 3.1 %pooled_gradient.1 = (bf16[128,512]{1,0:T(8,128)(2,1)S(1)}, f32[8,640]{1,0:T(8,128)S(1)}) custom-call(bf16[8,24,768]{2,1,0:T(8,128)(2,1)S(1)} %all-to-all-done.1.got_ref, bf16[512,5120]{1,0:T(8,128)(2,1)} %w_hbm.1, f32[24,512]{1,0:T(8,128)S(1)} %get-tuple-element.110.pooled_ref, f32[24,128]{1,0:T(8,128)S(1)} %broadcast_select_fusion.refs_9_.meta_ref, ...), custom_call_target="tpu_custom_call" | custom-call | tf_op jit(solution)/shard_map/pooled_gradient/pallas_call | solution.py:515
  126.2 1.6 collective-permute-start.23
  127.8 1.7 collective-permute-start.24
  129.5 8.4 %attention_back.2 = bf16[8,288,256]{2,1,0:T(8,128)(2,1)} custom-call(bf16[4,1024,128]{2,1,0:T(8,128)(2,1)} %get-tuple-element.79.refs_8_.q_ref, bf16[4,1024,128]{2,1,0:T(8,128)(2,1)} %get-tuple-element.80.refs_9_.k_ref, bf16[2,1024,128]{2,1,0:T(8,128)(2,1)} %get-tuple-element.115.v_ref, bf16[2,1024,128]{2,1,0:T(8,128)(2,1)} %get-tuple-element.86.o_ref, ...), custom_call_target="tpu_custom_call" | custom-call | flops 2147483648 | bytes 4194304 | tf_op jit(solution)/shard_map/attention_back/pallas_call | solution.py:537
  138.8 7.2 %all-to-all-start.2 = ((bf16[8,288,256]{2,1,0:T(8,128)(2,1)}), bf16[8,288,256]{2,1,0:T(8,128)(2,1)S(1)}, u32[]{:S(2)}, u32[]{:S(2)}) async-start(bf16[8,288,256]{2,1,0:T(8,128)(2,1)} %attention_back.2), calls=%async_computation.2 | async-start | bytes 2359296 | tf_op jit(solution)/shard_map/all_to_all | solution.py:349
  146.0 1.2 collective-permute-done.25
  147.2 1.5 collective-permute-start.26
  148.7 2.3 %collective-permute-done.26 = f32[8,640]{1,0:T(8,128)S(1)} collective-permute-done((f32[8,640]{1,0:T(8,128)S(1)}, f32[8,640]{1,0:T(8,128)S(1)}, u32[]{:S(2)}, u32[]{:S(2)}) %collective-permute-start.26) | collective-permute-done | bytes 20512 | tf_op jit(solution)/shard_map/ppermute | solution.py:566
  151.0 8.5 %attention_back.3 = (bf16[336,256]{1,0:T(8,128)(2,1)}, bf16[336,256]{1,0:T(8,128)(2,1)}, bf16[336,256]{1,0:T(8,128)(2,1)}, bf16[336,256]{1,0:T(8,128)(2,1)}, bf1...) custom-call(bf16[4,1024,128]{2,1,0:T(8,128)(2,1)} %get-tuple-element.79.r, ...), custom_call_target="tpu_custom_call" | custom-call | flops 2147483648 | bytes 4194304 | tf_op jit(solution)/shard_map/attention_back/pallas_call | solution.py:537
  159.6 1.5 collective-permute-start.27
  161.7 1.5 collective-permute-start.29
  163.1 2.4 %collective-permute-start.30 = (bf16[336,256]{1,0:T(8,128)(2,1)}, bf16[336,256]{1,0:T(8,128)(2,1)S(1)}, u32[]{:S(2)}, u32[]{:S(2)}) collective-permute-start(bf16[336,256]{1,0:T(8,128)(2,1)} %get-tuple-element.123), channel_id=1, source_target_pairs={{0,16},{4,20},{8,24},{12,28},{16,0},{20,4},{24,8},{28,12},{1,17},{... | collective-permute-start | bytes 516104 | tf_op jit(solution)/shard_map/ppermute | solution.py:375
  165.5 1.5 collective-permute-start.31
  166.9 1.7 collective-permute-done.27.refs_13_
  168.6 3.0 %collective-permute-start.32 = (bf16[336,256]{1,0:T(8,128)(2,1)}, bf16[336,256]{1,0:T(8,128)(2,1)S(1)}, u32[]{:S(2)}, u32[]{:S(2)}) collective-permute-start(bf16[336,256]{1,0:T(8,128)(2,1)} %get-tuple-element.125), channel_id=1, source_target_pairs={{0,24},{4,28},{8,16},{12,20},{16,8},{20,12},{24,0},{28,4},{1,25},{... | collective-permute-start | bytes 516104 | tf_op jit(solution)/shard_map/ppermute | solution.py:375
  171.6 1.0 collective-permute-done.28.refs_14_
  172.6 0.8 collective-permute-start.33
  173.5 0.7 copy-done.12
  174.2 2.4 %latents.1 = bf16[128,4096]{1,0:T(8,128)(2,1)} custom-call(bf16[160,512]{1,0:T(8,128)(2,1)} %copy-done.12, bf16[160,512]{1,0:T(8,128)(2,1)} %copy-done.15, bf16[160,512]{1,0:T(8,128)(2,1)} %copy-done.14, bf16[160,512]{1,0:T(8,128)(2,1)} %copy-done.13, bf16[160,256]{1,0:T(8,128)(2,1)} %copy-done.16, bf16[160,256]{1,0:T(8,128)(2,1)} %copy-done.17, ...), custom_call_target="tpu_custom_call" | custom-call | tf_op jit(solution)/shard_map/latents/pallas_call | solution.py:583
  176.6 11.2 %collective-permute-done.30.refs_16_ = bf16[336,256]{1,0:T(8,128)(2,1)S(1)} collective-permute-done((bf16[336,256]{1,0:T(8,128)(2,1)}, bf16[336,256]{1,0:T(8,128)(2,1)S(1)}, u32[]{:S(2)}, u32[]{:S(2)}) %collective-permute-start.30) | collective-permute-done | bytes 172064 | tf_op jit(solution)/shard_map/ppermute | solution.py:375
  187.8 3.7 %collective-permute-done.31.refs_17_ = bf16[336,256]{1,0:T(8,128)(2,1)S(1)} collective-permute-done((bf16[336,256]{1,0:T(8,128)(2,1)}, bf16[336,256]{1,0:T(8,128)(2,1)S(1)}, u32[]{:S(2)}, u32[]{:S(2)}) %collective-permute-start.31) | collective-permute-done | bytes 172064 | tf_op jit(solution)/shard_map/ppermute | solution.py:375
  191.5 5.0 %collective-permute-done.32.refs_18_ = bf16[336,256]{1,0:T(8,128)(2,1)S(1)} collective-permute-done((bf16[336,256]{1,0:T(8,128)(2,1)}, bf16[336,256]{1,0:T(8,128)(2,1)S(1)}, u32[]{:S(2)}, u32[]{:S(2)}) %collective-permute-start.32) | collective-permute-done | bytes 172064 | tf_op jit(solution)/shard_map/ppermute | solution.py:375
  196.4 2.4 %collective-permute-done.33.refs_19_ = bf16[336,256]{1,0:T(8,128)(2,1)S(1)} collective-permute-done((bf16[336,256]{1,0:T(8,128)(2,1)}, bf16[336,256]{1,0:T(8,128)(2,1)S(1)}, u32[]{:S(2)}, u32[]{:S(2)}) %collective-permute-start.33) | collective-permute-done | bytes 172064 | tf_op jit(solution)/shard_map/ppermute | solution.py:375
  199.5 1.0 copy-done.10
  200.5 4.4 %finish.1 = (bf16[128,4096]{1,0:T(8,128)(2,1)}, bf16[128,4096]{1,0:T(8,128)(2,1)}, bf16[128,4096]{1,0:T(8,128)(2,1)}, f32[8,5120]{1,0:T(8,128)}) custom-call(bf16[160,512]{1,0:T(8,128)(2,1)} %copy-done.12, bf16[160,512]{1,0:T(8,128)(2,1)} %copy-done.15, bf16[160,512]{1,0:T(8,128)(2,1)} %copy-done.14, bf16[160,512]{1,0:T(8,128)(2,1)} %copy-done.13, ...), custom_call_target="tpu_custom_call" | custom-call | tf_op jit(solution)/shard_map/finish/pallas_call | solution.py:590
  (148 shorter events, 5.4 us)
Async XLA Ops:
  0.6 84.0 %copy-start = (f32[8,5120]{1,0:T(8,128)S(1)}, f32[8,5120]{1,0:T(8,128)}, u32[]{:S(2)}) copy-start(f32[8,5120]{1,0:T(8,128)} %param.12) | copy-start | bytes 491524
  2.5 9.3 %copy-start.24 = (s32[1,1024]{1,0:T(1,128)S(1)}, s32[1,1024]{1,0:T(1,128)}, u32[]{:S(2)}) copy-start(s32[1,1024]{1,0:T(1,128)} %param.13) | copy-start | bytes 12292
  2.5 29.5 %collective-permute-start.9 = (bf16[2,128,512]{2,1,0:T(8,128)(2,1)S(1)}, bf16[2,128,512]{2,1,0:T(8,128)(2,1)}, u32[]{:S(2)}, u32[]{:S(2)}) collective-permute-start(bf16[2,128,512]{2,1,0:T(8,128)(2,1)S(1)} %pad_maximum_fusion.4), channel_id=1, source_target_pairs={{0,28},{4,24},{8,20},{12,16},{16,12},{20,8},{24,4},{28,0},{1,29},{... | collective-permute-start | bytes 786440 | tf_op jit(solution)/shard_map/ppermute | solution.py:375
  5.2 14.6 %copy-start.11 = (bf16[1,128,4096]{2,1,0:T(8,128)(2,1)S(1)}, bf16[1,128,4096]{2,1,0:T(8,128)(2,1)}, u32[]{:S(2)}) copy-start(bf16[1,128,4096]{2,1,0:T(8,128)(2,1)} %param.10) | copy-start | bytes 3145732
  5.2 35.5 %collective-permute-start.6 = (bf16[2,128,512]{2,1,0:T(8,128)(2,1)S(1)}, bf16[2,128,512]{2,1,0:T(8,128)(2,1)}, u32[]{:S(2)}, u32[]{:S(2)}) collective-permute-start(bf16[2,128,512]{2,1,0:T(8,128)(2,1)S(1)} %pad_maximum_fusion.3), channel_id=1, source_target_pairs={{0,24},{4,28},{8,16},{12,20},{16,8},{20,12},{24,0},{28,4},{1,25},{... | collective-permute-start | bytes 786440 | tf_op jit(solution)/shard_map/ppermute | solution.py:375
  5.7 39.9 %collective-permute-start.5 = (bf16[2,128,512]{2,1,0:T(8,128)(2,1)S(1)}, bf16[2,128,512]{2,1,0:T(8,128)(2,1)}, u32[]{:S(2)}, u32[]{:S(2)}) collective-permute-start(bf16[2,128,512]{2,1,0:T(8,128)(2,1)S(1)} %pad_maximum_fusion.2), channel_id=1, source_target_pairs={{0,20},{4,16},{8,28},{12,24},{16,4},{20,0},{24,12},{28,8},{1,21},{... | collective-permute-start | bytes 786440 | tf_op jit(solution)/shard_map/ppermute | solution.py:375
  10.2 7.5 %collective-permute-start = (bf16[2,128,512]{2,1,0:T(8,128)(2,1)S(1)}, bf16[2,128,512]{2,1,0:T(8,128)(2,1)}, u32[]{:S(2)}, u32[]{:S(2)}) collective-permute-start(bf16[2,128,512]{2,1,0:T(8,128)(2,1)S(1)} %pad_maximum_fusion), channel_id=1, source_target_pairs={{0,4},{4,0},{8,12},{12,8},{16,20},{20,16},{24,28},{28,24},{1,5},{5... | collective-permute-start | bytes 786440 | tf_op jit(solution)/shard_map/ppermute | solution.py:375
  12.6 48.3 %copy-start.44 = (s32[1,21]{1,0:T(1,128)S(1)}, s32[1,21]{1,0:T(1,128)}, u32[]{:S(2)}) copy-start(s32[1,21]{1,0:T(1,128)} %param.14) | copy-start | bytes 256
  17.7 12.9 %collective-permute-start.12 = (bf16[2,128,512]{2,1,0:T(8,128)(2,1)S(1)}, bf16[2,128,512]{2,1,0:T(8,128)(2,1)S(1)}, u32[]{:S(2)}, u32[]{:S(2)}) collective-permute-start(bf16[2,128,512]{2,1,0:T(8,128)(2,1)S(1)} %pad_maximum_fusion.6), channel_id=1, source_target_pairs={{0,8},{4,12},{8,0},{12,4},{16,24},{20,28},{24,16},{28,20},{1,9},{5... | collective-permute-start | bytes 786440 | tf_op jit(solution)/shard_map/ppermute | solution.py:375
  20.5 52.1 %copy-start.2 = (bf16[128,512]{1,0:T(8,128)(2,1)}, bf16[128,512]{1,0:T(8,128)(2,1)S(1)}, u32[]{:S(2)}) copy-start(bf16[128,512]{1,0:T(8,128)(2,1)S(1)} %get-tuple-element.155.refs_0_) | copy-start | bytes 393220
  20.5 10.7 %collective-permute-start.1 = (bf16[128,512]{1,0:T(8,128)(2,1)S(1)}, bf16[128,512]{1,0:T(8,128)(2,1)S(1)}, u32[]{:S(2)}, u32[]{:S(2)}) collective-permute-start(bf16[128,512]{1,0:T(8,128)(2,1)S(1)} %get-tuple-element.70), channel_id=1, source_target_pairs={{0,4},{4,0},{8,12},{12,8},{16,20},{20,16},{24,28},{28,24},{1,5},{5... | collective-permute-start | bytes 393224 | tf_op jit(solution)/shard_map/ppermute | solution.py:375
  30.5 29.6 %copy-start.37 = (bf16[2,128,512]{2,1,0:T(8,128)(2,1)}, bf16[2,128,512]{2,1,0:T(8,128)(2,1)S(1)}, u32[]{:S(2)}) copy-start(bf16[2,128,512]{2,1,0:T(8,128)(2,1)S(1)} %collective-permute-done.12.refs_2_) | copy-start | bytes 786436
  30.5 19.7 %collective-permute-start.4 = (bf16[2,128,512]{2,1,0:T(8,128)(2,1)S(1)}, bf16[2,128,512]{2,1,0:T(8,128)(2,1)S(1)}, u32[]{:S(2)}, u32[]{:S(2)}) collective-permute-start(bf16[2,128,512]{2,1,0:T(8,128)(2,1)S(1)} %pad_maximum_fusion.1), channel_id=1, source_target_pairs={{0,16},{4,20},{8,24},{12,28},{16,0},{20,4},{24,8},{28,12},{1,17},{... | collective-permute-start | bytes 786440 | tf_op jit(solution)/shard_map/ppermute | solution.py:375
  31.2 41.5 %copy-start.3 = (bf16[128,512]{1,0:T(8,128)(2,1)}, bf16[128,512]{1,0:T(8,128)(2,1)S(1)}, u32[]{:S(2)}) copy-start(bf16[128,512]{1,0:T(8,128)(2,1)S(1)} %collective-permute-done.1.refs_1_) | copy-start | bytes 393220
  31.2 27.1 %collective-permute-start.13 = (bf16[2,128,512]{2,1,0:T(8,128)(2,1)S(1)}, bf16[2,128,512]{2,1,0:T(8,128)(2,1)S(1)}, u32[]{:S(2)}, u32[]{:S(2)}) collective-permute-start(bf16[2,128,512]{2,1,0:T(8,128)(2,1)S(1)} %pad_maximum_fusion.7), channel_id=1, source_target_pairs={{0,12},{4,8},{8,4},{12,0},{16,28},{20,24},{24,20},{28,16},{1,13},{... | collective-permute-start | bytes 786440 | tf_op jit(solution)/shard_map/ppermute | solution.py:375
  32.1 26.3 %collective-permute-start.2 = (bf16[128,512]{1,0:T(8,128)(2,1)S(1)}, bf16[128,512]{1,0:T(8,128)(2,1)S(1)}, u32[]{:S(2)}, u32[]{:S(2)}) collective-permute-start(bf16[128,512]{1,0:T(8,128)(2,1)S(1)} %get-tuple-element.71), channel_id=1, source_target_pairs={{0,8},{4,12},{8,0},{12,4},{16,24},{20,28},{24,16},{28,20},{1,9},{5... | collective-permute-start | bytes 393224 | tf_op jit(solution)/shard_map/ppermute | solution.py:375
  50.2 10.7 %copy-start.38 = (bf16[2,128,512]{2,1,0:T(8,128)(2,1)}, bf16[2,128,512]{2,1,0:T(8,128)(2,1)S(1)}, u32[]{:S(2)}) copy-start(bf16[2,128,512]{2,1,0:T(8,128)(2,1)S(1)} %collective-permute-done.4.refs_4_) | copy-start | bytes 786436
  50.2 22.3 %collective-permute-start.11 = (bf16[128,512]{1,0:T(8,128)(2,1)}, bf16[128,512]{1,0:T(8,128)(2,1)S(1)}, u32[]{:S(2)}, u32[]{:S(2)}) collective-permute-start(bf16[128,512]{1,0:T(8,128)(2,1)} %get-tuple-element.76), channel_id=1, source_target_pairs={{0,28},{4,24},{8,20},{12,16},{16,12},{20,8},{24,4},{28,0},{1,29},{... | collective-permute-start | bytes 393224 | tf_op jit(solution)/shard_map/ppermute | solution.py:375
  50.5 22.1 %collective-permute-start.10 = (bf16[128,512]{1,0:T(8,128)(2,1)}, bf16[128,512]{1,0:T(8,128)(2,1)S(1)}, u32[]{:S(2)}, u32[]{:S(2)}) collective-permute-start(bf16[128,512]{1,0:T(8,128)(2,1)} %get-tuple-element.75), channel_id=1, source_target_pairs={{0,24},{4,28},{8,16},{12,20},{16,8},{20,12},{24,0},{28,4},{1,25},{... | collective-permute-start | bytes 393224 | tf_op jit(solution)/shard_map/ppermute | solution.py:375
  52.1 20.5 %collective-permute-start.8 = (bf16[128,512]{1,0:T(8,128)(2,1)S(1)}, bf16[128,512]{1,0:T(8,128)(2,1)S(1)}, u32[]{:S(2)}, u32[]{:S(2)}) collective-permute-start(bf16[128,512]{1,0:T(8,128)(2,1)S(1)} %get-tuple-element.74), channel_id=1, source_target_pairs={{0,20},{4,16},{8,28},{12,24},{16,4},{20,0},{24,12},{28,8},{1,21},{... | collective-permute-start | bytes 393224 | tf_op jit(solution)/shard_map/ppermute | solution.py:375
  58.3 14.4 %copy-start.4 = (bf16[128,512]{1,0:T(8,128)(2,1)}, bf16[128,512]{1,0:T(8,128)(2,1)S(1)}, u32[]{:S(2)}) copy-start(bf16[128,512]{1,0:T(8,128)(2,1)S(1)} %collective-permute-done.2.refs_2_) | copy-start | bytes 393220
  58.3 14.3 %collective-permute-start.7 = (bf16[128,512]{1,0:T(8,128)(2,1)S(1)}, bf16[128,512]{1,0:T(8,128)(2,1)S(1)}, u32[]{:S(2)}, u32[]{:S(2)}) collective-permute-start(bf16[128,512]{1,0:T(8,128)(2,1)S(1)} %get-tuple-element.73), channel_id=1, source_target_pairs={{0,16},{4,20},{8,24},{12,28},{16,0},{20,4},{24,8},{28,12},{1,17},{... | collective-permute-start | bytes 393224 | tf_op jit(solution)/shard_map/ppermute | solution.py:375
  58.4 14.3 %collective-permute-start.3 = (bf16[128,512]{1,0:T(8,128)(2,1)S(1)}, bf16[128,512]{1,0:T(8,128)(2,1)S(1)}, u32[]{:S(2)}, u32[]{:S(2)}) collective-permute-start(bf16[128,512]{1,0:T(8,128)(2,1)S(1)} %get-tuple-element.72), channel_id=1, source_target_pairs={{0,12},{4,8},{8,4},{12,0},{16,28},{20,24},{24,20},{28,16},{1,13},{... | collective-permute-start | bytes 393224 | tf_op jit(solution)/shard_map/ppermute | solution.py:375
  72.6 5.1 %copy-start.5 = (bf16[128,512]{1,0:T(8,128)(2,1)}, bf16[128,512]{1,0:T(8,128)(2,1)S(1)}, u32[]{:S(2)}) copy-start(bf16[128,512]{1,0:T(8,128)(2,1)S(1)} %collective-permute-done.11.refs_7_) | copy-start | bytes 393220
  72.6 5.1 %copy-start.6 = (bf16[128,512]{1,0:T(8,128)(2,1)}, bf16[128,512]{1,0:T(8,128)(2,1)S(1)}, u32[]{:S(2)}) copy-start(bf16[128,512]{1,0:T(8,128)(2,1)S(1)} %collective-permute-done.10.refs_6_) | copy-start | bytes 393220
  77.8 16.0 %all-to-all-start = ((bf16[8,24,768]{2,1,0:T(8,128)(2,1)}), bf16[8,24,768]{2,1,0:T(8,128)(2,1)S(1)}, u32[]{:S(2)}, u32[]{:S(2)}) async-start(bf16[8,24,768]{2,1,0:T(8,128)(2,1)} %get-tuple-element.83), calls=%async_computation | async-start | bytes 589824 | tf_op jit(solution)/shard_map/all_to_all | solution.py:349
  89.6 14.7 %copy-start.42 = (bf16[160,256]{1,0:T(8,128)(2,1)S(1)}, bf16[160,256]{1,0:T(8,128)(2,1)}, u32[]{:S(2)}) copy-start(bf16[160,256]{1,0:T(8,128)(2,1)} %get-tuple-element.99) | copy-start | bytes 245764
  89.7 16.3 %copy-start.40 = (bf16[160,256]{1,0:T(8,128)(2,1)S(1)}, bf16[160,256]{1,0:T(8,128)(2,1)}, u32[]{:S(2)}) copy-start(bf16[160,256]{1,0:T(8,128)(2,1)} %get-tuple-element.100) | copy-start | bytes 245764
  89.7 6.8 %collective-permute-start.17 = (bf16[160,256]{1,0:T(8,128)(2,1)}, bf16[160,256]{1,0:T(8,128)(2,1)S(1)}, u32[]{:S(2)}, u32[]{:S(2)}) collective-permute-start(bf16[160,256]{1,0:T(8,128)(2,1)} %get-tuple-element.97), channel_id=1, source_target_pairs={{0,16},{4,20},{8,24},{12,28},{16,0},{20,4},{24,8},{28,12},{1,17},{... | collective-permute-start | bytes 245768 | tf_op jit(solution)/shard_map/ppermute | solution.py:375
  92.1 6.5 %collective-permute-start.18 = (bf16[160,256]{1,0:T(8,128)(2,1)}, bf16[160,256]{1,0:T(8,128)(2,1)S(1)}, u32[]{:S(2)}, u32[]{:S(2)}) collective-permute-start(bf16[160,256]{1,0:T(8,128)(2,1)} %get-tuple-element.98), channel_id=1, source_target_pairs={{0,20},{4,16},{8,28},{12,24},{16,4},{20,0},{24,12},{28,8},{1,21},{... | collective-permute-start | bytes 245768 | tf_op jit(solution)/shard_map/ppermute | solution.py:375
  96.4 16.0 %copy-start.16 = (bf16[160,256]{1,0:T(8,128)(2,1)}, bf16[160,256]{1,0:T(8,128)(2,1)S(1)}, u32[]{:S(2)}) copy-start(bf16[160,256]{1,0:T(8,128)(2,1)S(1)} %collective-permute-done.17.refs_4_) | copy-start | bytes 245764
  98.6 13.8 %copy-start.17 = (bf16[160,256]{1,0:T(8,128)(2,1)}, bf16[160,256]{1,0:T(8,128)(2,1)S(1)}, u32[]{:S(2)}) copy-start(bf16[160,256]{1,0:T(8,128)(2,1)S(1)} %collective-permute-done.18.refs_5_) | copy-start | bytes 245764
  98.6 24.4 %all-to-all-start.1 = ((bf16[8,24,768]{2,1,0:T(8,128)(2,1)}), bf16[8,24,768]{2,1,0:T(8,128)(2,1)S(1)}, u32[]{:S(2)}, u32[]{:S(2)}) async-start(bf16[8,24,768]{2,1,0:T(8,128)(2,1)} %get-tuple-element.107), calls=%async_computation.1 | async-start | bytes 589824 | tf_op jit(solution)/shard_map/all_to_all | solution.py:349
  104.4 17.0 %collective-permute-start.19 = (bf16[160,256]{1,0:T(8,128)(2,1)S(1)}, bf16[160,256]{1,0:T(8,128)(2,1)S(1)}, u32[]{:S(2)}, u32[]{:S(2)}) collective-permute-start(bf16[160,256]{1,0:T(8,128)(2,1)S(1)} %copy-done.42), channel_id=1, source_target_pairs={{0,24},{4,28},{8,16},{12,20},{16,8},{20,12},{24,0},{28,4},{1,25},{... | collective-permute-start | bytes 245768 | tf_op jit(solution)/shard_map/ppermute | solution.py:375
  105.9 6.5 %copy-start.34 = (bf16[160,256]{1,0:T(8,128)(2,1)S(1)}, bf16[160,256]{1,0:T(8,128)(2,1)}, u32[]{:S(2)}) copy-start(bf16[160,256]{1,0:T(8,128)(2,1)} %get-tuple-element.95) | copy-start | bytes 245764
  105.9 13.7 %copy-start.33 = (bf16[160,256]{1,0:T(8,128)(2,1)S(1)}, bf16[160,256]{1,0:T(8,128)(2,1)}, u32[]{:S(2)}) copy-start(bf16[160,256]{1,0:T(8,128)(2,1)} %get-tuple-element.93) | copy-start | bytes 245764
  105.9 14.6 %copy-start.32 = (bf16[160,256]{1,0:T(8,128)(2,1)S(1)}, bf16[160,256]{1,0:T(8,128)(2,1)}, u32[]{:S(2)}) copy-start(bf16[160,256]{1,0:T(8,128)(2,1)} %get-tuple-element.91) | copy-start | bytes 245764
  105.9 16.8 %collective-permute-start.20 = (bf16[160,256]{1,0:T(8,128)(2,1)S(1)}, bf16[160,256]{1,0:T(8,128)(2,1)S(1)}, u32[]{:S(2)}, u32[]{:S(2)}) collective-permute-start(bf16[160,256]{1,0:T(8,128)(2,1)S(1)} %copy-done.40), channel_id=1, source_target_pairs={{0,28},{4,24},{8,20},{12,16},{16,12},{20,8},{24,4},{28,0},{1,29},{... | collective-permute-start | bytes 245768 | tf_op jit(solution)/shard_map/ppermute | solution.py:375
  113.4 24.6 %collective-permute-start.16 = (bf16[160,512]{1,0:T(8,128)(2,1)S(1)}, bf16[160,512]{1,0:T(8,128)(2,1)S(1)}, u32[]{:S(2)}, u32[]{:S(2)}) collective-permute-start(bf16[160,512]{1,0:T(8,128)(2,1)S(1)} %pad_maximum_fusion.10), channel_id=1, source_target_pairs={{0,12},{4,8},{8,4},{12,0},{16,28},{20,24},{24,20},{28,16},{1,13},{... | collective-permute-start | bytes 491528 | tf_op jit(solution)/shard_map/ppermute | solution.py:375
  115.4 10.8 %collective-permute-start.21 = (bf16[160,256]{1,0:T(8,128)(2,1)}, bf16[160,256]{1,0:T(8,128)(2,1)S(1)}, u32[]{:S(2)}, u32[]{:S(2)}) collective-permute-start(bf16[160,256]{1,0:T(8,128)(2,1)} %get-tuple-element.101), channel_id=1, source_target_pairs={{0,16},{4,20},{8,24},{12,28},{16,0},{20,4},{24,8},{28,12},{1,17},{... | collective-permute-start | bytes 245768 | tf_op jit(solution)/shard_map/ppermute | solution.py:375
  117.7 10.1 %collective-permute-start.22 = (bf16[160,256]{1,0:T(8,128)(2,1)}, bf16[160,256]{1,0:T(8,128)(2,1)S(1)}, u32[]{:S(2)}, u32[]{:S(2)}) collective-permute-start(bf16[160,256]{1,0:T(8,128)(2,1)} %get-tuple-element.102), channel_id=1, source_target_pairs={{0,20},{4,16},{8,28},{12,24},{16,4},{20,0},{24,12},{28,8},{1,21},{... | collective-permute-start | bytes 245768 | tf_op jit(solution)/shard_map/ppermute | solution.py:375
  121.5 16.6 %collective-permute-start.15 = (bf16[160,512]{1,0:T(8,128)(2,1)S(1)}, bf16[160,512]{1,0:T(8,128)(2,1)S(1)}, u32[]{:S(2)}, u32[]{:S(2)}) collective-permute-start(bf16[160,512]{1,0:T(8,128)(2,1)S(1)} %pad_maximum_fusion.9), channel_id=1, source_target_pairs={{0,8},{4,12},{8,0},{12,4},{16,24},{20,28},{24,16},{28,20},{1,9},{5... | collective-permute-start | bytes 491528 | tf_op jit(solution)/shard_map/ppermute | solution.py:375
  122.7 15.3 %collective-permute-start.14 = (bf16[160,512]{1,0:T(8,128)(2,1)S(1)}, bf16[160,512]{1,0:T(8,128)(2,1)S(1)}, u32[]{:S(2)}, u32[]{:S(2)}) collective-permute-start(bf16[160,512]{1,0:T(8,128)(2,1)S(1)} %pad_maximum_fusion.8), channel_id=1, source_target_pairs={{0,4},{4,0},{8,12},{12,8},{16,20},{20,16},{24,28},{28,24},{1,5},{5... | collective-permute-start | bytes 491528 | tf_op jit(solution)/shard_map/ppermute | solution.py:375
  126.2 11.8 %copy-start.20 = (bf16[160,256]{1,0:T(8,128)(2,1)}, bf16[160,256]{1,0:T(8,128)(2,1)S(1)}, u32[]{:S(2)}) copy-start(bf16[160,256]{1,0:T(8,128)(2,1)S(1)} %collective-permute-done.21.refs_8_) | copy-start | bytes 245764
  126.2 11.8 %collective-permute-start.23 = (bf16[160,256]{1,0:T(8,128)(2,1)S(1)}, bf16[160,256]{1,0:T(8,128)(2,1)S(1)}, u32[]{:S(2)}, u32[]{:S(2)}) collective-permute-start(bf16[160,256]{1,0:T(8,128)(2,1)S(1)} %copy-done.43), channel_id=1, source_target_pairs={{0,24},{4,28},{8,16},{12,20},{16,8},{20,12},{24,0},{28,4},{1,25},{... | collective-permute-start | bytes 245768 | tf_op jit(solution)/shard_map/ppermute | solution.py:375
  127.8 10.1 %copy-start.21 = (bf16[160,256]{1,0:T(8,128)(2,1)}, bf16[160,256]{1,0:T(8,128)(2,1)S(1)}, u32[]{:S(2)}) copy-start(bf16[160,256]{1,0:T(8,128)(2,1)S(1)} %collective-permute-done.22.refs_9_) | copy-start | bytes 245764
  127.8 10.2 %collective-permute-start.24 = (bf16[160,256]{1,0:T(8,128)(2,1)S(1)}, bf16[160,256]{1,0:T(8,128)(2,1)S(1)}, u32[]{:S(2)}, u32[]{:S(2)}) collective-permute-start(bf16[160,256]{1,0:T(8,128)(2,1)S(1)} %copy-done.41), channel_id=1, source_target_pairs={{0,28},{4,24},{8,20},{12,16},{16,12},{20,8},{24,4},{28,0},{1,29},{... | collective-permute-start | bytes 245768 | tf_op jit(solution)/shard_map/ppermute | solution.py:375
  138.8 60.0 %all-to-all-start.2 = ((bf16[8,288,256]{2,1,0:T(8,128)(2,1)}), bf16[8,288,256]{2,1,0:T(8,128)(2,1)S(1)}, u32[]{:S(2)}, u32[]{:S(2)}) async-start(bf16[8,288,256]{2,1,0:T(8,128)(2,1)} %attention_back.2), calls=%async_computation.2 | async-start | bytes 2359296 | tf_op jit(solution)/shard_map/all_to_all | solution.py:349
  146.0 1.2 collective-permute-start.25
  147.2 3.8 %collective-permute-start.26 = (f32[8,640]{1,0:T(8,128)S(1)}, f32[8,640]{1,0:T(8,128)S(1)}, u32[]{:S(2)}, u32[]{:S(2)}) collective-permute-start(f32[8,640]{1,0:T(8,128)S(1)} %add.89), channel_id=1, source_target_pairs={{0,2},{1,3},{2,0},{3,1},{4,6},{5,7},{6,4},{7,5},{8,10},{9,11},{10,... | collective-permute-start | bytes 61448 | tf_op jit(solution)/shard_map/ppermute | solution.py:566
  151.0 22.4 %copy-start.35 = (bf16[160,256]{1,0:T(8,128)(2,1)S(1)}, bf16[160,256]{1,0:T(8,128)(2,1)}, u32[]{:S(2)}) copy-start(bf16[160,256]{1,0:T(8,128)(2,1)} %get-tuple-element.85) | copy-start | bytes 245764
  151.0 22.4 %copy-start.36 = (bf16[160,256]{1,0:T(8,128)(2,1)S(1)}, bf16[160,256]{1,0:T(8,128)(2,1)}, u32[]{:S(2)}) copy-start(bf16[160,256]{1,0:T(8,128)(2,1)} %get-tuple-element.90) | copy-start | bytes 245764
  159.6 9.0 %collective-permute-start.27 = (bf16[336,256]{1,0:T(8,128)(2,1)}, bf16[336,256]{1,0:T(8,128)(2,1)S(1)}, u32[]{:S(2)}, u32[]{:S(2)}) collective-permute-start(bf16[336,256]{1,0:T(8,128)(2,1)} %get-tuple-element.120), channel_id=1, source_target_pairs={{0,4},{4,0},{8,12},{12,8},{16,20},{20,16},{24,28},{28,24},{1,5},{5... | collective-permute-start | bytes 516104 | tf_op jit(solution)/shard_map/ppermute | solution.py:375
  161.1 11.5 %collective-permute-start.28 = (bf16[336,256]{1,0:T(8,128)(2,1)}, bf16[336,256]{1,0:T(8,128)(2,1)S(1)}, u32[]{:S(2)}, u32[]{:S(2)}) collective-permute-start(bf16[336,256]{1,0:T(8,128)(2,1)} %get-tuple-element.121), channel_id=1, source_target_pairs={{0,8},{4,12},{8,0},{12,4},{16,24},{20,28},{24,16},{28,20},{1,9},{5... | collective-permute-start | bytes 516104 | tf_op jit(solution)/shard_map/ppermute | solution.py:375
  161.7 14.9 %collective-permute-start.29 = (bf16[336,256]{1,0:T(8,128)(2,1)}, bf16[336,256]{1,0:T(8,128)(2,1)S(1)}, u32[]{:S(2)}, u32[]{:S(2)}) collective-permute-start(bf16[336,256]{1,0:T(8,128)(2,1)} %get-tuple-element.122), channel_id=1, source_target_pairs={{0,12},{4,8},{8,4},{12,0},{16,28},{20,24},{24,20},{28,16},{1,13},{... | collective-permute-start | bytes 516104 | tf_op jit(solution)/shard_map/ppermute | solution.py:375
  163.1 24.7 %collective-permute-start.30 = (bf16[336,256]{1,0:T(8,128)(2,1)}, bf16[336,256]{1,0:T(8,128)(2,1)S(1)}, u32[]{:S(2)}, u32[]{:S(2)}) collective-permute-start(bf16[336,256]{1,0:T(8,128)(2,1)} %get-tuple-element.123), channel_id=1, source_target_pairs={{0,16},{4,20},{8,24},{12,28},{16,0},{20,4},{24,8},{28,12},{1,17},{... | collective-permute-start | bytes 516104 | tf_op jit(solution)/shard_map/ppermute | solution.py:375
  165.5 26.0 %collective-permute-start.31 = (bf16[336,256]{1,0:T(8,128)(2,1)}, bf16[336,256]{1,0:T(8,128)(2,1)S(1)}, u32[]{:S(2)}, u32[]{:S(2)}) collective-permute-start(bf16[336,256]{1,0:T(8,128)(2,1)} %get-tuple-element.124), channel_id=1, source_target_pairs={{0,20},{4,16},{8,28},{12,24},{16,4},{20,0},{24,12},{28,8},{1,21},{... | collective-permute-start | bytes 516104 | tf_op jit(solution)/shard_map/ppermute | solution.py:375
  168.6 8.0 %copy-start.25 = (bf16[336,256]{1,0:T(8,128)(2,1)}, bf16[336,256]{1,0:T(8,128)(2,1)S(1)}, u32[]{:S(2)}) copy-start(bf16[336,256]{1,0:T(8,128)(2,1)S(1)} %collective-permute-done.27.refs_13_) | copy-start | bytes 516100
  168.6 27.8 %collective-permute-start.32 = (bf16[336,256]{1,0:T(8,128)(2,1)}, bf16[336,256]{1,0:T(8,128)(2,1)S(1)}, u32[]{:S(2)}, u32[]{:S(2)}) collective-permute-start(bf16[336,256]{1,0:T(8,128)(2,1)} %get-tuple-element.125), channel_id=1, source_target_pairs={{0,24},{4,28},{8,16},{12,20},{16,8},{20,12},{24,0},{28,4},{1,25},{... | collective-permute-start | bytes 516104 | tf_op jit(solution)/shard_map/ppermute | solution.py:375
  172.6 26.2 %copy-start.26 = (bf16[336,256]{1,0:T(8,128)(2,1)}, bf16[336,256]{1,0:T(8,128)(2,1)S(1)}, u32[]{:S(2)}) copy-start(bf16[336,256]{1,0:T(8,128)(2,1)S(1)} %collective-permute-done.28.refs_14_) | copy-start | bytes 516100
  172.6 26.2 %collective-permute-start.33 = (bf16[336,256]{1,0:T(8,128)(2,1)}, bf16[336,256]{1,0:T(8,128)(2,1)S(1)}, u32[]{:S(2)}, u32[]{:S(2)}) collective-permute-start(bf16[336,256]{1,0:T(8,128)(2,1)} %get-tuple-element.126), channel_id=1, source_target_pairs={{0,28},{4,24},{8,20},{12,16},{16,12},{20,8},{24,4},{28,0},{1,29},{... | collective-permute-start | bytes 516104 | tf_op jit(solution)/shard_map/ppermute | solution.py:375
  176.6 22.2 %copy-start.27 = (bf16[336,256]{1,0:T(8,128)(2,1)}, bf16[336,256]{1,0:T(8,128)(2,1)S(1)}, u32[]{:S(2)}) copy-start(bf16[336,256]{1,0:T(8,128)(2,1)S(1)} %collective-permute-done.29.refs_15_) | copy-start | bytes 516100
  187.8 11.0 %copy-start.28 = (bf16[336,256]{1,0:T(8,128)(2,1)}, bf16[336,256]{1,0:T(8,128)(2,1)S(1)}, u32[]{:S(2)}) copy-start(bf16[336,256]{1,0:T(8,128)(2,1)S(1)} %collective-permute-done.30.refs_16_) | copy-start | bytes 516100
  191.5 7.4 %copy-start.29 = (bf16[336,256]{1,0:T(8,128)(2,1)}, bf16[336,256]{1,0:T(8,128)(2,1)S(1)}, u32[]{:S(2)}) copy-start(bf16[336,256]{1,0:T(8,128)(2,1)S(1)} %collective-permute-done.31.refs_17_) | copy-start | bytes 516100
  (18 other events, 42.4 us)

commit v3 on v2

--- a/solution.py
+++ b/solution.py
@@ -120,7 +120,7 @@
 
     r = run_steps(tokens // chunk, step, jnp.zeros((RR, tokens), F32))
     for s in range(blocks):
-        r_ref[s, 0] = r[:, s * LANES : (s + 1) * LANES].astype(BF)
+        r_ref[s, 0] = r[:FR, s * LANES : (s + 1) * LANES].astype(BF)
 
 
 def pool_kernel(blocks, heads, chunk, *refs):
@@ -136,7 +136,7 @@
         v = jnp.concatenate(
             [v_refs[s][:, h * HS : (h + 1) * HS] for s in range(blocks)], axis=0
         )
-        columns.append(dot_nn(r, v)[:FR])
+        columns.append(dot_nn(r, v))
     pooled = jnp.concatenate(columns, axis=1) if heads > 1 else columns[0]
     pooled = pooled / count
     pooled_ref[...] = pooled
@@ -230,7 +230,7 @@
 
 def output_kernel(blocks, *refs):
     v_refs, (q_ref, k_ref, aug_ref, r_ref) = refs[:blocks], refs[blocks : blocks + 4]
-    send_refs, (v_ref, o_ref) = refs[blocks + 4 : -2], refs[-2:]
+    send_refs, (v_ref, o_ref) = refs[-2 - blocks : -2], refs[-2:]
     tokens = blocks * LANES
     chunk = row_chunk(tokens)
     for s in range(blocks):
@@ -257,36 +257,53 @@
     out_refs, dk_ref, dq_ref = refs[:-2], refs[-2], refs[-1]
     tokens = blocks * LANES
     chunk = row_chunk(tokens)
+    count = tokens // chunk
     plain = k_ref[0]
     keys = jnp.concatenate([plain, ones_three((tokens, LANES))], axis=1)
     values = v_ref[0]
     spread = spread_ref[...]
-    dk_ref[...] = jnp.zeros(dk_ref.shape, F32)
-
-    def step(i, carry):
+
+    def scores(i):
         at = chunk_rows(i, chunk)
-        q = q_ref[0, at]
-        s = dot_nt(jnp.concatenate([q, aug_ref[0, at]], axis=1), keys)
-        p = jnp.exp2(s * (SCALE * LOG2E))
+        s = dot_nt(jnp.concatenate([q_ref[0, at], aug_ref[0, at]], axis=1), keys)
         grad = dot_nn(m_ref[at], spread)
         delta = jnp.sum(grad * o_ref[0, at].astype(F32), axis=1, keepdims=True)
-        dp = dot_nt(grad.astype(BF), values)
-        ds = (p * (dp - delta)).astype(BF)
+        return s, dot_nt(grad.astype(BF), values), delta
+
+    def products(i, s, dp, delta):
+        at = chunk_rows(i, chunk)
+        ds = (jnp.exp2(s * (SCALE * LOG2E)) * (dp - delta)).astype(BF)
         dq_ref[at] = (dot_nn(ds, plain) * SCALE).astype(BF)
-        dk_ref[...] += dot_tn(ds, q)
-        return carry
-
-    run_steps(tokens // chunk, step, 0)
-    dk = (dk_ref[...] * SCALE).astype(BF)
+        return dot_tn(ds, q_ref[0, at])
+
+    if count <= 4:
+        ahead = scores(0)
+        total = None
+        for i in range(count):
+            now = ahead
+            if i + 1 < count:
+                ahead = scores(i + 1)
+            part = products(i, *now)
+            total = part if total is None else total + part
+        dk = (total * SCALE).astype(BF)
+    else:
+        dk_ref[...] = jnp.zeros(dk_ref.shape, F32)
+
+        def step(i, carry):
+            dk_ref[...] += products(i, *scores(i))
+            return carry
+
+        lax.fori_loop(0, count, step, 0)
+        dk = (dk_ref[...] * SCALE).astype(BF)
     me = lax.axis_index("gen")
     for s in range(blocks):
         at = slice(s * LANES, (s + 1) * LANES)
         out_ref = out_refs[s] if apart else out_refs[0].at[me ^ s]
         out_ref[:LANES] = dq_ref[at]
         out_ref[LANES : 2 * LANES] = dk[at]
-        out_ref[2 * LANES : 2 * LANES + RR] = spread[:RR]
+        out_ref[2 * LANES : 2 * LANES + FR] = spread[:FR]
         if apart:
-            out_ref[2 * LANES + RR :] = extra_ref[...]
+            out_ref[2 * LANES + FR :] = extra_ref[...]
 
 
 def received(blocks, near_refs, far_refs, s):
@@ -296,53 +313,65 @@
     return [far_refs[i + s - near] for i in range(0, len(far_refs), blocks - near)]
 
 
-def latent_kernel(blocks, lw, *refs):
-    near = blocks - blocks // 2
+def value_columns(rows, spread):
+    parts = [
+        dot_tn(rows[:, at : at + HS], spread[:, at : at + HS]).astype(BF)
+        for at in range(0, rows.shape[1], HS)
+    ]
+    return jnp.concatenate(parts, axis=1) if len(parts) > 1 else parts[0]
+
+
+def settle_kernel(blocks, lw, first, near, far, *refs):
+    near_refs, far_refs, refs = refs[:near], refs[near : near + far], refs[near + far :]
+    if first:
+        early_ref, latent_ref, rows_ref, dq_ref, dk_ref, dv_ref = refs
+    else:
+        latent_ref, rows_ref = refs
     me = lax.axis_index("gen")
     for s in range(blocks):
-        first = 0
-        for ref in received(blocks, refs[:near], refs[near:-1], s):
-            at = pl.ds(pl.multiple_of((me ^ s) * lw + first, LANES), ref.shape[1])
-            refs[-1][:, at] = ref[:LANES]
-            first += ref.shape[1]
-
-
-def finish_kernel(blocks, lw, chunk, near, far, split, *refs):
-    near_refs, far_refs = refs[:near], refs[near : near + far]
-    late_refs, early_refs = refs[near + far :][:blocks], refs[near + far + blocks : -4]
-    dq_ref, dk_ref, dv_ref, heads_ref = refs[-4:]
+        d = me ^ s
+        start = 0
+        for ref in received(blocks, near_refs, far_refs, s):
+            at = pl.ds(pl.multiple_of(d * lw + start, LANES), ref.shape[1])
+            latent_ref[:, at] = ref[:LANES]
+            start += ref.shape[1]
+        rows = [ref[LANES:] for ref in received(blocks, near_refs, far_refs, s)]
+        rows = jnp.concatenate(rows, axis=1) if len(rows) > 1 else rows[0]
+        rows_ref[s] = rows[:, first:]
+        if first:
+            spread = early_ref[d, 2 * LANES :]
+            at = pl.ds(pl.multiple_of(d * lw, LANES), first)
+            dq_ref[:, at] = early_ref[d, :LANES]
+            dk_ref[:, at] = early_ref[d, LANES : 2 * LANES]
+            dv_ref[:, at] = value_columns(rows[:, :first], spread)
+
+
+def finish_kernel(blocks, lw, chunk, *refs):
+    late_refs, rows_ref = refs[:blocks], refs[blocks]
+    dq_ref, dk_ref, dv_ref, heads_ref, made_ref, sems = refs[-6:]
     me = lax.axis_index("gen")
-    first = split * HS
-    last = lw - first
+    last = rows_ref.shape[2]
+    per = last // LANES
+    copies = []
     for s in range(blocks):
         d = me ^ s
         late = late_refs[s]
-        at = pl.ds(pl.multiple_of(d * lw + first, LANES), last)
-        dq_ref[:, at] = late[:LANES]
-        dk_ref[:, at] = late[LANES : 2 * LANES]
-        spreads = [late[2 * LANES : 2 * LANES + RR]]
-        if split:
-            at = pl.ds(pl.multiple_of(d * lw, LANES), first)
-            early = early_refs[0].at[d]
-            dq_ref[:, at] = early[:LANES]
-            dk_ref[:, at] = early[LANES : 2 * LANES]
-            spreads = [early[2 * LANES : 2 * LANES + RR]] + spreads
-        rows = [ref[LANES:] for ref in received(blocks, near_refs, far_refs, s)]
-        rows = jnp.concatenate(rows, axis=1) if len(rows) > 1 else rows[0]
-        spread = jnp.concatenate(spreads, axis=1) if split else spreads[0]
-        parts = [
-            dot_tn(rows[:, h : h + HS], spread[:, h : h + HS]).astype(BF)
-            for h in range(0, lw, HS)
-        ]
-        at = pl.ds(pl.multiple_of(d * lw, LANES), lw)
-        dv_ref[:, at] = jnp.concatenate(parts, axis=1) if len(parts) > 1 else parts[0]
-        per = last // LANES
+        at = pl.ds(pl.multiple_of(d * lw + lw - last, LANES), last)
+        made_ref[s] = value_columns(rows_ref[s], late[2 * LANES : 2 * LANES + FR])
+        for source, out in (
+            (late.at[:LANES], dq_ref),
+            (late.at[LANES : 2 * LANES], dk_ref),
+            (made_ref.at[s], dv_ref),
+        ):
+            copies.append(pltpu.make_async_copy(source, out.at[:, at], sems.at[len(copies)]))
+            copies[-1].start()
         for piece in range(chunk // LANES):
-            row = 2 * LANES + RR + piece // per * 2 * NDH
+            row = 2 * LANES + FR + piece // per * NDH
             lane = piece % per * LANES
-            both = late[row : row + 2 * NDH, lane : lane + LANES].astype(F32)
             at = pl.ds(pl.multiple_of(d * chunk + piece * LANES, LANES), LANES)
-            heads_ref[:, at] = both[:NDH] + both[NDH:]
+            heads_ref[:, at] = late[row : row + NDH, lane : lane + LANES].astype(F32)
+    for copy in copies:
+        copy.wait()
 
 
 def exchange(array):
@@ -421,7 +450,7 @@
 
     head_block = pl.BlockSpec((1, tokens, HS), lambda h: (h, 0, 0))
     head_shape = pltpu.HBM((heads, tokens, HS), BF)
-    r_block = pl.BlockSpec((n, 1, RR, LANES), lambda h: (0, h, 0, 0))
+    r_block = pl.BlockSpec((n, 1, FR, LANES), lambda h: (0, h, 0, 0))
     square = 2 * tokens * tokens * HS
     in_vmem = pl.BlockSpec(memory_space=pltpu.VMEM)
     anywhere = pl.BlockSpec(memory_space=pl.ANY)
@@ -436,7 +465,7 @@
             out_specs=[head_block, r_block, head_block, head_block],
             out_shape=[
                 head_shape,
-                pltpu.HBM((n, heads, RR, LANES), BF),
+                pltpu.HBM((n, heads, FR, LANES), BF),
                 head_shape,
                 head_shape,
             ],
@@ -463,31 +492,38 @@
     split = heads // 2
     parts = [(0, split), (split, heads)] if split else [(0, heads)]
 
-    def output(first, last, behind):
+    def output(first, last, behind, before):
         at = pl.BlockSpec((1, tokens, HS), lambda h: (h + first, 0, 0))
-        own = pltpu.HBM((last - first, tokens, HS), BF)
+        near_at = pl.BlockSpec((LANES + FR, HS), lambda h: (0, h + first))
+        far_at = pl.BlockSpec((LANES + FR, HS), lambda h: (0, h))
+        shared = [pltpu.HBM((LANES + FR, lw), BF)] * (n - half)
+        inputs = list(map(hbm, v + [q_rows, k_rows, aug, after(r, behind)] + before))
+        kept = list(range(n - half)) + [n, n + 1]
         with jax.named_scope("attention_output"):
-            *made, v_rows, o_rows = pl.pallas_call(
+            made = pl.pallas_call(
                 functools.partial(output_kernel, n),
                 grid=(last - first,),
                 in_specs=[pl.BlockSpec((LANES, HS), lambda h: (0, h + first))] * n
                 + [at] * 3
-                + [pl.BlockSpec((n, 1, RR, LANES), lambda h: (0, h + first, 0, 0))],
-                out_specs=[pl.BlockSpec((LANES + RR, HS), lambda h: (0, h))] * n
-                + [head_block, head_block],
-                out_shape=[pltpu.HBM((LANES + RR, (last - first) * HS), BF)] * n + [own, own],
+                + [pl.BlockSpec((n, 1, FR, LANES), lambda h: (0, h + first, 0, 0))]
+                + [anywhere] * len(before),
+                out_specs=[near_at] * (n - half) + [far_at] * half + [at] * 2,
+                out_shape=shared
+                + [pltpu.HBM((LANES + FR, (last - first) * HS), BF)] * half
+                + [head_shape] * 2,
+                input_output_aliases={n + 4 + i: kept[i] for i in range(len(before))},
                 compiler_params=params(tokens),
                 cost_estimate=pl.CostEstimate(
                     flops=2 * (last - first) * square,
                     bytes_accessed=(last - first) << 20,
                     transcendentals=(last - first) * tokens**2,
                 ),
-            )(*map(hbm, v), *map(hbm, (q_rows, k_rows, aug, after(r, behind))))
-        return made, v_rows, o_rows
-
-    outputs = [output(*parts[0], part)]
-    got = after(got, outputs[0][2])
-    mixed = [[send(outputs[0][0][s], s) for s in far]]
+            )(*inputs)
+        return made[: n - half], made[n - half : n], made[n:]
+
+    mixed_near, made, own = output(*parts[0], part, [])
+    got = after(got, own[1])
+    mixed = [[send(made[i], s) for i, s in enumerate(far)]]
 
     with jax.named_scope("discriminator"):
         direction, feature, root = pl.pallas_call(
@@ -500,16 +536,12 @@
             compiler_params=params(tokens, 0),
         )(got, head_rows)
 
-    got_back = exchange(after(direction, *mixed[0][:2]))
-    got_back = after(got_back, *mixed[0][2:])
+    got_back = exchange(after(direction, mixed[0][0]))
+    got_back = after(got_back, *mixed[0][1:])
     if split:
-        outputs.append(output(*parts[1], direction))
-        got_back = after(got_back, outputs[1][2])
-        mixed.append([send(outputs[1][0][s], s) for s in far])
-    mixed_near = []
-    for s in range(n - half):
-        block = jnp.concatenate([made[0][s] for made in outputs], axis=1) if split else outputs[0][0][s]
-        mixed_near.append(send(block, s) if s else block)
+        mixed_near, made, own = output(*parts[1], direction, list(mixed_near) + list(own))
+        got_back = after(got_back, own[1])
+        rest = made
 
     with jax.named_scope("pooled_gradient"):
         spread, head_part = pl.pallas_call(
@@ -523,13 +555,12 @@
             compiler_params=params(tokens, 0),
         )(got_back, hbm(w), pooled, meta, root, feature, picked)
 
-    def back(i, apart, extra):
-        first, last = parts[i]
+    def back(first, last, apart, extra):
         part = (last - first) * HS
         if apart:
-            block = (2 * LANES + RR + extra.shape[0], HS)
+            block = (2 * LANES + FR + extra.shape[0], HS)
         else:
-            block = (n, 2 * LANES + RR, HS)
+            block = (n, 2 * LANES + FR, HS)
         shape = block[:-1] + (part,)
         count = n if apart else 1
         at = pl.BlockSpec((1, tokens, HS), lambda h: (h + first, 0, 0))
@@ -537,7 +568,7 @@
             return pl.pallas_call(
                 functools.partial(back_kernel, n, apart),
                 grid=(last - first,),
-                in_specs=[at, at, head_block, head_block, at]
+                in_specs=[at] * 5
                 + [
                     pl.BlockSpec((tokens, LANES), lambda h: (0, 0)),
                     pl.BlockSpec((LANES, HS), lambda h: (0, h + first)),
@@ -552,48 +583,59 @@
                     bytes_accessed=(last - first) * (2 << 20),
                     transcendentals=(last - first) * tokens**2,
                 ),
-            )(*map(hbm, (q_rows, k_rows) + outputs[i][1:] + (aug,)), member, spread, extra)
-
+            )(*map(hbm, [q_rows, k_rows, *own, aug]), member, spread, extra)
+
+    mixed_near = [mixed_near[0]] + [send(mixed_near[s], s) for s in near]
+    if split:
+        mixed.append([send(after(rest[i], spread), s) for i, s in enumerate(far)])
+        spread = after(spread, mixed[1][0], *mixed_near[1:])
+    head_sum = head_part
+    if grp > 1:
+        head_sum = head_sum + lax.ppermute(head_part, "grp", [(i, i ^ 1) for i in range(grp)])
     early = []
-    if split:
-        made = back(0, False, jnp.zeros((2 * NDH, split * HS), BF))[0]
-        spread, head_part, made = lax.optimization_barrier((spread, head_part, made))
-        made = after(made, *(block for blocks in mixed for block in blocks), *mixed_near[1:])
-        early = [exchange(made)]
-
-    step = 1
+    first = split
+    if first:
+        made = back(0, first, False, jnp.zeros((NDH, first * HS), BF))[0]
+        spread, head_sum, made = lax.optimization_barrier((spread, head_sum, made))
+        early = [exchange(after(made, mixed[0][-1], *mixed[1]))]
+
+    step = 2
     while step < grp:
-        head_part = head_part + lax.ppermute(
-            head_part, "grp", [(i, i ^ step) for i in range(grp)]
+        head_sum = head_sum + lax.ppermute(
+            head_sum, "grp", [(i, i ^ step) for i in range(grp)]
         )
         step *= 2
-    high = head_part.astype(BF)
-    low = (head_part - high.astype(F32)).astype(BF)
-    late_width = lw - split * HS
+    late_width = lw - first * HS
     groups = -(-chunk // late_width)
-    extra = jnp.concatenate([high, low], axis=0)
-    extra = jnp.pad(extra, ((0, 0), (0, groups * late_width - chunk)))
-    extra = jnp.transpose(extra.reshape(2 * NDH, groups, late_width), (1, 0, 2))
-    made = back(len(parts) - 1, True, extra.reshape(groups * 2 * NDH, late_width))
+    extra = jnp.pad(head_sum.astype(BF), ((0, 0), (0, groups * late_width - chunk)))
+    extra = jnp.transpose(extra.reshape(NDH, groups, late_width), (1, 0, 2))
+    made = back(first, heads, True, extra.reshape(groups * NDH, late_width))
     late = [made[0]] + [send(made[s], s) for s in range(1, n)]
 
     whole = jax.ShapeDtypeStruct((tok, width), BF)
-    mixed = mixed_near + [block for blocks in mixed for block in blocks]
-    with jax.named_scope("latents"):
-        latents = pl.pallas_call(
-            functools.partial(latent_kernel, n, lw),
-            out_shape=whole,
+    far_blocks = [block for blocks in mixed for block in blocks]
+    frame_rows = jax.ShapeDtypeStruct((n, FR, late_width), BF)
+    with jax.named_scope("settle"):
+        latents, frame_rows, *begun = pl.pallas_call(
+            functools.partial(settle_kernel, n, lw, first * HS, n - half, len(far_blocks)),
+            out_shape=[whole, frame_rows] + ([pltpu.HBM((tok, width), BF)] * 3 if first else []),
             compiler_params=params(tokens, 0),
-        )(*map(hbm, mixed))
+        )(*map(hbm, mixed_near + far_blocks + early))
+    late[0] = after(late[0], latents)
     with jax.named_scope("finish"):
-        late[0] = after(late[0], latents)
         out_query, out_key, out_value, grad_heads = pl.pallas_call(
-            functools.partial(
-                finish_kernel, n, lw, chunk, n - half, len(mixed) - (n - half), split
-            ),
-            out_shape=[whole] * 3 + [jax.ShapeDtypeStruct((NDH, n * chunk), F32)],
+            functools.partial(finish_kernel, n, lw, chunk),
+            in_specs=[in_vmem] * (n + 1) + [anywhere] * len(begun),
+            out_specs=[anywhere] * 3 + [in_vmem],
+            out_shape=[pltpu.HBM((tok, width), BF)] * 3
+            + [jax.ShapeDtypeStruct((NDH, n * chunk), F32)],
+            input_output_aliases={n + 1 + i: i for i in range(len(begun))},
+            scratch_shapes=[
+                pltpu.VMEM((n, LANES, late_width), BF),
+                pltpu.SemaphoreType.DMA((3 * n,)),
+            ],
             compiler_params=params(tokens, 0),
-        )(*map(hbm, mixed + late + early))
+        )(*map(hbm, late), frame_rows, *map(hbm, begun))
     if chunk != columns:
         grad_heads = grad_heads.reshape(NDH, n, chunk)[:, :, :columns].reshape(NDH, dh)
 

time: 206 us -> 202 us (0.981)
  other arithmetic: 4.49 us -> 1.78 us
    ppermute x32, starting transfers between devices: 54.5 us -> 57.2 us  [send(): return lax.ppermute(array, 'gen', [(i, i ^ s) for i in range(n)])]
    concatenate x4 -> x0, other arithmetic: 2.71 us -> none  [the longest x3 2.7 us: on_device(): jnp.concatenate([made[0][s] for made in outputs], axis=1)]
    unnamed x91 -> x78, local copies, waits for them, and re-layouts: 4.29 us -> 3.49 us
  transfers between devices with their start and end apart: 37 -> 37, of which waited for: 17 -> 16; matrix products, arithmetic and copies ran while one was open for 3% -> 2% of each run, Pallas kernels for 22% -> 23%
where the time goes in v3:
time: 202 us
  starting transfers between devices  76.4 us (38%)
  waiting for transfers between devices  61.4 us (30%)
  Pallas kernels  53.3 us (26%)
  local copies, waits for them, and re-layouts  6.67 us (3%)
  between operations  2.07 us (1%)
    ppermute x32, waiting for transfers between devices, send(): return lax.ppermute(array, 'gen', [(i, i ^ s) for i in range(n)])  58.1 us
    ppermute x32, starting transfers between devices, send(): return lax.ppermute(array, 'gen', [(i, i ^ s) for i in range(n)])  57.2 us
    all_to_all x3, starting transfers between devices, exchange(): return lax.all_to_all(array, 'gen', split_axis=0, concat_axis=0, tiled=True)  17.7 us
    pallas_call x2, Pallas kernels, back(): pl.pallas_call(functools.partial(back_kernel, n, apart), grid=(last - fir...  16.2 us
    pallas_call x1, Pallas kernels, on_device(): pl.pallas_call(functools.partial(stats_kernel, n), grid=(heads,), in_spec...  11.6 us
    pallas_call x2, Pallas kernels, output(): pl.pallas_call(functools.partial(output_kernel, n), grid=(last - first,),...  9.9 us
  transfers between devices with their start and end apart: 37, of which 16 were waited for; matrix products, arithmetic and copies ran while one was open for 2% of the time, Pallas kernels for 23%

profile of v3, /device:TPU:8, one launch (start us, length us, event | category | flops | bytes accessed | tf_op | source)
XLA Modules:
  0.0 201.6 jit_solution(4316799300652877821)
XLA Ops:
  0.7 1.8 constant_dynamic-slice_fusion.1
  2.5 2.6 %collective-permute-start.9 = (bf16[2,128,512]{2,1,0:T(8,128)(2,1)S(1)}, bf16[2,128,512]{2,1,0:T(8,128)(2,1)}, u32[]{:S(2)}, u32[]{:S(2)}) collective-permute-start(bf16[2,128,512]{2,1,0:T(8,128)(2,1)S(1)} %pad_maximum_fusion.4), channel_id=1, source_target_pairs={{0,28},{4,24},{8,20},{12,16},{16,12},{20,8},{24,4},{28,0},{1,29},{... | collective-permute-start | bytes 786440 | tf_op jit(solution)/shard_map/ppermute | solution.py:404
  5.2 0.5 collective-permute-start.6
  5.7 4.4 %collective-permute-start.5 = (bf16[2,128,512]{2,1,0:T(8,128)(2,1)S(1)}, bf16[2,128,512]{2,1,0:T(8,128)(2,1)}, u32[]{:S(2)}, u32[]{:S(2)}) collective-permute-start(bf16[2,128,512]{2,1,0:T(8,128)(2,1)S(1)} %pad_maximum_fusion.2), channel_id=1, source_target_pairs={{0,20},{4,16},{8,28},{12,24},{16,4},{20,0},{24,12},{28,8},{1,21},{... | collective-permute-start | bytes 786440 | tf_op jit(solution)/shard_map/ppermute | solution.py:404
  10.2 1.6 collective-permute-start
  11.8 0.6 gather_fusion
  12.6 5.1 %collective-permute-done.refs_1_ = bf16[2,128,512]{2,1,0:T(8,128)(2,1)} collective-permute-done((bf16[2,128,512]{2,1,0:T(8,128)(2,1)S(1)}, bf16[2,128,512]{2,1,0:T(8,128)(2,1)}, u32[]{:S(2)}, u32[]{:S(2)}) %collective-permute-start) | collective-permute-done | bytes 262176 | tf_op jit(solution)/shard_map/ppermute | solution.py:404
  17.7 2.1 %collective-permute-start.12 = (bf16[2,128,512]{2,1,0:T(8,128)(2,1)S(1)}, bf16[2,128,512]{2,1,0:T(8,128)(2,1)S(1)}, u32[]{:S(2)}, u32[]{:S(2)}) collective-permute-start(bf16[2,128,512]{2,1,0:T(8,128)(2,1)S(1)} %pad_maximum_fusion.6), channel_id=1, source_target_pairs={{0,8},{4,12},{8,0},{12,4},{16,24},{20,28},{24,16},{28,20},{1,9},{5... | collective-permute-start | bytes 786440 | tf_op jit(solution)/shard_map/ppermute | solution.py:404
  19.7 0.8 dynamic-slice_bitcast_fusion
  20.5 1.4 collective-permute-start.1
  22.1 8.4 %collective-permute-done.12.refs_2_ = bf16[2,128,512]{2,1,0:T(8,128)(2,1)S(1)} collective-permute-done((bf16[2,128,512]{2,1,0:T(8,128)(2,1)S(1)}, bf16[2,128,512]{2,1,0:T(8,128)(2,1)S(1)}, u32[]{:S(2)}, u32[]{:S(2)}) %collective-permute-start.12) | collective-permute-done | bytes 262176 | tf_op jit(solution)/shard_map/ppermute | solution.py:404
  30.5 0.7 collective-permute-done.1.refs_1_
  32.1 2.9 %collective-permute-start.2 = (bf16[128,512]{1,0:T(8,128)(2,1)S(1)}, bf16[128,512]{1,0:T(8,128)(2,1)S(1)}, u32[]{:S(2)}, u32[]{:S(2)}) collective-permute-start(bf16[128,512]{1,0:T(8,128)(2,1)S(1)} %get-tuple-element.81), channel_id=1, source_target_pairs={{0,8},{4,12},{8,0},{12,4},{16,24},{20,28},{24,16},{28,20},{1,9},{5... | collective-permute-start | bytes 393224 | tf_op jit(solution)/shard_map/ppermute | solution.py:404
  35.0 5.7 %collective-permute-done.6.refs_6_ = bf16[2,128,512]{2,1,0:T(8,128)(2,1)} collective-permute-done((bf16[2,128,512]{2,1,0:T(8,128)(2,1)S(1)}, bf16[2,128,512]{2,1,0:T(8,128)(2,1)}, u32[]{:S(2)}, u32[]{:S(2)}) %collective-permute-start.6) | collective-permute-done | bytes 262176 | tf_op jit(solution)/shard_map/ppermute | solution.py:404
  40.7 4.9 %collective-permute-done.5.refs_5_ = bf16[2,128,512]{2,1,0:T(8,128)(2,1)} collective-permute-done((bf16[2,128,512]{2,1,0:T(8,128)(2,1)S(1)}, bf16[2,128,512]{2,1,0:T(8,128)(2,1)}, u32[]{:S(2)}, u32[]{:S(2)}) %collective-permute-start.5) | collective-permute-done | bytes 262176 | tf_op jit(solution)/shard_map/ppermute | solution.py:404
  45.6 4.6 %collective-permute-done.4.refs_4_ = bf16[2,128,512]{2,1,0:T(8,128)(2,1)S(1)} collective-permute-done((bf16[2,128,512]{2,1,0:T(8,128)(2,1)S(1)}, bf16[2,128,512]{2,1,0:T(8,128)(2,1)S(1)}, u32[]{:S(2)}, u32[]{:S(2)}) %collective-permute-start.4) | collective-permute-done | bytes 262176 | tf_op jit(solution)/shard_map/ppermute | solution.py:404
  50.5 1.6 collective-permute-start.10
  52.1 6.3 %collective-permute-start.8 = (bf16[128,512]{1,0:T(8,128)(2,1)S(1)}, bf16[128,512]{1,0:T(8,128)(2,1)S(1)}, u32[]{:S(2)}, u32[]{:S(2)}) collective-permute-start(bf16[128,512]{1,0:T(8,128)(2,1)S(1)} %get-tuple-element.84), channel_id=1, source_target_pairs={{0,20},{4,16},{8,28},{12,24},{16,4},{20,0},{24,12},{28,8},{1,21},{... | collective-permute-start | bytes 393224 | tf_op jit(solution)/shard_map/ppermute | solution.py:404
  58.4 1.8 collective-permute-start.3
  60.2 0.7 pad_maximum_fusion.5.refs_0_
  60.9 11.6 %softmax_stats.1 = (bf16[4,1024,128]{2,1,0:T(8,128)(2,1)}, bf16[8,4,24,128]{3,2,1,0:T(8,128)(2,1)}, bf16[4,1024,128]{2,1,0:T(8,128)(2,1)}, bf16[4,1024,128]{2,1,0:T(8,128)(2,1)}) custom-call(bf16[2,128,512]{2,1,0:T(8,128)(2,1)} %pad_maximum_fusion.5.refs_0_, bf16[2,128,512]{2,1,0:T(8,128)(2,1)} %collective-permute-done.refs_1_, ...), custom_call_target="tpu_custom_call" | custom-call | flops 1073741824 | bytes 4194304 | tf_op jit(solution)/shard_map/softmax_stats/pallas_call | solution.py:460
  72.7 1.0 copy-done.2
  73.7 3.9 %pool_project.1 = (bf16[8,24,768]{2,1,0:T(8,128)(2,1)}, f32[24,512]{1,0:T(8,128)S(1)}) custom-call(bf16[128,512]{1,0:T(8,128)(2,1)S(1)} %get-tuple-element.175.refs_0_, bf16[128,512]{1,0:T(8,128)(2,1)S(1)} %collective-permute-done.1.refs_1_, bf16[128,512]{1,0:T(8,128)(2,1)S(1)} %collective-permute-done.2.refs_2_, ...), custom_call_target="tpu_custom_call" | custom-call | tf_op jit(solution)/shard_map/pool_project/pallas_call | solution.py:479
  77.6 6.9 %all-to-all-start = ((bf16[8,24,768]{2,1,0:T(8,128)(2,1)}), bf16[8,24,768]{2,1,0:T(8,128)(2,1)S(1)}, u32[]{:S(2)}, u32[]{:S(2)}) async-start(bf16[8,24,768]{2,1,0:T(8,128)(2,1)} %get-tuple-element.93), calls=%async_computation | async-start | bytes 589824 | tf_op jit(solution)/shard_map/all_to_all | solution.py:378
  84.6 4.9 %attention_output.2 = (bf16[152,512]{1,0:T(8,128)(2,1)}, bf16[152,512]{1,0:T(8,128)(2,1)}, bf16[152,512]{1,0:T(8,128)(2,1)}, bf16[152,512]{1,0:T(8,128)(2,1)}, b...) custom-call(bf16[128,512]{1,0:T(8,128)(2,1)} %copy-done.1, ...), custom_call_target="tpu_custom_call" | custom-call | flops 1073741824 | bytes 2097152 | tf_op jit(solution)/shard_map/attention_output/pallas_call | solution.py:503
  89.6 2.4 %collective-permute-start.17 = (bf16[152,256]{1,0:T(8,128)(2,1)}, bf16[152,256]{1,0:T(8,128)(2,1)S(1)}, u32[]{:S(2)}, u32[]{:S(2)}) collective-permute-start(bf16[152,256]{1,0:T(8,128)(2,1)} %get-tuple-element.108), channel_id=1, source_target_pairs={{0,16},{4,20},{8,24},{12,28},{16,0},{20,4},{24,8},{28,12},{1,17},{... | collective-permute-start | bytes 233480 | tf_op jit(solution)/shard_map/ppermute | solution.py:404
  92.2 0.9 discriminator.1
  93.2 2.0 collective-permute-done.17.refs_4_
  95.2 6.8 %all-to-all-start.1 = ((bf16[8,24,768]{2,1,0:T(8,128)(2,1)}), bf16[8,24,768]{2,1,0:T(8,128)(2,1)S(1)}, u32[]{:S(2)}, u32[]{:S(2)}) async-start(bf16[8,24,768]{2,1,0:T(8,128)(2,1)} %get-tuple-element.113), calls=%async_computation.1 | async-start | bytes 589824 | tf_op jit(solution)/shard_map/all_to_all | solution.py:378
  102.0 3.3 %collective-permute-start.18 = (bf16[152,256]{1,0:T(8,128)(2,1)}, bf16[152,256]{1,0:T(8,128)(2,1)S(1)}, u32[]{:S(2)}, u32[]{:S(2)}) collective-permute-start(bf16[152,256]{1,0:T(8,128)(2,1)} %get-tuple-element.109), channel_id=1, source_target_pairs={{0,20},{4,16},{8,28},{12,24},{16,4},{20,0},{24,12},{28,8},{1,21},{... | collective-permute-start | bytes 233480 | tf_op jit(solution)/shard_map/ppermute | solution.py:404
  105.3 2.0 %collective-permute-start.20 = (bf16[152,256]{1,0:T(8,128)(2,1)}, bf16[152,256]{1,0:T(8,128)(2,1)S(1)}, u32[]{:S(2)}, u32[]{:S(2)}) collective-permute-start(bf16[152,256]{1,0:T(8,128)(2,1)} %get-tuple-element.111), channel_id=1, source_target_pairs={{0,28},{4,24},{8,20},{12,16},{16,12},{20,8},{24,4},{28,0},{1,29},{... | collective-permute-start | bytes 233480 | tf_op jit(solution)/shard_map/ppermute | solution.py:404
  107.3 5.0 %attention_output.3 = (bf16[152,512]{1,0:T(8,128)(2,1)}, bf16[152,512]{1,0:T(8,128)(2,1)}, bf16[152,512]{1,0:T(8,128)(2,1)}, bf16[152,512]{1,0:T(8,128)(2,1)}, b...) custom-call(bf16[128,512]{1,0:T(8,128)(2,1)} %copy-done.1, ...), custom_call_target="tpu_custom_call", output_to_operand_aliasing={{0}: (12, {}), {1}: (13, {}), {2}: (14, {}), {3}: (15, {}),... | custom-call | flops 1073741824 | bytes 2097152 | tf_op jit(solution)/shard_map/attention_output/pallas_call | solution.py:503
  112.3 1.5 collective-permute-start.14
  113.8 2.4 %collective-permute-start.15 = (bf16[152,512]{1,0:T(8,128)(2,1)}, bf16[152,512]{1,0:T(8,128)(2,1)S(1)}, u32[]{:S(2)}, u32[]{:S(2)}) collective-permute-start(bf16[152,512]{1,0:T(8,128)(2,1)} %get-tuple-element.106), channel_id=1, source_target_pairs={{0,8},{4,12},{8,0},{12,4},{16,24},{20,28},{24,16},{28,20},{1,9},{5... | collective-permute-start | bytes 466952 | tf_op jit(solution)/shard_map/ppermute | solution.py:404
  116.1 1.5 collective-permute-start.16
  117.6 0.3 collective-permute-done.20.refs_7_
  118.0 3.2 %pooled_gradient.1 = (bf16[128,512]{1,0:T(8,128)(2,1)S(1)}, f32[8,640]{1,0:T(8,128)S(1)}) custom-call(bf16[8,24,768]{2,1,0:T(8,128)(2,1)S(1)} %all-to-all-done.1.got_ref, bf16[512,5120]{1,0:T(8,128)(2,1)} %w_hbm.1, f32[24,512]{1,0:T(8,128)S(1)} %get-tuple-element.117.pooled_ref, f32[24,128]{1,0:T(8,128)S(1)} %broadcast_select_fusion.refs_9_.meta_ref, ...), custom_call_target="tpu_custom_call" | custom-call | tf_op jit(solution)/shard_map/pooled_gradient/pallas_call | solution.py:547
  121.2 0.4 collective-permute-start.21
  121.8 1.0 collective-permute-done.25
  122.8 2.4 %collective-permute-start.24 = (bf16[152,256]{1,0:T(8,128)(2,1)S(1)}, bf16[152,256]{1,0:T(8,128)(2,1)S(1)}, u32[]{:S(2)}, u32[]{:S(2)}) collective-permute-start(bf16[152,256]{1,0:T(8,128)(2,1)S(1)} %copy-done.36), channel_id=1, source_target_pairs={{0,28},{4,24},{8,20},{12,16},{16,12},{20,8},{24,4},{28,0},{1,29},{... | collective-permute-start | bytes 233480 | tf_op jit(solution)/shard_map/ppermute | solution.py:404
  125.1 0.6 collective-permute-start.23
  125.8 4.5 %collective-permute-start.22 = (bf16[152,256]{1,0:T(8,128)(2,1)S(1)}, bf16[152,256]{1,0:T(8,128)(2,1)S(1)}, u32[]{:S(2)}, u32[]{:S(2)}) collective-permute-start(bf16[152,256]{1,0:T(8,128)(2,1)S(1)} %copy-done.34), channel_id=1, source_target_pairs={{0,20},{4,16},{8,28},{12,24},{16,4},{20,0},{24,12},{28,8},{1,21},{... | collective-permute-start | bytes 233480 | tf_op jit(solution)/shard_map/ppermute | solution.py:404
  130.3 8.1 %attention_back.2 = bf16[8,280,256]{2,1,0:T(8,128)(2,1)} custom-call(bf16[4,1024,128]{2,1,0:T(8,128)(2,1)} %get-tuple-element.89.refs_8_.q_ref, bf16[4,1024,128]{2,1,0:T(8,128)(2,1)} %get-tuple-element.90.refs_9_.k_ref, bf16[4,1024,128]{2,1,0:T(8,128)(2,1)} %get-tuple-element.130.v_ref, bf16[4,1024,128]{2,1,0:T(8,128)(2,1)} %get-tuple-element.115.o_ref, ...), custom_call_target="tpu_custom_call" | custom-call | flops 2147483648 | bytes 4194304 | tf_op jit(solution)/shard_map/attention_back/pallas_call | solution.py:568
  138.5 0.6 copy-done.28
  139.1 3.9 %all-to-all-start.2 = ((bf16[8,280,256]{2,1,0:T(8,128)(2,1)}), bf16[8,280,256]{2,1,0:T(8,128)(2,1)S(1)}, u32[]{:S(2)}, u32[]{:S(2)}) async-start(bf16[8,280,256]{2,1,0:T(8,128)(2,1)} %attention_back.2), calls=%async_computation.2 | async-start | bytes 2293760 | tf_op jit(solution)/shard_map/all_to_all | solution.py:378
  143.1 1.5 collective-permute-start.26
  144.6 2.3 %collective-permute-done.26 = f32[8,640]{1,0:T(8,128)S(1)} collective-permute-done((f32[8,640]{1,0:T(8,128)S(1)}, f32[8,640]{1,0:T(8,128)S(1)}, u32[]{:S(2)}, u32[]{:S(2)}) %collective-permute-start.26) | collective-permute-done | bytes 20512 | tf_op jit(solution)/shard_map/ppermute | solution.py:604
  146.9 8.1 %attention_back.3 = (bf16[304,256]{1,0:T(8,128)(2,1)}, bf16[304,256]{1,0:T(8,128)(2,1)}, bf16[304,256]{1,0:T(8,128)(2,1)}, bf16[304,256]{1,0:T(8,128)(2,1)}, bf1...) custom-call(bf16[4,1024,128]{2,1,0:T(8,128)(2,1)} %get-tuple-element.89.r, ...), custom_call_target="tpu_custom_call" | custom-call | flops 2147483648 | bytes 4194304 | tf_op jit(solution)/shard_map/attention_back/pallas_call | solution.py:568
  155.0 1.5 collective-permute-start.27
  156.5 0.6 collective-permute-start.28
  157.1 1.5 collective-permute-start.29
  158.5 2.4 %collective-permute-start.30 = (bf16[304,256]{1,0:T(8,128)(2,1)}, bf16[304,256]{1,0:T(8,128)(2,1)S(1)}, u32[]{:S(2)}, u32[]{:S(2)}) collective-permute-start(bf16[304,256]{1,0:T(8,128)(2,1)} %get-tuple-element.141), channel_id=1, source_target_pairs={{0,16},{4,20},{8,24},{12,28},{16,0},{20,4},{24,8},{28,12},{1,17},{... | collective-permute-start | bytes 466952 | tf_op jit(solution)/shard_map/ppermute | solution.py:404
  160.9 1.5 collective-permute-start.31
  162.4 1.3 collective-permute-done.27.refs_1_
  163.8 3.4 %collective-permute-done.28.refs_2_ = bf16[304,256]{1,0:T(8,128)(2,1)S(1)} collective-permute-done((bf16[304,256]{1,0:T(8,128)(2,1)}, bf16[304,256]{1,0:T(8,128)(2,1)S(1)}, u32[]{:S(2)}, u32[]{:S(2)}) %collective-permute-start.28) | collective-permute-done | bytes 155680 | tf_op jit(solution)/shard_map/ppermute | solution.py:404
  167.2 3.3 %collective-permute-start.33 = (bf16[304,256]{1,0:T(8,128)(2,1)}, bf16[304,256]{1,0:T(8,128)(2,1)S(1)}, u32[]{:S(2)}, u32[]{:S(2)}) collective-permute-start(bf16[304,256]{1,0:T(8,128)(2,1)} %get-tuple-element.144), channel_id=1, source_target_pairs={{0,28},{4,24},{8,20},{12,16},{16,12},{20,8},{24,4},{28,0},{1,29},{... | collective-permute-start | bytes 466952 | tf_op jit(solution)/shard_map/ppermute | solution.py:404
  170.5 1.0 copy-done.10
  171.5 4.0 %settle.1 = (bf16[128,4096]{1,0:T(8,128)(2,1)}, bf16[8,24,256]{2,1,0:T(8,128)(2,1)S(1)}, bf16[128,4096]{1,0:T(8,128)(2,1)}, bf16[128,4096]{1,0:T(8,128)(2,1)}, bf16[128,4096]{1,0:T(8,128)(2,1)}) custom-call(bf16[152,512]{1,0:T(8,128)(2,1)} %get-tuple-element.104.refs_0_, bf16[152,512]{1,0:T(8,128)(2,1)} %copy-done.13, bf16[152,512]{1,0:T(8,128)(2,1)} %copy-done.14, ...), custom_call_target="tpu_custom_call" | custom-call | tf_op jit(solution)/shard_map/settle/pallas_call | solution.py:619
  175.5 9.4 %collective-permute-done.30.refs_4_ = bf16[304,256]{1,0:T(8,128)(2,1)S(1)} collective-permute-done((bf16[304,256]{1,0:T(8,128)(2,1)}, bf16[304,256]{1,0:T(8,128)(2,1)S(1)}, u32[]{:S(2)}, u32[]{:S(2)}) %collective-permute-start.30) | collective-permute-done | bytes 155680 | tf_op jit(solution)/shard_map/ppermute | solution.py:404
  185.0 3.3 %collective-permute-done.31.refs_5_ = bf16[304,256]{1,0:T(8,128)(2,1)S(1)} collective-permute-done((bf16[304,256]{1,0:T(8,128)(2,1)}, bf16[304,256]{1,0:T(8,128)(2,1)S(1)}, u32[]{:S(2)}, u32[]{:S(2)}) %collective-permute-start.31) | collective-permute-done | bytes 155680 | tf_op jit(solution)/shard_map/ppermute | solution.py:404
  188.3 6.0 %collective-permute-done.32.refs_6_ = bf16[304,256]{1,0:T(8,128)(2,1)S(1)} collective-permute-done((bf16[304,256]{1,0:T(8,128)(2,1)}, bf16[304,256]{1,0:T(8,128)(2,1)S(1)}, u32[]{:S(2)}, u32[]{:S(2)}) %collective-permute-start.32) | collective-permute-done | bytes 155680 | tf_op jit(solution)/shard_map/ppermute | solution.py:404
  194.3 3.0 %collective-permute-done.33.refs_7_ = bf16[304,256]{1,0:T(8,128)(2,1)S(1)} collective-permute-done((bf16[304,256]{1,0:T(8,128)(2,1)}, bf16[304,256]{1,0:T(8,128)(2,1)S(1)}, u32[]{:S(2)}, u32[]{:S(2)}) %collective-permute-start.33) | collective-permute-done | bytes 155680 | tf_op jit(solution)/shard_map/ppermute | solution.py:404
  197.3 0.6 copy-done.22
  197.9 3.5 %finish.1 = (bf16[128,4096]{1,0:T(8,128)(2,1)}, bf16[128,4096]{1,0:T(8,128)(2,1)}, bf16[128,4096]{1,0:T(8,128)(2,1)}, f32[8,5120]{1,0:T(8,128)}) custom-call(bf16[304,256]{1,0:T(8,128)(2,1)} %get-tuple-element.137.refs_0_, bf16[304,256]{1,0:T(8,128)(2,1)} %copy-done.16, ...), custom_call_target="tpu_custom_call", output_to_operand_aliasing={{0}: (9, {}), {1}: (10, {}), {2}: (11, {})} | custom-call | tf_op jit(solution)/shard_map/finish/pallas_call | solution.py:626
  (129 shorter events, 2.0 us)
Async XLA Ops:
  0.6 83.9 %copy-start = (f32[8,5120]{1,0:T(8,128)S(1)}, f32[8,5120]{1,0:T(8,128)}, u32[]{:S(2)}) copy-start(f32[8,5120]{1,0:T(8,128)} %param.12) | copy-start | bytes 491524
  2.5 9.3 %copy-start.12 = (s32[1,1024]{1,0:T(1,128)S(1)}, s32[1,1024]{1,0:T(1,128)}, u32[]{:S(2)}) copy-start(s32[1,1024]{1,0:T(1,128)} %param.13) | copy-start | bytes 12292
  2.5 29.5 %collective-permute-start.9 = (bf16[2,128,512]{2,1,0:T(8,128)(2,1)S(1)}, bf16[2,128,512]{2,1,0:T(8,128)(2,1)}, u32[]{:S(2)}, u32[]{:S(2)}) collective-permute-start(bf16[2,128,512]{2,1,0:T(8,128)(2,1)S(1)} %pad_maximum_fusion.4), channel_id=1, source_target_pairs={{0,28},{4,24},{8,20},{12,16},{16,12},{20,8},{24,4},{28,0},{1,29},{... | collective-permute-start | bytes 786440 | tf_op jit(solution)/shard_map/ppermute | solution.py:404
  5.2 14.6 %copy-start.11 = (bf16[1,128,4096]{2,1,0:T(8,128)(2,1)S(1)}, bf16[1,128,4096]{2,1,0:T(8,128)(2,1)}, u32[]{:S(2)}) copy-start(bf16[1,128,4096]{2,1,0:T(8,128)(2,1)} %param.10) | copy-start | bytes 3145732
  5.2 35.5 %collective-permute-start.6 = (bf16[2,128,512]{2,1,0:T(8,128)(2,1)S(1)}, bf16[2,128,512]{2,1,0:T(8,128)(2,1)}, u32[]{:S(2)}, u32[]{:S(2)}) collective-permute-start(bf16[2,128,512]{2,1,0:T(8,128)(2,1)S(1)} %pad_maximum_fusion.3), channel_id=1, source_target_pairs={{0,24},{4,28},{8,16},{12,20},{16,8},{20,12},{24,0},{28,4},{1,25},{... | collective-permute-start | bytes 786440 | tf_op jit(solution)/shard_map/ppermute | solution.py:404
  5.7 39.9 %collective-permute-start.5 = (bf16[2,128,512]{2,1,0:T(8,128)(2,1)S(1)}, bf16[2,128,512]{2,1,0:T(8,128)(2,1)}, u32[]{:S(2)}, u32[]{:S(2)}) collective-permute-start(bf16[2,128,512]{2,1,0:T(8,128)(2,1)S(1)} %pad_maximum_fusion.2), channel_id=1, source_target_pairs={{0,20},{4,16},{8,28},{12,24},{16,4},{20,0},{24,12},{28,8},{1,21},{... | collective-permute-start | bytes 786440 | tf_op jit(solution)/shard_map/ppermute | solution.py:404
  10.2 7.5 %collective-permute-start = (bf16[2,128,512]{2,1,0:T(8,128)(2,1)S(1)}, bf16[2,128,512]{2,1,0:T(8,128)(2,1)}, u32[]{:S(2)}, u32[]{:S(2)}) collective-permute-start(bf16[2,128,512]{2,1,0:T(8,128)(2,1)S(1)} %pad_maximum_fusion), channel_id=1, source_target_pairs={{0,4},{4,0},{8,12},{12,8},{16,20},{20,16},{24,28},{28,24},{1,5},{5... | collective-permute-start | bytes 786440 | tf_op jit(solution)/shard_map/ppermute | solution.py:404
  12.6 48.3 %copy-start.38 = (s32[1,21]{1,0:T(1,128)S(1)}, s32[1,21]{1,0:T(1,128)}, u32[]{:S(2)}) copy-start(s32[1,21]{1,0:T(1,128)} %param.14) | copy-start | bytes 256
  17.7 12.9 %collective-permute-start.12 = (bf16[2,128,512]{2,1,0:T(8,128)(2,1)S(1)}, bf16[2,128,512]{2,1,0:T(8,128)(2,1)S(1)}, u32[]{:S(2)}, u32[]{:S(2)}) collective-permute-start(bf16[2,128,512]{2,1,0:T(8,128)(2,1)S(1)} %pad_maximum_fusion.6), channel_id=1, source_target_pairs={{0,8},{4,12},{8,0},{12,4},{16,24},{20,28},{24,16},{28,20},{1,9},{5... | collective-permute-start | bytes 786440 | tf_op jit(solution)/shard_map/ppermute | solution.py:404
  20.5 52.1 %copy-start.1 = (bf16[128,512]{1,0:T(8,128)(2,1)}, bf16[128,512]{1,0:T(8,128)(2,1)S(1)}, u32[]{:S(2)}) copy-start(bf16[128,512]{1,0:T(8,128)(2,1)S(1)} %get-tuple-element.175.refs_0_) | copy-start | bytes 393220
  20.5 10.7 %collective-permute-start.1 = (bf16[128,512]{1,0:T(8,128)(2,1)S(1)}, bf16[128,512]{1,0:T(8,128)(2,1)S(1)}, u32[]{:S(2)}, u32[]{:S(2)}) collective-permute-start(bf16[128,512]{1,0:T(8,128)(2,1)S(1)} %get-tuple-element.80), channel_id=1, source_target_pairs={{0,4},{4,0},{8,12},{12,8},{16,20},{20,16},{24,28},{28,24},{1,5},{5... | collective-permute-start | bytes 393224 | tf_op jit(solution)/shard_map/ppermute | solution.py:404
  30.5 29.6 %copy-start.31 = (bf16[2,128,512]{2,1,0:T(8,128)(2,1)}, bf16[2,128,512]{2,1,0:T(8,128)(2,1)S(1)}, u32[]{:S(2)}) copy-start(bf16[2,128,512]{2,1,0:T(8,128)(2,1)S(1)} %collective-permute-done.12.refs_2_) | copy-start | bytes 786436
  30.5 19.7 %collective-permute-start.4 = (bf16[2,128,512]{2,1,0:T(8,128)(2,1)S(1)}, bf16[2,128,512]{2,1,0:T(8,128)(2,1)S(1)}, u32[]{:S(2)}, u32[]{:S(2)}) collective-permute-start(bf16[2,128,512]{2,1,0:T(8,128)(2,1)S(1)} %pad_maximum_fusion.1), channel_id=1, source_target_pairs={{0,16},{4,20},{8,24},{12,28},{16,0},{20,4},{24,8},{28,12},{1,17},{... | collective-permute-start | bytes 786440 | tf_op jit(solution)/shard_map/ppermute | solution.py:404
  31.2 41.4 %copy-start.3 = (bf16[128,512]{1,0:T(8,128)(2,1)}, bf16[128,512]{1,0:T(8,128)(2,1)S(1)}, u32[]{:S(2)}) copy-start(bf16[128,512]{1,0:T(8,128)(2,1)S(1)} %collective-permute-done.1.refs_1_) | copy-start | bytes 393220
  31.2 27.1 %collective-permute-start.13 = (bf16[2,128,512]{2,1,0:T(8,128)(2,1)S(1)}, bf16[2,128,512]{2,1,0:T(8,128)(2,1)S(1)}, u32[]{:S(2)}, u32[]{:S(2)}) collective-permute-start(bf16[2,128,512]{2,1,0:T(8,128)(2,1)S(1)} %pad_maximum_fusion.7), channel_id=1, source_target_pairs={{0,12},{4,8},{8,4},{12,0},{16,28},{20,24},{24,20},{28,16},{1,13},{... | collective-permute-start | bytes 786440 | tf_op jit(solution)/shard_map/ppermute | solution.py:404
  32.1 26.3 %collective-permute-start.2 = (bf16[128,512]{1,0:T(8,128)(2,1)S(1)}, bf16[128,512]{1,0:T(8,128)(2,1)S(1)}, u32[]{:S(2)}, u32[]{:S(2)}) collective-permute-start(bf16[128,512]{1,0:T(8,128)(2,1)S(1)} %get-tuple-element.81), channel_id=1, source_target_pairs={{0,8},{4,12},{8,0},{12,4},{16,24},{20,28},{24,16},{28,20},{1,9},{5... | collective-permute-start | bytes 393224 | tf_op jit(solution)/shard_map/ppermute | solution.py:404
  50.2 10.7 %copy-start.32 = (bf16[2,128,512]{2,1,0:T(8,128)(2,1)}, bf16[2,128,512]{2,1,0:T(8,128)(2,1)S(1)}, u32[]{:S(2)}) copy-start(bf16[2,128,512]{2,1,0:T(8,128)(2,1)S(1)} %collective-permute-done.4.refs_4_) | copy-start | bytes 786436
  50.2 22.3 %collective-permute-start.11 = (bf16[128,512]{1,0:T(8,128)(2,1)}, bf16[128,512]{1,0:T(8,128)(2,1)S(1)}, u32[]{:S(2)}, u32[]{:S(2)}) collective-permute-start(bf16[128,512]{1,0:T(8,128)(2,1)} %get-tuple-element.86), channel_id=1, source_target_pairs={{0,28},{4,24},{8,20},{12,16},{16,12},{20,8},{24,4},{28,0},{1,29},{... | collective-permute-start | bytes 393224 | tf_op jit(solution)/shard_map/ppermute | solution.py:404
  50.5 22.0 %collective-permute-start.10 = (bf16[128,512]{1,0:T(8,128)(2,1)}, bf16[128,512]{1,0:T(8,128)(2,1)S(1)}, u32[]{:S(2)}, u32[]{:S(2)}) collective-permute-start(bf16[128,512]{1,0:T(8,128)(2,1)} %get-tuple-element.85), channel_id=1, source_target_pairs={{0,24},{4,28},{8,16},{12,20},{16,8},{20,12},{24,0},{28,4},{1,25},{... | collective-permute-start | bytes 393224 | tf_op jit(solution)/shard_map/ppermute | solution.py:404
  52.1 20.5 %collective-permute-start.8 = (bf16[128,512]{1,0:T(8,128)(2,1)S(1)}, bf16[128,512]{1,0:T(8,128)(2,1)S(1)}, u32[]{:S(2)}, u32[]{:S(2)}) collective-permute-start(bf16[128,512]{1,0:T(8,128)(2,1)S(1)} %get-tuple-element.84), channel_id=1, source_target_pairs={{0,20},{4,16},{8,28},{12,24},{16,4},{20,0},{24,12},{28,8},{1,21},{... | collective-permute-start | bytes 393224 | tf_op jit(solution)/shard_map/ppermute | solution.py:404
  58.3 14.3 %copy-start.4 = (bf16[128,512]{1,0:T(8,128)(2,1)}, bf16[128,512]{1,0:T(8,128)(2,1)S(1)}, u32[]{:S(2)}) copy-start(bf16[128,512]{1,0:T(8,128)(2,1)S(1)} %collective-permute-done.2.refs_2_) | copy-start | bytes 393220
  58.3 14.2 %collective-permute-start.7 = (bf16[128,512]{1,0:T(8,128)(2,1)S(1)}, bf16[128,512]{1,0:T(8,128)(2,1)S(1)}, u32[]{:S(2)}, u32[]{:S(2)}) collective-permute-start(bf16[128,512]{1,0:T(8,128)(2,1)S(1)} %get-tuple-element.83), channel_id=1, source_target_pairs={{0,16},{4,20},{8,24},{12,28},{16,0},{20,4},{24,8},{28,12},{1,17},{... | collective-permute-start | bytes 393224 | tf_op jit(solution)/shard_map/ppermute | solution.py:404
  58.4 14.2 %collective-permute-start.3 = (bf16[128,512]{1,0:T(8,128)(2,1)S(1)}, bf16[128,512]{1,0:T(8,128)(2,1)S(1)}, u32[]{:S(2)}, u32[]{:S(2)}) collective-permute-start(bf16[128,512]{1,0:T(8,128)(2,1)S(1)} %get-tuple-element.82), channel_id=1, source_target_pairs={{0,12},{4,8},{8,4},{12,0},{16,28},{20,24},{24,20},{28,16},{1,13},{... | collective-permute-start | bytes 393224 | tf_op jit(solution)/shard_map/ppermute | solution.py:404
  72.5 5.1 %copy-start.5 = (bf16[128,512]{1,0:T(8,128)(2,1)}, bf16[128,512]{1,0:T(8,128)(2,1)S(1)}, u32[]{:S(2)}) copy-start(bf16[128,512]{1,0:T(8,128)(2,1)S(1)} %collective-permute-done.11.refs_7_) | copy-start | bytes 393220
  72.6 5.0 %copy-start.6 = (bf16[128,512]{1,0:T(8,128)(2,1)}, bf16[128,512]{1,0:T(8,128)(2,1)S(1)}, u32[]{:S(2)}) copy-start(bf16[128,512]{1,0:T(8,128)(2,1)S(1)} %collective-permute-done.10.refs_6_) | copy-start | bytes 393220
  72.6 5.0 %copy-start.7 = (bf16[128,512]{1,0:T(8,128)(2,1)}, bf16[128,512]{1,0:T(8,128)(2,1)S(1)}, u32[]{:S(2)}) copy-start(bf16[128,512]{1,0:T(8,128)(2,1)S(1)} %collective-permute-done.8.refs_5_) | copy-start | bytes 393220
  72.6 5.0 %copy-start.8 = (bf16[128,512]{1,0:T(8,128)(2,1)}, bf16[128,512]{1,0:T(8,128)(2,1)S(1)}, u32[]{:S(2)}) copy-start(bf16[128,512]{1,0:T(8,128)(2,1)S(1)} %collective-permute-done.7.refs_4_) | copy-start | bytes 393220
  72.6 5.0 %copy-start.9 = (bf16[128,512]{1,0:T(8,128)(2,1)}, bf16[128,512]{1,0:T(8,128)(2,1)S(1)}, u32[]{:S(2)}) copy-start(bf16[128,512]{1,0:T(8,128)(2,1)S(1)} %collective-permute-done.3.refs_3_) | copy-start | bytes 393220
  77.6 14.6 %all-to-all-start = ((bf16[8,24,768]{2,1,0:T(8,128)(2,1)}), bf16[8,24,768]{2,1,0:T(8,128)(2,1)S(1)}, u32[]{:S(2)}, u32[]{:S(2)}) async-start(bf16[8,24,768]{2,1,0:T(8,128)(2,1)} %get-tuple-element.93), calls=%async_computation | async-start | bytes 589824 | tf_op jit(solution)/shard_map/all_to_all | solution.py:378
  89.6 5.6 %collective-permute-start.17 = (bf16[152,256]{1,0:T(8,128)(2,1)}, bf16[152,256]{1,0:T(8,128)(2,1)S(1)}, u32[]{:S(2)}, u32[]{:S(2)}) collective-permute-start(bf16[152,256]{1,0:T(8,128)(2,1)} %get-tuple-element.108), channel_id=1, source_target_pairs={{0,16},{4,20},{8,24},{12,28},{16,0},{20,4},{24,8},{28,12},{1,17},{... | collective-permute-start | bytes 233480 | tf_op jit(solution)/shard_map/ppermute | solution.py:404
  95.2 17.1 %copy-start.23 = (bf16[152,256]{1,0:T(8,128)(2,1)}, bf16[152,256]{1,0:T(8,128)(2,1)S(1)}, u32[]{:S(2)}) copy-start(bf16[152,256]{1,0:T(8,128)(2,1)S(1)} %collective-permute-done.17.refs_4_) | copy-start | bytes 233476
  95.2 22.8 %all-to-all-start.1 = ((bf16[8,24,768]{2,1,0:T(8,128)(2,1)}), bf16[8,24,768]{2,1,0:T(8,128)(2,1)S(1)}, u32[]{:S(2)}, u32[]{:S(2)}) async-start(bf16[8,24,768]{2,1,0:T(8,128)(2,1)} %get-tuple-element.113), calls=%async_computation.1 | async-start | bytes 589824 | tf_op jit(solution)/shard_map/all_to_all | solution.py:378
  102.0 14.1 %collective-permute-start.18 = (bf16[152,256]{1,0:T(8,128)(2,1)}, bf16[152,256]{1,0:T(8,128)(2,1)S(1)}, u32[]{:S(2)}, u32[]{:S(2)}) collective-permute-start(bf16[152,256]{1,0:T(8,128)(2,1)} %get-tuple-element.109), channel_id=1, source_target_pairs={{0,20},{4,16},{8,28},{12,24},{16,4},{20,0},{24,12},{28,8},{1,21},{... | collective-permute-start | bytes 233480 | tf_op jit(solution)/shard_map/ppermute | solution.py:404
  105.3 12.4 %collective-permute-start.19 = (bf16[152,256]{1,0:T(8,128)(2,1)}, bf16[152,256]{1,0:T(8,128)(2,1)S(1)}, u32[]{:S(2)}, u32[]{:S(2)}) collective-permute-start(bf16[152,256]{1,0:T(8,128)(2,1)} %get-tuple-element.110), channel_id=1, source_target_pairs={{0,24},{4,28},{8,16},{12,20},{16,8},{20,12},{24,0},{28,4},{1,25},{... | collective-permute-start | bytes 233480 | tf_op jit(solution)/shard_map/ppermute | solution.py:404
  105.3 12.7 %collective-permute-start.20 = (bf16[152,256]{1,0:T(8,128)(2,1)}, bf16[152,256]{1,0:T(8,128)(2,1)S(1)}, u32[]{:S(2)}, u32[]{:S(2)}) collective-permute-start(bf16[152,256]{1,0:T(8,128)(2,1)} %get-tuple-element.111), channel_id=1, source_target_pairs={{0,28},{4,24},{8,20},{12,16},{16,12},{20,8},{24,4},{28,0},{1,29},{... | collective-permute-start | bytes 233480 | tf_op jit(solution)/shard_map/ppermute | solution.py:404
  112.3 12.9 %collective-permute-start.14 = (bf16[152,512]{1,0:T(8,128)(2,1)}, bf16[152,512]{1,0:T(8,128)(2,1)S(1)}, u32[]{:S(2)}, u32[]{:S(2)}) collective-permute-start(bf16[152,512]{1,0:T(8,128)(2,1)} %get-tuple-element.105), channel_id=1, source_target_pairs={{0,4},{4,0},{8,12},{12,8},{16,20},{20,16},{24,28},{28,24},{1,5},{5... | collective-permute-start | bytes 466952 | tf_op jit(solution)/shard_map/ppermute | solution.py:404
  113.8 12.0 %collective-permute-start.15 = (bf16[152,512]{1,0:T(8,128)(2,1)}, bf16[152,512]{1,0:T(8,128)(2,1)S(1)}, u32[]{:S(2)}, u32[]{:S(2)}) collective-permute-start(bf16[152,512]{1,0:T(8,128)(2,1)} %get-tuple-element.106), channel_id=1, source_target_pairs={{0,8},{4,12},{8,0},{12,4},{16,24},{20,28},{24,16},{28,20},{1,9},{5... | collective-permute-start | bytes 466952 | tf_op jit(solution)/shard_map/ppermute | solution.py:404
  116.1 5.0 %copy-start.24 = (bf16[152,256]{1,0:T(8,128)(2,1)}, bf16[152,256]{1,0:T(8,128)(2,1)S(1)}, u32[]{:S(2)}) copy-start(bf16[152,256]{1,0:T(8,128)(2,1)S(1)} %collective-permute-done.18.refs_5_) | copy-start | bytes 233476
  116.1 14.1 %collective-permute-start.16 = (bf16[152,512]{1,0:T(8,128)(2,1)}, bf16[152,512]{1,0:T(8,128)(2,1)S(1)}, u32[]{:S(2)}, u32[]{:S(2)}) collective-permute-start(bf16[152,512]{1,0:T(8,128)(2,1)} %get-tuple-element.107), channel_id=1, source_target_pairs={{0,12},{4,8},{8,4},{12,0},{16,28},{20,24},{24,20},{28,16},{1,13},{... | collective-permute-start | bytes 466952 | tf_op jit(solution)/shard_map/ppermute | solution.py:404
  117.9 7.2 %copy-start.35 = (bf16[152,256]{1,0:T(8,128)(2,1)S(1)}, bf16[152,256]{1,0:T(8,128)(2,1)}, u32[]{:S(2)}) copy-start(bf16[152,256]{1,0:T(8,128)(2,1)} %get-tuple-element.125) | copy-start | bytes 233476
  118.0 7.8 %copy-start.34 = (bf16[152,256]{1,0:T(8,128)(2,1)S(1)}, bf16[152,256]{1,0:T(8,128)(2,1)}, u32[]{:S(2)}) copy-start(bf16[152,256]{1,0:T(8,128)(2,1)} %get-tuple-element.123) | copy-start | bytes 233476
  121.2 9.1 %collective-permute-start.21 = (bf16[152,256]{1,0:T(8,128)(2,1)S(1)}, bf16[152,256]{1,0:T(8,128)(2,1)S(1)}, u32[]{:S(2)}, u32[]{:S(2)}) collective-permute-start(bf16[152,256]{1,0:T(8,128)(2,1)S(1)} %copy-done.37), channel_id=1, source_target_pairs={{0,16},{4,20},{8,24},{12,28},{16,0},{20,4},{24,8},{28,12},{1,17},{... | collective-permute-start | bytes 233480 | tf_op jit(solution)/shard_map/ppermute | solution.py:404
  121.6 1.2 collective-permute-start.25
  122.8 15.7 %collective-permute-start.24 = (bf16[152,256]{1,0:T(8,128)(2,1)S(1)}, bf16[152,256]{1,0:T(8,128)(2,1)S(1)}, u32[]{:S(2)}, u32[]{:S(2)}) collective-permute-start(bf16[152,256]{1,0:T(8,128)(2,1)S(1)} %copy-done.36), channel_id=1, source_target_pairs={{0,28},{4,24},{8,20},{12,16},{16,12},{20,8},{24,4},{28,0},{1,29},{... | collective-permute-start | bytes 233480 | tf_op jit(solution)/shard_map/ppermute | solution.py:404
  125.1 13.3 %copy-start.13 = (bf16[152,512]{1,0:T(8,128)(2,1)}, bf16[152,512]{1,0:T(8,128)(2,1)S(1)}, u32[]{:S(2)}) copy-start(bf16[152,512]{1,0:T(8,128)(2,1)S(1)} %collective-permute-done.14.refs_1_) | copy-start | bytes 466948
  125.1 13.3 %collective-permute-start.23 = (bf16[152,256]{1,0:T(8,128)(2,1)S(1)}, bf16[152,256]{1,0:T(8,128)(2,1)S(1)}, u32[]{:S(2)}, u32[]{:S(2)}) collective-permute-start(bf16[152,256]{1,0:T(8,128)(2,1)S(1)} %copy-done.35), channel_id=1, source_target_pairs={{0,24},{4,28},{8,16},{12,20},{16,8},{20,12},{24,0},{28,4},{1,25},{... | collective-permute-start | bytes 233480 | tf_op jit(solution)/shard_map/ppermute | solution.py:404
  125.8 12.6 %copy-start.14 = (bf16[152,512]{1,0:T(8,128)(2,1)}, bf16[152,512]{1,0:T(8,128)(2,1)S(1)}, u32[]{:S(2)}) copy-start(bf16[152,512]{1,0:T(8,128)(2,1)S(1)} %collective-permute-done.15.refs_2_) | copy-start | bytes 466948
  125.8 12.7 %collective-permute-start.22 = (bf16[152,256]{1,0:T(8,128)(2,1)S(1)}, bf16[152,256]{1,0:T(8,128)(2,1)S(1)}, u32[]{:S(2)}, u32[]{:S(2)}) collective-permute-start(bf16[152,256]{1,0:T(8,128)(2,1)S(1)} %copy-done.34), channel_id=1, source_target_pairs={{0,20},{4,16},{8,28},{12,24},{16,4},{20,0},{24,12},{28,8},{1,21},{... | collective-permute-start | bytes 233480 | tf_op jit(solution)/shard_map/ppermute | solution.py:404
  130.3 8.2 %copy-start.15 = (bf16[152,512]{1,0:T(8,128)(2,1)}, bf16[152,512]{1,0:T(8,128)(2,1)S(1)}, u32[]{:S(2)}) copy-start(bf16[152,512]{1,0:T(8,128)(2,1)S(1)} %collective-permute-done.16.refs_3_) | copy-start | bytes 466948
  130.3 8.2 %copy-start.27 = (bf16[152,256]{1,0:T(8,128)(2,1)}, bf16[152,256]{1,0:T(8,128)(2,1)S(1)}, u32[]{:S(2)}) copy-start(bf16[152,256]{1,0:T(8,128)(2,1)S(1)} %collective-permute-done.21.refs_8_) | copy-start | bytes 233476
  139.1 31.4 %all-to-all-start.2 = ((bf16[8,280,256]{2,1,0:T(8,128)(2,1)}), bf16[8,280,256]{2,1,0:T(8,128)(2,1)S(1)}, u32[]{:S(2)}, u32[]{:S(2)}) async-start(bf16[8,280,256]{2,1,0:T(8,128)(2,1)} %attention_back.2), calls=%async_computation.2 | async-start | bytes 2293760 | tf_op jit(solution)/shard_map/all_to_all | solution.py:378
  143.1 3.8 %collective-permute-start.26 = (f32[8,640]{1,0:T(8,128)S(1)}, f32[8,640]{1,0:T(8,128)S(1)}, u32[]{:S(2)}, u32[]{:S(2)}) collective-permute-start(f32[8,640]{1,0:T(8,128)S(1)} %add.89), channel_id=1, source_target_pairs={{0,2},{1,3},{2,0},{3,1},{4,6},{5,7},{6,4},{7,5},{8,10},{9,11},{10,... | collective-permute-start | bytes 61448 | tf_op jit(solution)/shard_map/ppermute | solution.py:604
  155.0 8.6 %collective-permute-start.27 = (bf16[304,256]{1,0:T(8,128)(2,1)}, bf16[304,256]{1,0:T(8,128)(2,1)S(1)}, u32[]{:S(2)}, u32[]{:S(2)}) collective-permute-start(bf16[304,256]{1,0:T(8,128)(2,1)} %get-tuple-element.138), channel_id=1, source_target_pairs={{0,4},{4,0},{8,12},{12,8},{16,20},{20,16},{24,28},{28,24},{1,5},{5... | collective-permute-start | bytes 466952 | tf_op jit(solution)/shard_map/ppermute | solution.py:404
  156.5 10.7 %collective-permute-start.28 = (bf16[304,256]{1,0:T(8,128)(2,1)}, bf16[304,256]{1,0:T(8,128)(2,1)S(1)}, u32[]{:S(2)}, u32[]{:S(2)}) collective-permute-start(bf16[304,256]{1,0:T(8,128)(2,1)} %get-tuple-element.139), channel_id=1, source_target_pairs={{0,8},{4,12},{8,0},{12,4},{16,24},{20,28},{24,16},{28,20},{1,9},{5... | collective-permute-start | bytes 466952 | tf_op jit(solution)/shard_map/ppermute | solution.py:404
  157.1 18.5 %collective-permute-start.29 = (bf16[304,256]{1,0:T(8,128)(2,1)}, bf16[304,256]{1,0:T(8,128)(2,1)S(1)}, u32[]{:S(2)}, u32[]{:S(2)}) collective-permute-start(bf16[304,256]{1,0:T(8,128)(2,1)} %get-tuple-element.140), channel_id=1, source_target_pairs={{0,12},{4,8},{8,4},{12,0},{16,28},{20,24},{24,20},{28,16},{1,13},{... | collective-permute-start | bytes 466952 | tf_op jit(solution)/shard_map/ppermute | solution.py:404
  158.5 26.4 %collective-permute-start.30 = (bf16[304,256]{1,0:T(8,128)(2,1)}, bf16[304,256]{1,0:T(8,128)(2,1)S(1)}, u32[]{:S(2)}, u32[]{:S(2)}) collective-permute-start(bf16[304,256]{1,0:T(8,128)(2,1)} %get-tuple-element.141), channel_id=1, source_target_pairs={{0,16},{4,20},{8,24},{12,28},{16,0},{20,4},{24,8},{28,12},{1,17},{... | collective-permute-start | bytes 466952 | tf_op jit(solution)/shard_map/ppermute | solution.py:404
  160.9 27.4 %collective-permute-start.31 = (bf16[304,256]{1,0:T(8,128)(2,1)}, bf16[304,256]{1,0:T(8,128)(2,1)S(1)}, u32[]{:S(2)}, u32[]{:S(2)}) collective-permute-start(bf16[304,256]{1,0:T(8,128)(2,1)} %get-tuple-element.142), channel_id=1, source_target_pairs={{0,20},{4,16},{8,28},{12,24},{16,4},{20,0},{24,12},{28,8},{1,21},{... | collective-permute-start | bytes 466952 | tf_op jit(solution)/shard_map/ppermute | solution.py:404
  163.6 33.6 %copy-start.16 = (bf16[304,256]{1,0:T(8,128)(2,1)}, bf16[304,256]{1,0:T(8,128)(2,1)S(1)}, u32[]{:S(2)}) copy-start(bf16[304,256]{1,0:T(8,128)(2,1)S(1)} %collective-permute-done.27.refs_1_) | copy-start | bytes 466948
  163.6 30.7 %collective-permute-start.32 = (bf16[304,256]{1,0:T(8,128)(2,1)}, bf16[304,256]{1,0:T(8,128)(2,1)S(1)}, u32[]{:S(2)}, u32[]{:S(2)}) collective-permute-start(bf16[304,256]{1,0:T(8,128)(2,1)} %get-tuple-element.143), channel_id=1, source_target_pairs={{0,24},{4,28},{8,16},{12,20},{16,8},{20,12},{24,0},{28,4},{1,25},{... | collective-permute-start | bytes 466952 | tf_op jit(solution)/shard_map/ppermute | solution.py:404
  167.2 30.0 %copy-start.17 = (bf16[304,256]{1,0:T(8,128)(2,1)}, bf16[304,256]{1,0:T(8,128)(2,1)S(1)}, u32[]{:S(2)}) copy-start(bf16[304,256]{1,0:T(8,128)(2,1)S(1)} %collective-permute-done.28.refs_2_) | copy-start | bytes 466948
  167.2 30.0 %collective-permute-start.33 = (bf16[304,256]{1,0:T(8,128)(2,1)}, bf16[304,256]{1,0:T(8,128)(2,1)S(1)}, u32[]{:S(2)}, u32[]{:S(2)}) collective-permute-start(bf16[304,256]{1,0:T(8,128)(2,1)} %get-tuple-element.144), channel_id=1, source_target_pairs={{0,28},{4,24},{8,20},{12,16},{16,12},{20,8},{24,4},{28,0},{1,29},{... | collective-permute-start | bytes 466952 | tf_op jit(solution)/shard_map/ppermute | solution.py:404
  175.5 21.7 %copy-start.18 = (bf16[304,256]{1,0:T(8,128)(2,1)}, bf16[304,256]{1,0:T(8,128)(2,1)S(1)}, u32[]{:S(2)}) copy-start(bf16[304,256]{1,0:T(8,128)(2,1)S(1)} %collective-permute-done.29.refs_3_) | copy-start | bytes 466948
  185.0 12.3 %copy-start.19 = (bf16[304,256]{1,0:T(8,128)(2,1)}, bf16[304,256]{1,0:T(8,128)(2,1)S(1)}, u32[]{:S(2)}) copy-start(bf16[304,256]{1,0:T(8,128)(2,1)S(1)} %collective-permute-done.30.refs_4_) | copy-start | bytes 466948
  188.3 9.0 %copy-start.20 = (bf16[304,256]{1,0:T(8,128)(2,1)}, bf16[304,256]{1,0:T(8,128)(2,1)S(1)}, u32[]{:S(2)}) copy-start(bf16[304,256]{1,0:T(8,128)(2,1)S(1)} %collective-permute-done.31.refs_5_) | copy-start | bytes 466948
  (12 other events, 24.3 us)

commit v4 on v3

--- a/solution.py
+++ b/solution.py
@@ -124,19 +124,22 @@
 
 
 def pool_kernel(blocks, heads, chunk, *refs):
-    v_refs, (r_ref, meta_ref, w_hbm, part_ref, pooled_ref, w_ref, sems) = (
-        refs[:blocks],
-        refs[blocks:],
-    )
+    v_hbm, refs = refs[:blocks], refs[blocks:]
+    r_hbm, meta_ref, w_hbm, part_ref, pooled_ref, v_ref, r_ref, near_sems, w_ref, sems = refs
+    fetches = [pltpu.make_async_copy(r_hbm, r_ref, near_sems.at[blocks])]
+    for s in range(blocks):
+        at = slice(s * LANES, (s + 1) * LANES)
+        fetches.append(pltpu.make_async_copy(v_hbm[s], v_ref.at[at], near_sems.at[s]))
+    for fetch in fetches:
+        fetch.start()
     copies = start_weights(w_hbm, w_ref, sems, blocks, chunk)
     count = jnp.maximum(take_lanes(meta_ref[...], 0, 1), 1.0)
+    for fetch in fetches:
+        fetch.wait()
     columns = []
     for h in range(heads):
         r = jnp.concatenate([r_ref[s, h] for s in range(blocks)], axis=1)
-        v = jnp.concatenate(
-            [v_refs[s][:, h * HS : (h + 1) * HS] for s in range(blocks)], axis=0
-        )
-        columns.append(dot_nn(r, v))
+        columns.append(dot_nn(r, v_ref[:, h * HS : (h + 1) * HS]))
     pooled = jnp.concatenate(columns, axis=1) if heads > 1 else columns[0]
     pooled = pooled / count
     pooled_ref[...] = pooled
@@ -478,14 +481,19 @@
     with jax.named_scope("pool_project"):
         part, pooled = pl.pallas_call(
             functools.partial(pool_kernel, n, heads, chunk),
-            in_specs=[in_vmem] * (n + 2) + [anywhere],
-            scratch_shapes=weights_scratch,
+            in_specs=[anywhere] * (n + 1) + [in_vmem, anywhere],
+            scratch_shapes=[
+                pltpu.VMEM((tokens, lw), BF),
+                pltpu.VMEM((n, heads, FR, LANES), BF),
+                pltpu.SemaphoreType.DMA((n + 1,)),
+            ]
+            + weights_scratch,
             out_shape=[
                 jax.ShapeDtypeStruct((n, FR, chunk + LANES), BF),
                 jax.ShapeDtypeStruct((FR, lw), F32),
             ],
             compiler_params=params(tokens, 0),
-        )(*v, r, meta, hbm(w))
+        )(*v, hbm(r), meta, hbm(w))
 
     got = exchange(part)
 
@@ -620,7 +628,7 @@
             functools.partial(settle_kernel, n, lw, first * HS, n - half, len(far_blocks)),
             out_shape=[whole, frame_rows] + ([pltpu.HBM((tok, width), BF)] * 3 if first else []),
             compiler_params=params(tokens, 0),
-        )(*map(hbm, mixed_near + far_blocks + early))
+        )(*mixed_near, *far_blocks, *map(hbm, early))
     late[0] = after(late[0], latents)
     with jax.named_scope("finish"):
         out_query, out_key, out_value, grad_heads = pl.pallas_call(
@@ -635,7 +643,7 @@
                 pltpu.SemaphoreType.DMA((3 * n,)),
             ],
             compiler_params=params(tokens, 0),
-        )(*map(hbm, late), frame_rows, *map(hbm, begun))
+        )(*late, frame_rows, *map(hbm, begun))
     if chunk != columns:
         grad_heads = grad_heads.reshape(NDH, n, chunk)[:, :, :columns].reshape(NDH, dh)
 

time: 202 us -> 200 us (0.990)
  local copies, waits for them, and re-layouts: 6.67 us -> 3.27 us
  waiting for transfers between devices: 61.4 us -> 63.6 us
    unnamed x78 -> x42, local copies, waits for them, and re-layouts: 3.49 us -> 0.09 us
    ppermute x32, waiting for transfers between devices: 58.1 us -> 60.3 us  [send(): return lax.ppermute(array, 'gen', [(i, i ^ s) for i in range(n)])]
where the time goes in v4:
time: 200 us
  starting transfers between devices  76.5 us (38%)
  waiting for transfers between devices  63.6 us (32%)
  Pallas kernels  52.7 us (26%)
  local copies, waits for them, and re-layouts  3.27 us (2%)
    ppermute x32, waiting for transfers between devices, send(): return lax.ppermute(array, 'gen', [(i, i ^ s) for i in range(n)])  60.3 us
    ppermute x32, starting transfers between devices, send(): return lax.ppermute(array, 'gen', [(i, i ^ s) for i in range(n)])  56.7 us
    all_to_all x3, starting transfers between devices, exchange(): return lax.all_to_all(array, 'gen', split_axis=0, concat_axis=0, tiled=True)  18.3 us
    pallas_call x2, Pallas kernels, back(): pl.pallas_call(functools.partial(back_kernel, n, apart), grid=(last - fir...  16.3 us
    pallas_call x1, Pallas kernels, on_device(): pl.pallas_call(functools.partial(stats_kernel, n), grid=(heads,), in_spec...  11.6 us
    pallas_call x2, Pallas kernels, output(): pl.pallas_call(functools.partial(output_kernel, n), grid=(last - first,),...  9.89 us
    pallas_call x1, Pallas kernels, on_device(): pl.pallas_call(functools.partial(pool_kernel, n, heads, chunk), in_specs=...  5.14 us
  transfers between devices with their start and end apart: 37, of which 16 were waited for; matrix products, arithmetic and copies ran while one was open for 2% of the time, Pallas kernels for 23%

profile of v4, /device:TPU:8, one launch (start us, length us, event | category | flops | bytes accessed | tf_op | source)
XLA Modules:
  0.0 199.8 jit_solution(15506127886110760679)
XLA Ops:
  0.7 1.8 constant_dynamic-slice_fusion.1
  2.6 2.6 %collective-permute-start.9 = (bf16[2,128,512]{2,1,0:T(8,128)(2,1)S(1)}, bf16[2,128,512]{2,1,0:T(8,128)(2,1)}, u32[]{:S(2)}, u32[]{:S(2)}) collective-permute-start(bf16[2,128,512]{2,1,0:T(8,128)(2,1)S(1)} %pad_maximum_fusion.4), channel_id=1, source_target_pairs={{0,28},{4,24},{8,20},{12,16},{16,12},{20,8},{24,4},{28,0},{1,29},{... | collective-permute-start | bytes 786440 | tf_op jit(solution)/shard_map/ppermute | solution.py:407
  5.2 0.5 collective-permute-start.6
  5.8 4.4 %collective-permute-start.5 = (bf16[2,128,512]{2,1,0:T(8,128)(2,1)S(1)}, bf16[2,128,512]{2,1,0:T(8,128)(2,1)}, u32[]{:S(2)}, u32[]{:S(2)}) collective-permute-start(bf16[2,128,512]{2,1,0:T(8,128)(2,1)S(1)} %pad_maximum_fusion.2), channel_id=1, source_target_pairs={{0,20},{4,16},{8,28},{12,24},{16,4},{20,0},{24,12},{28,8},{1,21},{... | collective-permute-start | bytes 786440 | tf_op jit(solution)/shard_map/ppermute | solution.py:407
  10.2 1.6 collective-permute-start
  11.9 0.6 gather_fusion
  12.6 5.1 %collective-permute-done.refs_1_ = bf16[2,128,512]{2,1,0:T(8,128)(2,1)} collective-permute-done((bf16[2,128,512]{2,1,0:T(8,128)(2,1)S(1)}, bf16[2,128,512]{2,1,0:T(8,128)(2,1)}, u32[]{:S(2)}, u32[]{:S(2)}) %collective-permute-start) | collective-permute-done | bytes 262176 | tf_op jit(solution)/shard_map/ppermute | solution.py:407
  17.7 2.1 %collective-permute-start.12 = (bf16[2,128,512]{2,1,0:T(8,128)(2,1)S(1)}, bf16[2,128,512]{2,1,0:T(8,128)(2,1)S(1)}, u32[]{:S(2)}, u32[]{:S(2)}) collective-permute-start(bf16[2,128,512]{2,1,0:T(8,128)(2,1)S(1)} %pad_maximum_fusion.6), channel_id=1, source_target_pairs={{0,8},{4,12},{8,0},{12,4},{16,24},{20,28},{24,16},{28,20},{1,9},{5... | collective-permute-start | bytes 786440 | tf_op jit(solution)/shard_map/ppermute | solution.py:407
  19.8 0.8 dynamic-slice_bitcast_fusion
  20.5 1.4 collective-permute-start.1
  22.1 8.5 %collective-permute-done.12.refs_2_ = bf16[2,128,512]{2,1,0:T(8,128)(2,1)S(1)} collective-permute-done((bf16[2,128,512]{2,1,0:T(8,128)(2,1)S(1)}, bf16[2,128,512]{2,1,0:T(8,128)(2,1)S(1)}, u32[]{:S(2)}, u32[]{:S(2)}) %collective-permute-start.12) | collective-permute-done | bytes 262176 | tf_op jit(solution)/shard_map/ppermute | solution.py:407
  30.6 0.7 collective-permute-done.1.refs_1_
  31.3 0.2 collective-permute-start.13
  32.1 2.9 %collective-permute-start.2 = (bf16[128,512]{1,0:T(8,128)(2,1)S(1)}, bf16[128,512]{1,0:T(8,128)(2,1)S(1)}, u32[]{:S(2)}, u32[]{:S(2)}) collective-permute-start(bf16[128,512]{1,0:T(8,128)(2,1)S(1)} %get-tuple-element.81), channel_id=1, source_target_pairs={{0,8},{4,12},{8,0},{12,4},{16,24},{20,28},{24,16},{28,20},{1,9},{5... | collective-permute-start | bytes 393224 | tf_op jit(solution)/shard_map/ppermute | solution.py:407
  35.0 5.7 %collective-permute-done.6.refs_6_ = bf16[2,128,512]{2,1,0:T(8,128)(2,1)} collective-permute-done((bf16[2,128,512]{2,1,0:T(8,128)(2,1)S(1)}, bf16[2,128,512]{2,1,0:T(8,128)(2,1)}, u32[]{:S(2)}, u32[]{:S(2)}) %collective-permute-start.6) | collective-permute-done | bytes 262176 | tf_op jit(solution)/shard_map/ppermute | solution.py:407
  40.7 4.9 %collective-permute-done.5.refs_5_ = bf16[2,128,512]{2,1,0:T(8,128)(2,1)} collective-permute-done((bf16[2,128,512]{2,1,0:T(8,128)(2,1)S(1)}, bf16[2,128,512]{2,1,0:T(8,128)(2,1)}, u32[]{:S(2)}, u32[]{:S(2)}) %collective-permute-start.5) | collective-permute-done | bytes 262176 | tf_op jit(solution)/shard_map/ppermute | solution.py:407
  45.7 4.6 %collective-permute-done.4.refs_4_ = bf16[2,128,512]{2,1,0:T(8,128)(2,1)S(1)} collective-permute-done((bf16[2,128,512]{2,1,0:T(8,128)(2,1)S(1)}, bf16[2,128,512]{2,1,0:T(8,128)(2,1)S(1)}, u32[]{:S(2)}, u32[]{:S(2)}) %collective-permute-start.4) | collective-permute-done | bytes 262176 | tf_op jit(solution)/shard_map/ppermute | solution.py:407
  50.3 0.3 collective-permute-start.11
  50.6 1.6 collective-permute-start.10
  52.1 6.3 %collective-permute-start.8 = (bf16[128,512]{1,0:T(8,128)(2,1)S(1)}, bf16[128,512]{1,0:T(8,128)(2,1)S(1)}, u32[]{:S(2)}, u32[]{:S(2)}) collective-permute-start(bf16[128,512]{1,0:T(8,128)(2,1)S(1)} %get-tuple-element.84), channel_id=1, source_target_pairs={{0,20},{4,16},{8,28},{12,24},{16,4},{20,0},{24,12},{28,8},{1,21},{... | collective-permute-start | bytes 393224 | tf_op jit(solution)/shard_map/ppermute | solution.py:407
  58.4 1.8 collective-permute-start.3
  60.2 0.7 pad_maximum_fusion.5.refs_0_
  60.9 11.6 %softmax_stats.1 = (bf16[4,1024,128]{2,1,0:T(8,128)(2,1)}, bf16[8,4,24,128]{3,2,1,0:T(8,128)(2,1)}, bf16[4,1024,128]{2,1,0:T(8,128)(2,1)}, bf16[4,1024,128]{2,1,0:T(8,128)(2,1)}) custom-call(bf16[2,128,512]{2,1,0:T(8,128)(2,1)} %pad_maximum_fusion.5.refs_0_, bf16[2,128,512]{2,1,0:T(8,128)(2,1)} %collective-permute-done.refs_1_, ...), custom_call_target="tpu_custom_call" | custom-call | flops 1073741824 | bytes 4194304 | tf_op jit(solution)/shard_map/softmax_stats/pallas_call | solution.py:463
  72.7 5.1 %pool_project.1 = (bf16[8,24,768]{2,1,0:T(8,128)(2,1)}, f32[24,512]{1,0:T(8,128)S(1)}) custom-call(bf16[128,512]{1,0:T(8,128)(2,1)S(1)} %get-tuple-element.175.refs_0_, bf16[128,512]{1,0:T(8,128)(2,1)S(1)} %collective-permute-done.1.refs_1_, bf16[128,512]{1,0:T(8,128)(2,1)S(1)} %collective-permute-done.2.refs_2_, ...), custom_call_target="tpu_custom_call" | custom-call | tf_op jit(solution)/shard_map/pool_project/pallas_call | solution.py:482
  77.9 7.0 %all-to-all-start = ((bf16[8,24,768]{2,1,0:T(8,128)(2,1)}), bf16[8,24,768]{2,1,0:T(8,128)(2,1)S(1)}, u32[]{:S(2)}, u32[]{:S(2)}) async-start(bf16[8,24,768]{2,1,0:T(8,128)(2,1)} %get-tuple-element.93), calls=%async_computation | async-start | bytes 589824 | tf_op jit(solution)/shard_map/all_to_all | solution.py:381
  84.9 4.9 %attention_output.2 = (bf16[152,512]{1,0:T(8,128)(2,1)}, bf16[152,512]{1,0:T(8,128)(2,1)}, bf16[152,512]{1,0:T(8,128)(2,1)}, bf16[152,512]{1,0:T(8,128)(2,1)}, b...) custom-call(bf16[128,512]{1,0:T(8,128)(2,1)} %copy-done.1, ...), custom_call_target="tpu_custom_call" | custom-call | flops 1073741824 | bytes 2097152 | tf_op jit(solution)/shard_map/attention_output/pallas_call | solution.py:511
  89.9 2.4 %collective-permute-start.17 = (bf16[152,256]{1,0:T(8,128)(2,1)}, bf16[152,256]{1,0:T(8,128)(2,1)S(1)}, u32[]{:S(2)}, u32[]{:S(2)}) collective-permute-start(bf16[152,256]{1,0:T(8,128)(2,1)} %get-tuple-element.108), channel_id=1, source_target_pairs={{0,16},{4,20},{8,24},{12,28},{16,0},{20,4},{24,8},{28,12},{1,17},{... | collective-permute-start | bytes 233480 | tf_op jit(solution)/shard_map/ppermute | solution.py:407
  92.3 0.2 multiply_reduce_fusion.rows_ref
  92.5 0.9 discriminator.1
  93.5 2.0 collective-permute-done.17.refs_4_
  95.5 6.8 %all-to-all-start.1 = ((bf16[8,24,768]{2,1,0:T(8,128)(2,1)}), bf16[8,24,768]{2,1,0:T(8,128)(2,1)S(1)}, u32[]{:S(2)}, u32[]{:S(2)}) async-start(bf16[8,24,768]{2,1,0:T(8,128)(2,1)} %get-tuple-element.113), calls=%async_computation.1 | async-start | bytes 589824 | tf_op jit(solution)/shard_map/all_to_all | solution.py:381
  102.3 3.3 %collective-permute-start.18 = (bf16[152,256]{1,0:T(8,128)(2,1)}, bf16[152,256]{1,0:T(8,128)(2,1)S(1)}, u32[]{:S(2)}, u32[]{:S(2)}) collective-permute-start(bf16[152,256]{1,0:T(8,128)(2,1)} %get-tuple-element.109), channel_id=1, source_target_pairs={{0,20},{4,16},{8,28},{12,24},{16,4},{20,0},{24,12},{28,8},{1,21},{... | collective-permute-start | bytes 233480 | tf_op jit(solution)/shard_map/ppermute | solution.py:407
  105.6 2.0 %collective-permute-start.20 = (bf16[152,256]{1,0:T(8,128)(2,1)}, bf16[152,256]{1,0:T(8,128)(2,1)S(1)}, u32[]{:S(2)}, u32[]{:S(2)}) collective-permute-start(bf16[152,256]{1,0:T(8,128)(2,1)} %get-tuple-element.111), channel_id=1, source_target_pairs={{0,28},{4,24},{8,20},{12,16},{16,12},{20,8},{24,4},{28,0},{1,29},{... | collective-permute-start | bytes 233480 | tf_op jit(solution)/shard_map/ppermute | solution.py:407
  107.6 5.0 %attention_output.3 = (bf16[152,512]{1,0:T(8,128)(2,1)}, bf16[152,512]{1,0:T(8,128)(2,1)}, bf16[152,512]{1,0:T(8,128)(2,1)}, bf16[152,512]{1,0:T(8,128)(2,1)}, b...) custom-call(bf16[128,512]{1,0:T(8,128)(2,1)} %copy-done.1, ...), custom_call_target="tpu_custom_call", output_to_operand_aliasing={{0}: (12, {}), {1}: (13, {}), {2}: (14, {}), {3}: (15, {}),... | custom-call | flops 1073741824 | bytes 2097152 | tf_op jit(solution)/shard_map/attention_output/pallas_call | solution.py:511
  112.5 1.5 collective-permute-start.14
  114.1 2.4 %collective-permute-start.15 = (bf16[152,512]{1,0:T(8,128)(2,1)}, bf16[152,512]{1,0:T(8,128)(2,1)S(1)}, u32[]{:S(2)}, u32[]{:S(2)}) collective-permute-start(bf16[152,512]{1,0:T(8,128)(2,1)} %get-tuple-element.106), channel_id=1, source_target_pairs={{0,8},{4,12},{8,0},{12,4},{16,24},{20,28},{24,16},{28,20},{1,9},{5... | collective-permute-start | bytes 466952 | tf_op jit(solution)/shard_map/ppermute | solution.py:407
  116.4 1.5 collective-permute-start.16
  117.9 0.3 collective-permute-done.20.refs_7_
  118.2 3.1 %pooled_gradient.1 = (bf16[128,512]{1,0:T(8,128)(2,1)S(1)}, f32[8,640]{1,0:T(8,128)S(1)}) custom-call(bf16[8,24,768]{2,1,0:T(8,128)(2,1)S(1)} %all-to-all-done.1.got_ref, bf16[512,5120]{1,0:T(8,128)(2,1)} %w_hbm.1, f32[24,512]{1,0:T(8,128)S(1)} %get-tuple-element.117.pooled_ref, f32[24,128]{1,0:T(8,128)S(1)} %broadcast_select_fusion.refs_9_.meta_ref, ...), custom_call_target="tpu_custom_call" | custom-call | tf_op jit(solution)/shard_map/pooled_gradient/pallas_call | solution.py:555
  121.4 0.4 collective-permute-start.21
  121.8 0.2 fusion.m_ref
  122.0 1.0 collective-permute-done.25
  122.9 2.4 %collective-permute-start.24 = (bf16[152,256]{1,0:T(8,128)(2,1)S(1)}, bf16[152,256]{1,0:T(8,128)(2,1)S(1)}, u32[]{:S(2)}, u32[]{:S(2)}) collective-permute-start(bf16[152,256]{1,0:T(8,128)(2,1)S(1)} %copy-done.18), channel_id=1, source_target_pairs={{0,28},{4,24},{8,20},{12,16},{16,12},{20,8},{24,4},{28,0},{1,29},{... | collective-permute-start | bytes 233480 | tf_op jit(solution)/shard_map/ppermute | solution.py:407
  125.3 0.6 collective-permute-start.23
  125.9 4.4 %collective-permute-start.22 = (bf16[152,256]{1,0:T(8,128)(2,1)S(1)}, bf16[152,256]{1,0:T(8,128)(2,1)S(1)}, u32[]{:S(2)}, u32[]{:S(2)}) collective-permute-start(bf16[152,256]{1,0:T(8,128)(2,1)S(1)} %copy-done.16), channel_id=1, source_target_pairs={{0,20},{4,16},{8,28},{12,24},{16,4},{20,0},{24,12},{28,8},{1,21},{... | collective-permute-start | bytes 233480 | tf_op jit(solution)/shard_map/ppermute | solution.py:407
  130.4 8.1 %attention_back.2 = bf16[8,280,256]{2,1,0:T(8,128)(2,1)} custom-call(bf16[4,1024,128]{2,1,0:T(8,128)(2,1)} %get-tuple-element.89.refs_8_.q_ref, bf16[4,1024,128]{2,1,0:T(8,128)(2,1)} %get-tuple-element.90.refs_9_.k_ref, bf16[4,1024,128]{2,1,0:T(8,128)(2,1)} %get-tuple-element.130.v_ref, bf16[4,1024,128]{2,1,0:T(8,128)(2,1)} %get-tuple-element.115.o_ref, ...), custom_call_target="tpu_custom_call" | custom-call | flops 2147483648 | bytes 4194304 | tf_op jit(solution)/shard_map/attention_back/pallas_call | solution.py:576
  138.5 4.5 %all-to-all-start.2 = ((bf16[8,280,256]{2,1,0:T(8,128)(2,1)}), bf16[8,280,256]{2,1,0:T(8,128)(2,1)}, u32[]{:S(2)}, u32[]{:S(2)}) async-start(bf16[8,280,256]{2,1,0:T(8,128)(2,1)} %attention_back.2), calls=%async_computation.2 | async-start | bytes 2293760 | tf_op jit(solution)/shard_map/all_to_all | solution.py:381
  143.0 1.5 collective-permute-start.26
  144.5 2.3 %collective-permute-done.26 = f32[8,640]{1,0:T(8,128)S(1)} collective-permute-done((f32[8,640]{1,0:T(8,128)S(1)}, f32[8,640]{1,0:T(8,128)S(1)}, u32[]{:S(2)}, u32[]{:S(2)}) %collective-permute-start.26) | collective-permute-done | bytes 20512 | tf_op jit(solution)/shard_map/ppermute | solution.py:612
  146.8 8.2 %attention_back.3 = (bf16[304,256]{1,0:T(8,128)(2,1)}, bf16[304,256]{1,0:T(8,128)(2,1)}, bf16[304,256]{1,0:T(8,128)(2,1)}, bf16[304,256]{1,0:T(8,128)(2,1)}, bf1...) custom-call(bf16[4,1024,128]{2,1,0:T(8,128)(2,1)} %get-tuple-element.89.r, ...), custom_call_target="tpu_custom_call" | custom-call | flops 2147483648 | bytes 4194304 | tf_op jit(solution)/shard_map/attention_back/pallas_call | solution.py:576
  155.0 1.5 collective-permute-start.27
  156.5 0.5 collective-permute-start.28
  157.1 1.5 collective-permute-start.29
  158.5 2.4 %collective-permute-start.30 = (bf16[304,256]{1,0:T(8,128)(2,1)}, bf16[304,256]{1,0:T(8,128)(2,1)S(1)}, u32[]{:S(2)}, u32[]{:S(2)}) collective-permute-start(bf16[304,256]{1,0:T(8,128)(2,1)} %get-tuple-element.141), channel_id=1, source_target_pairs={{0,16},{4,20},{8,24},{12,28},{16,0},{20,4},{24,8},{28,12},{1,17},{... | collective-permute-start | bytes 466952 | tf_op jit(solution)/shard_map/ppermute | solution.py:407
  160.9 1.4 collective-permute-start.31
  162.4 1.7 collective-permute-done.27.refs_1_
  164.1 3.4 %collective-permute-done.28.refs_2_ = bf16[304,256]{1,0:T(8,128)(2,1)S(1)} collective-permute-done((bf16[304,256]{1,0:T(8,128)(2,1)}, bf16[304,256]{1,0:T(8,128)(2,1)S(1)}, u32[]{:S(2)}, u32[]{:S(2)}) %collective-permute-start.28) | collective-permute-done | bytes 155680 | tf_op jit(solution)/shard_map/ppermute | solution.py:407
  167.5 3.0 %collective-permute-start.33 = (bf16[304,256]{1,0:T(8,128)(2,1)}, bf16[304,256]{1,0:T(8,128)(2,1)S(1)}, u32[]{:S(2)}, u32[]{:S(2)}) collective-permute-start(bf16[304,256]{1,0:T(8,128)(2,1)} %get-tuple-element.144), channel_id=1, source_target_pairs={{0,28},{4,24},{8,20},{12,16},{16,12},{20,8},{24,4},{28,0},{1,29},{... | collective-permute-start | bytes 466952 | tf_op jit(solution)/shard_map/ppermute | solution.py:407
  170.5 3.6 %settle.1 = (bf16[128,4096]{1,0:T(8,128)(2,1)}, bf16[8,24,256]{2,1,0:T(8,128)(2,1)S(1)}, bf16[128,4096]{1,0:T(8,128)(2,1)}, bf16[128,4096]{1,0:T(8,128)(2,1)}, bf16[128,4096]{1,0:T(8,128)(2,1)}) custom-call(bf16[152,512]{1,0:T(8,128)(2,1)S(1)} %copy-done.9, bf16[152,512]{1,0:T(8,128)(2,1)S(1)} %collective-permute-done.14.refs_1_, ...), custom_call_target="tpu_custom_call" | custom-call | tf_op jit(solution)/shard_map/settle/pallas_call | solution.py:627
  174.1 11.5 %collective-permute-done.30.refs_4_ = bf16[304,256]{1,0:T(8,128)(2,1)S(1)} collective-permute-done((bf16[304,256]{1,0:T(8,128)(2,1)}, bf16[304,256]{1,0:T(8,128)(2,1)S(1)}, u32[]{:S(2)}, u32[]{:S(2)}) %collective-permute-start.30) | collective-permute-done | bytes 155680 | tf_op jit(solution)/shard_map/ppermute | solution.py:407
  185.5 3.3 %collective-permute-done.31.refs_5_ = bf16[304,256]{1,0:T(8,128)(2,1)S(1)} collective-permute-done((bf16[304,256]{1,0:T(8,128)(2,1)}, bf16[304,256]{1,0:T(8,128)(2,1)S(1)}, u32[]{:S(2)}, u32[]{:S(2)}) %collective-permute-start.31) | collective-permute-done | bytes 155680 | tf_op jit(solution)/shard_map/ppermute | solution.py:407
  188.9 5.3 %collective-permute-done.32.refs_6_ = bf16[304,256]{1,0:T(8,128)(2,1)S(1)} collective-permute-done((bf16[304,256]{1,0:T(8,128)(2,1)}, bf16[304,256]{1,0:T(8,128)(2,1)S(1)}, u32[]{:S(2)}, u32[]{:S(2)}) %collective-permute-start.32) | collective-permute-done | bytes 155680 | tf_op jit(solution)/shard_map/ppermute | solution.py:407
  194.2 3.2 %collective-permute-done.33.refs_7_ = bf16[304,256]{1,0:T(8,128)(2,1)S(1)} collective-permute-done((bf16[304,256]{1,0:T(8,128)(2,1)}, bf16[304,256]{1,0:T(8,128)(2,1)S(1)}, u32[]{:S(2)}, u32[]{:S(2)}) %collective-permute-start.33) | collective-permute-done | bytes 155680 | tf_op jit(solution)/shard_map/ppermute | solution.py:407
  197.5 2.2 %finish.1 = (bf16[128,4096]{1,0:T(8,128)(2,1)}, bf16[128,4096]{1,0:T(8,128)(2,1)}, bf16[128,4096]{1,0:T(8,128)(2,1)}, f32[8,5120]{1,0:T(8,128)}) custom-call(bf16[304,256]{1,0:T(8,128)(2,1)S(1)} %copy-done.10, bf16[304,256]{1,0:T(8,128)(2,1)S(1)} %collective-permute-done.27.refs_1_, ...), custom_call_target="tpu_custom_call", output_to_operand_aliasing={{0}: (9, {}), {1}: (10, {}), {2}: (11, {})} | custom-call | tf_op jit(solution)/shard_map/finish/pallas_call | solution.py:634
  (93 shorter events, 0.8 us)
Async XLA Ops:
  0.6 84.2 %copy-start = (f32[8,5120]{1,0:T(8,128)S(1)}, f32[8,5120]{1,0:T(8,128)}, u32[]{:S(2)}) copy-start(f32[8,5120]{1,0:T(8,128)} %param.12) | copy-start | bytes 491524
  2.6 9.3 %copy-start.12 = (s32[1,1024]{1,0:T(1,128)S(1)}, s32[1,1024]{1,0:T(1,128)}, u32[]{:S(2)}) copy-start(s32[1,1024]{1,0:T(1,128)} %param.13) | copy-start | bytes 12292
  2.6 29.5 %collective-permute-start.9 = (bf16[2,128,512]{2,1,0:T(8,128)(2,1)S(1)}, bf16[2,128,512]{2,1,0:T(8,128)(2,1)}, u32[]{:S(2)}, u32[]{:S(2)}) collective-permute-start(bf16[2,128,512]{2,1,0:T(8,128)(2,1)S(1)} %pad_maximum_fusion.4), channel_id=1, source_target_pairs={{0,28},{4,24},{8,20},{12,16},{16,12},{20,8},{24,4},{28,0},{1,29},{... | collective-permute-start | bytes 786440 | tf_op jit(solution)/shard_map/ppermute | solution.py:407
  5.2 14.6 %copy-start.11 = (bf16[1,128,4096]{2,1,0:T(8,128)(2,1)S(1)}, bf16[1,128,4096]{2,1,0:T(8,128)(2,1)}, u32[]{:S(2)}) copy-start(bf16[1,128,4096]{2,1,0:T(8,128)(2,1)} %param.10) | copy-start | bytes 3145732
  5.2 35.5 %collective-permute-start.6 = (bf16[2,128,512]{2,1,0:T(8,128)(2,1)S(1)}, bf16[2,128,512]{2,1,0:T(8,128)(2,1)}, u32[]{:S(2)}, u32[]{:S(2)}) collective-permute-start(bf16[2,128,512]{2,1,0:T(8,128)(2,1)S(1)} %pad_maximum_fusion.3), channel_id=1, source_target_pairs={{0,24},{4,28},{8,16},{12,20},{16,8},{20,12},{24,0},{28,4},{1,25},{... | collective-permute-start | bytes 786440 | tf_op jit(solution)/shard_map/ppermute | solution.py:407
  5.8 39.9 %collective-permute-start.5 = (bf16[2,128,512]{2,1,0:T(8,128)(2,1)S(1)}, bf16[2,128,512]{2,1,0:T(8,128)(2,1)}, u32[]{:S(2)}, u32[]{:S(2)}) collective-permute-start(bf16[2,128,512]{2,1,0:T(8,128)(2,1)S(1)} %pad_maximum_fusion.2), channel_id=1, source_target_pairs={{0,20},{4,16},{8,28},{12,24},{16,4},{20,0},{24,12},{28,8},{1,21},{... | collective-permute-start | bytes 786440 | tf_op jit(solution)/shard_map/ppermute | solution.py:407
  10.2 7.5 %collective-permute-start = (bf16[2,128,512]{2,1,0:T(8,128)(2,1)S(1)}, bf16[2,128,512]{2,1,0:T(8,128)(2,1)}, u32[]{:S(2)}, u32[]{:S(2)}) collective-permute-start(bf16[2,128,512]{2,1,0:T(8,128)(2,1)S(1)} %pad_maximum_fusion), channel_id=1, source_target_pairs={{0,4},{4,0},{8,12},{12,8},{16,20},{20,16},{24,28},{28,24},{1,5},{5... | collective-permute-start | bytes 786440 | tf_op jit(solution)/shard_map/ppermute | solution.py:407
  12.6 48.3 %copy-start.20 = (s32[1,21]{1,0:T(1,128)S(1)}, s32[1,21]{1,0:T(1,128)}, u32[]{:S(2)}) copy-start(s32[1,21]{1,0:T(1,128)} %param.14) | copy-start | bytes 256
  17.7 12.9 %collective-permute-start.12 = (bf16[2,128,512]{2,1,0:T(8,128)(2,1)S(1)}, bf16[2,128,512]{2,1,0:T(8,128)(2,1)S(1)}, u32[]{:S(2)}, u32[]{:S(2)}) collective-permute-start(bf16[2,128,512]{2,1,0:T(8,128)(2,1)S(1)} %pad_maximum_fusion.6), channel_id=1, source_target_pairs={{0,8},{4,12},{8,0},{12,4},{16,24},{20,28},{24,16},{28,20},{1,9},{5... | collective-permute-start | bytes 786440 | tf_op jit(solution)/shard_map/ppermute | solution.py:407
  20.5 52.1 %copy-start.1 = (bf16[128,512]{1,0:T(8,128)(2,1)}, bf16[128,512]{1,0:T(8,128)(2,1)S(1)}, u32[]{:S(2)}) copy-start(bf16[128,512]{1,0:T(8,128)(2,1)S(1)} %get-tuple-element.175.refs_0_) | copy-start | bytes 393220
  20.5 10.7 %collective-permute-start.1 = (bf16[128,512]{1,0:T(8,128)(2,1)S(1)}, bf16[128,512]{1,0:T(8,128)(2,1)S(1)}, u32[]{:S(2)}, u32[]{:S(2)}) collective-permute-start(bf16[128,512]{1,0:T(8,128)(2,1)S(1)} %get-tuple-element.80), channel_id=1, source_target_pairs={{0,4},{4,0},{8,12},{12,8},{16,20},{20,16},{24,28},{28,24},{1,5},{5... | collective-permute-start | bytes 393224 | tf_op jit(solution)/shard_map/ppermute | solution.py:407
  30.6 29.6 %copy-start.13 = (bf16[2,128,512]{2,1,0:T(8,128)(2,1)}, bf16[2,128,512]{2,1,0:T(8,128)(2,1)S(1)}, u32[]{:S(2)}) copy-start(bf16[2,128,512]{2,1,0:T(8,128)(2,1)S(1)} %collective-permute-done.12.refs_2_) | copy-start | bytes 786436
  30.6 19.7 %collective-permute-start.4 = (bf16[2,128,512]{2,1,0:T(8,128)(2,1)S(1)}, bf16[2,128,512]{2,1,0:T(8,128)(2,1)S(1)}, u32[]{:S(2)}, u32[]{:S(2)}) collective-permute-start(bf16[2,128,512]{2,1,0:T(8,128)(2,1)S(1)} %pad_maximum_fusion.1), channel_id=1, source_target_pairs={{0,16},{4,20},{8,24},{12,28},{16,0},{20,4},{24,8},{28,12},{1,17},{... | collective-permute-start | bytes 786440 | tf_op jit(solution)/shard_map/ppermute | solution.py:407
  31.3 41.4 %copy-start.2 = (bf16[128,512]{1,0:T(8,128)(2,1)}, bf16[128,512]{1,0:T(8,128)(2,1)S(1)}, u32[]{:S(2)}) copy-start(bf16[128,512]{1,0:T(8,128)(2,1)S(1)} %collective-permute-done.1.refs_1_) | copy-start | bytes 393220
  31.3 27.1 %collective-permute-start.13 = (bf16[2,128,512]{2,1,0:T(8,128)(2,1)S(1)}, bf16[2,128,512]{2,1,0:T(8,128)(2,1)S(1)}, u32[]{:S(2)}, u32[]{:S(2)}) collective-permute-start(bf16[2,128,512]{2,1,0:T(8,128)(2,1)S(1)} %pad_maximum_fusion.7), channel_id=1, source_target_pairs={{0,12},{4,8},{8,4},{12,0},{16,28},{20,24},{24,20},{28,16},{1,13},{... | collective-permute-start | bytes 786440 | tf_op jit(solution)/shard_map/ppermute | solution.py:407
  32.1 26.3 %collective-permute-start.2 = (bf16[128,512]{1,0:T(8,128)(2,1)S(1)}, bf16[128,512]{1,0:T(8,128)(2,1)S(1)}, u32[]{:S(2)}, u32[]{:S(2)}) collective-permute-start(bf16[128,512]{1,0:T(8,128)(2,1)S(1)} %get-tuple-element.81), channel_id=1, source_target_pairs={{0,8},{4,12},{8,0},{12,4},{16,24},{20,28},{24,16},{28,20},{1,9},{5... | collective-permute-start | bytes 393224 | tf_op jit(solution)/shard_map/ppermute | solution.py:407
  50.3 10.7 %copy-start.14 = (bf16[2,128,512]{2,1,0:T(8,128)(2,1)}, bf16[2,128,512]{2,1,0:T(8,128)(2,1)S(1)}, u32[]{:S(2)}) copy-start(bf16[2,128,512]{2,1,0:T(8,128)(2,1)S(1)} %collective-permute-done.4.refs_4_) | copy-start | bytes 786436
  50.3 22.3 %collective-permute-start.11 = (bf16[128,512]{1,0:T(8,128)(2,1)}, bf16[128,512]{1,0:T(8,128)(2,1)S(1)}, u32[]{:S(2)}, u32[]{:S(2)}) collective-permute-start(bf16[128,512]{1,0:T(8,128)(2,1)} %get-tuple-element.86), channel_id=1, source_target_pairs={{0,28},{4,24},{8,20},{12,16},{16,12},{20,8},{24,4},{28,0},{1,29},{... | collective-permute-start | bytes 393224 | tf_op jit(solution)/shard_map/ppermute | solution.py:407
  50.6 22.0 %collective-permute-start.10 = (bf16[128,512]{1,0:T(8,128)(2,1)S(1)}, bf16[128,512]{1,0:T(8,128)(2,1)S(1)}, u32[]{:S(2)}, u32[]{:S(2)}) collective-permute-start(bf16[128,512]{1,0:T(8,128)(2,1)S(1)} %get-tuple-element.85), channel_id=1, source_target_pairs={{0,24},{4,28},{8,16},{12,20},{16,8},{20,12},{24,0},{28,4},{1,25},{... | collective-permute-start | bytes 393224 | tf_op jit(solution)/shard_map/ppermute | solution.py:407
  52.1 20.5 %collective-permute-start.8 = (bf16[128,512]{1,0:T(8,128)(2,1)S(1)}, bf16[128,512]{1,0:T(8,128)(2,1)S(1)}, u32[]{:S(2)}, u32[]{:S(2)}) collective-permute-start(bf16[128,512]{1,0:T(8,128)(2,1)S(1)} %get-tuple-element.84), channel_id=1, source_target_pairs={{0,20},{4,16},{8,28},{12,24},{16,4},{20,0},{24,12},{28,8},{1,21},{... | collective-permute-start | bytes 393224 | tf_op jit(solution)/shard_map/ppermute | solution.py:407
  58.4 14.3 %copy-start.3 = (bf16[128,512]{1,0:T(8,128)(2,1)}, bf16[128,512]{1,0:T(8,128)(2,1)S(1)}, u32[]{:S(2)}) copy-start(bf16[128,512]{1,0:T(8,128)(2,1)S(1)} %collective-permute-done.2.refs_2_) | copy-start | bytes 393220
  58.4 14.2 %collective-permute-start.7 = (bf16[128,512]{1,0:T(8,128)(2,1)S(1)}, bf16[128,512]{1,0:T(8,128)(2,1)S(1)}, u32[]{:S(2)}, u32[]{:S(2)}) collective-permute-start(bf16[128,512]{1,0:T(8,128)(2,1)S(1)} %get-tuple-element.83), channel_id=1, source_target_pairs={{0,16},{4,20},{8,24},{12,28},{16,0},{20,4},{24,8},{28,12},{1,17},{... | collective-permute-start | bytes 393224 | tf_op jit(solution)/shard_map/ppermute | solution.py:407
  58.4 1.8 copy-start.15
  58.4 14.2 %collective-permute-start.3 = (bf16[128,512]{1,0:T(8,128)(2,1)S(1)}, bf16[128,512]{1,0:T(8,128)(2,1)S(1)}, u32[]{:S(2)}, u32[]{:S(2)}) collective-permute-start(bf16[128,512]{1,0:T(8,128)(2,1)S(1)} %get-tuple-element.82), channel_id=1, source_target_pairs={{0,12},{4,8},{8,4},{12,0},{16,28},{20,24},{24,20},{28,16},{1,13},{... | collective-permute-start | bytes 393224 | tf_op jit(solution)/shard_map/ppermute | solution.py:407
  72.6 5.3 %copy-start.4 = (bf16[128,512]{1,0:T(8,128)(2,1)}, bf16[128,512]{1,0:T(8,128)(2,1)S(1)}, u32[]{:S(2)}) copy-start(bf16[128,512]{1,0:T(8,128)(2,1)S(1)} %collective-permute-done.11.refs_7_) | copy-start | bytes 393220
  72.6 5.3 %copy-start.5 = (bf16[128,512]{1,0:T(8,128)(2,1)}, bf16[128,512]{1,0:T(8,128)(2,1)S(1)}, u32[]{:S(2)}) copy-start(bf16[128,512]{1,0:T(8,128)(2,1)S(1)} %collective-permute-done.10.refs_6_) | copy-start | bytes 393220
  72.6 5.2 %copy-start.6 = (bf16[128,512]{1,0:T(8,128)(2,1)}, bf16[128,512]{1,0:T(8,128)(2,1)S(1)}, u32[]{:S(2)}) copy-start(bf16[128,512]{1,0:T(8,128)(2,1)S(1)} %collective-permute-done.8.refs_5_) | copy-start | bytes 393220
  72.6 5.2 %copy-start.7 = (bf16[128,512]{1,0:T(8,128)(2,1)}, bf16[128,512]{1,0:T(8,128)(2,1)S(1)}, u32[]{:S(2)}) copy-start(bf16[128,512]{1,0:T(8,128)(2,1)S(1)} %collective-permute-done.7.refs_4_) | copy-start | bytes 393220
  72.7 5.2 %copy-start.8 = (bf16[128,512]{1,0:T(8,128)(2,1)}, bf16[128,512]{1,0:T(8,128)(2,1)S(1)}, u32[]{:S(2)}) copy-start(bf16[128,512]{1,0:T(8,128)(2,1)S(1)} %collective-permute-done.3.refs_3_) | copy-start | bytes 393220
  77.9 14.6 %all-to-all-start = ((bf16[8,24,768]{2,1,0:T(8,128)(2,1)}), bf16[8,24,768]{2,1,0:T(8,128)(2,1)S(1)}, u32[]{:S(2)}, u32[]{:S(2)}) async-start(bf16[8,24,768]{2,1,0:T(8,128)(2,1)} %get-tuple-element.93), calls=%async_computation | async-start | bytes 589824 | tf_op jit(solution)/shard_map/all_to_all | solution.py:381
  89.9 5.6 %collective-permute-start.17 = (bf16[152,256]{1,0:T(8,128)(2,1)}, bf16[152,256]{1,0:T(8,128)(2,1)S(1)}, u32[]{:S(2)}, u32[]{:S(2)}) collective-permute-start(bf16[152,256]{1,0:T(8,128)(2,1)} %get-tuple-element.108), channel_id=1, source_target_pairs={{0,16},{4,20},{8,24},{12,28},{16,0},{20,4},{24,8},{28,12},{1,17},{... | collective-permute-start | bytes 233480 | tf_op jit(solution)/shard_map/ppermute | solution.py:407
  95.5 22.8 %all-to-all-start.1 = ((bf16[8,24,768]{2,1,0:T(8,128)(2,1)}), bf16[8,24,768]{2,1,0:T(8,128)(2,1)S(1)}, u32[]{:S(2)}, u32[]{:S(2)}) async-start(bf16[8,24,768]{2,1,0:T(8,128)(2,1)} %get-tuple-element.113), calls=%async_computation.1 | async-start | bytes 589824 | tf_op jit(solution)/shard_map/all_to_all | solution.py:381
  102.3 14.1 %collective-permute-start.18 = (bf16[152,256]{1,0:T(8,128)(2,1)}, bf16[152,256]{1,0:T(8,128)(2,1)S(1)}, u32[]{:S(2)}, u32[]{:S(2)}) collective-permute-start(bf16[152,256]{1,0:T(8,128)(2,1)} %get-tuple-element.109), channel_id=1, source_target_pairs={{0,20},{4,16},{8,28},{12,24},{16,4},{20,0},{24,12},{28,8},{1,21},{... | collective-permute-start | bytes 233480 | tf_op jit(solution)/shard_map/ppermute | solution.py:407
  105.6 12.3 %collective-permute-start.19 = (bf16[152,256]{1,0:T(8,128)(2,1)}, bf16[152,256]{1,0:T(8,128)(2,1)S(1)}, u32[]{:S(2)}, u32[]{:S(2)}) collective-permute-start(bf16[152,256]{1,0:T(8,128)(2,1)} %get-tuple-element.110), channel_id=1, source_target_pairs={{0,24},{4,28},{8,16},{12,20},{16,8},{20,12},{24,0},{28,4},{1,25},{... | collective-permute-start | bytes 233480 | tf_op jit(solution)/shard_map/ppermute | solution.py:407
  105.6 12.7 %collective-permute-start.20 = (bf16[152,256]{1,0:T(8,128)(2,1)}, bf16[152,256]{1,0:T(8,128)(2,1)S(1)}, u32[]{:S(2)}, u32[]{:S(2)}) collective-permute-start(bf16[152,256]{1,0:T(8,128)(2,1)} %get-tuple-element.111), channel_id=1, source_target_pairs={{0,28},{4,24},{8,20},{12,16},{16,12},{20,8},{24,4},{28,0},{1,29},{... | collective-permute-start | bytes 233480 | tf_op jit(solution)/shard_map/ppermute | solution.py:407
  112.5 12.8 %collective-permute-start.14 = (bf16[152,512]{1,0:T(8,128)(2,1)}, bf16[152,512]{1,0:T(8,128)(2,1)S(1)}, u32[]{:S(2)}, u32[]{:S(2)}) collective-permute-start(bf16[152,512]{1,0:T(8,128)(2,1)} %get-tuple-element.105), channel_id=1, source_target_pairs={{0,4},{4,0},{8,12},{12,8},{16,20},{20,16},{24,28},{28,24},{1,5},{5... | collective-permute-start | bytes 466952 | tf_op jit(solution)/shard_map/ppermute | solution.py:407
  114.1 11.9 %collective-permute-start.15 = (bf16[152,512]{1,0:T(8,128)(2,1)}, bf16[152,512]{1,0:T(8,128)(2,1)S(1)}, u32[]{:S(2)}, u32[]{:S(2)}) collective-permute-start(bf16[152,512]{1,0:T(8,128)(2,1)} %get-tuple-element.106), channel_id=1, source_target_pairs={{0,8},{4,12},{8,0},{12,4},{16,24},{20,28},{24,16},{28,20},{1,9},{5... | collective-permute-start | bytes 466952 | tf_op jit(solution)/shard_map/ppermute | solution.py:407
  116.4 14.0 %collective-permute-start.16 = (bf16[152,512]{1,0:T(8,128)(2,1)}, bf16[152,512]{1,0:T(8,128)(2,1)S(1)}, u32[]{:S(2)}, u32[]{:S(2)}) collective-permute-start(bf16[152,512]{1,0:T(8,128)(2,1)} %get-tuple-element.107), channel_id=1, source_target_pairs={{0,12},{4,8},{8,4},{12,0},{16,28},{20,24},{24,20},{28,16},{1,13},{... | collective-permute-start | bytes 466952 | tf_op jit(solution)/shard_map/ppermute | solution.py:407
  118.2 3.2 %copy-start.19 = (bf16[152,256]{1,0:T(8,128)(2,1)S(1)}, bf16[152,256]{1,0:T(8,128)(2,1)}, u32[]{:S(2)}) copy-start(bf16[152,256]{1,0:T(8,128)(2,1)} %get-tuple-element.121) | copy-start | bytes 233476
  118.2 4.7 %copy-start.18 = (bf16[152,256]{1,0:T(8,128)(2,1)S(1)}, bf16[152,256]{1,0:T(8,128)(2,1)}, u32[]{:S(2)}) copy-start(bf16[152,256]{1,0:T(8,128)(2,1)} %get-tuple-element.127) | copy-start | bytes 233476
  118.2 7.1 %copy-start.17 = (bf16[152,256]{1,0:T(8,128)(2,1)S(1)}, bf16[152,256]{1,0:T(8,128)(2,1)}, u32[]{:S(2)}) copy-start(bf16[152,256]{1,0:T(8,128)(2,1)} %get-tuple-element.125) | copy-start | bytes 233476
  118.2 7.7 %copy-start.16 = (bf16[152,256]{1,0:T(8,128)(2,1)S(1)}, bf16[152,256]{1,0:T(8,128)(2,1)}, u32[]{:S(2)}) copy-start(bf16[152,256]{1,0:T(8,128)(2,1)} %get-tuple-element.123) | copy-start | bytes 233476
  121.4 9.0 %collective-permute-start.21 = (bf16[152,256]{1,0:T(8,128)(2,1)S(1)}, bf16[152,256]{1,0:T(8,128)(2,1)S(1)}, u32[]{:S(2)}, u32[]{:S(2)}) collective-permute-start(bf16[152,256]{1,0:T(8,128)(2,1)S(1)} %copy-done.19), channel_id=1, source_target_pairs={{0,16},{4,20},{8,24},{12,28},{16,0},{20,4},{24,8},{28,12},{1,17},{... | collective-permute-start | bytes 233480 | tf_op jit(solution)/shard_map/ppermute | solution.py:407
  121.8 1.2 collective-permute-start.25
  122.9 15.5 %collective-permute-start.24 = (bf16[152,256]{1,0:T(8,128)(2,1)S(1)}, bf16[152,256]{1,0:T(8,128)(2,1)S(1)}, u32[]{:S(2)}, u32[]{:S(2)}) collective-permute-start(bf16[152,256]{1,0:T(8,128)(2,1)S(1)} %copy-done.18), channel_id=1, source_target_pairs={{0,28},{4,24},{8,20},{12,16},{16,12},{20,8},{24,4},{28,0},{1,29},{... | collective-permute-start | bytes 233480 | tf_op jit(solution)/shard_map/ppermute | solution.py:407
  125.3 13.1 %collective-permute-start.23 = (bf16[152,256]{1,0:T(8,128)(2,1)S(1)}, bf16[152,256]{1,0:T(8,128)(2,1)S(1)}, u32[]{:S(2)}, u32[]{:S(2)}) collective-permute-start(bf16[152,256]{1,0:T(8,128)(2,1)S(1)} %copy-done.17), channel_id=1, source_target_pairs={{0,24},{4,28},{8,16},{12,20},{16,8},{20,12},{24,0},{28,4},{1,25},{... | collective-permute-start | bytes 233480 | tf_op jit(solution)/shard_map/ppermute | solution.py:407
  125.9 12.5 %collective-permute-start.22 = (bf16[152,256]{1,0:T(8,128)(2,1)S(1)}, bf16[152,256]{1,0:T(8,128)(2,1)S(1)}, u32[]{:S(2)}, u32[]{:S(2)}) collective-permute-start(bf16[152,256]{1,0:T(8,128)(2,1)S(1)} %copy-done.16), channel_id=1, source_target_pairs={{0,20},{4,16},{8,28},{12,24},{16,4},{20,0},{24,12},{28,8},{1,21},{... | collective-permute-start | bytes 233480 | tf_op jit(solution)/shard_map/ppermute | solution.py:407
  138.5 32.0 %all-to-all-start.2 = ((bf16[8,280,256]{2,1,0:T(8,128)(2,1)}), bf16[8,280,256]{2,1,0:T(8,128)(2,1)}, u32[]{:S(2)}, u32[]{:S(2)}) async-start(bf16[8,280,256]{2,1,0:T(8,128)(2,1)} %attention_back.2), calls=%async_computation.2 | async-start | bytes 2293760 | tf_op jit(solution)/shard_map/all_to_all | solution.py:381
  143.0 3.8 %collective-permute-start.26 = (f32[8,640]{1,0:T(8,128)S(1)}, f32[8,640]{1,0:T(8,128)S(1)}, u32[]{:S(2)}, u32[]{:S(2)}) collective-permute-start(f32[8,640]{1,0:T(8,128)S(1)} %add.89), channel_id=1, source_target_pairs={{0,2},{1,3},{2,0},{3,1},{4,6},{5,7},{6,4},{7,5},{8,10},{9,11},{10,... | collective-permute-start | bytes 61448 | tf_op jit(solution)/shard_map/ppermute | solution.py:612
  146.8 23.7 %copy-start.9 = (bf16[152,512]{1,0:T(8,128)(2,1)S(1)}, bf16[152,512]{1,0:T(8,128)(2,1)}, u32[]{:S(2)}) copy-start(bf16[152,512]{1,0:T(8,128)(2,1)} %get-tuple-element.104.refs_0_) | copy-start | bytes 466948
  155.0 9.1 %collective-permute-start.27 = (bf16[304,256]{1,0:T(8,128)(2,1)}, bf16[304,256]{1,0:T(8,128)(2,1)S(1)}, u32[]{:S(2)}, u32[]{:S(2)}) collective-permute-start(bf16[304,256]{1,0:T(8,128)(2,1)} %get-tuple-element.138), channel_id=1, source_target_pairs={{0,4},{4,0},{8,12},{12,8},{16,20},{20,16},{24,28},{28,24},{1,5},{5... | collective-permute-start | bytes 466952 | tf_op jit(solution)/shard_map/ppermute | solution.py:407
  156.5 11.0 %collective-permute-start.28 = (bf16[304,256]{1,0:T(8,128)(2,1)}, bf16[304,256]{1,0:T(8,128)(2,1)S(1)}, u32[]{:S(2)}, u32[]{:S(2)}) collective-permute-start(bf16[304,256]{1,0:T(8,128)(2,1)} %get-tuple-element.139), channel_id=1, source_target_pairs={{0,8},{4,12},{8,0},{12,4},{16,24},{20,28},{24,16},{28,20},{1,9},{5... | collective-permute-start | bytes 466952 | tf_op jit(solution)/shard_map/ppermute | solution.py:407
  157.1 17.0 %collective-permute-start.29 = (bf16[304,256]{1,0:T(8,128)(2,1)}, bf16[304,256]{1,0:T(8,128)(2,1)S(1)}, u32[]{:S(2)}, u32[]{:S(2)}) collective-permute-start(bf16[304,256]{1,0:T(8,128)(2,1)} %get-tuple-element.140), channel_id=1, source_target_pairs={{0,12},{4,8},{8,4},{12,0},{16,28},{20,24},{24,20},{28,16},{1,13},{... | collective-permute-start | bytes 466952 | tf_op jit(solution)/shard_map/ppermute | solution.py:407
  158.5 27.0 %collective-permute-start.30 = (bf16[304,256]{1,0:T(8,128)(2,1)}, bf16[304,256]{1,0:T(8,128)(2,1)S(1)}, u32[]{:S(2)}, u32[]{:S(2)}) collective-permute-start(bf16[304,256]{1,0:T(8,128)(2,1)} %get-tuple-element.141), channel_id=1, source_target_pairs={{0,16},{4,20},{8,24},{12,28},{16,0},{20,4},{24,8},{28,12},{1,17},{... | collective-permute-start | bytes 466952 | tf_op jit(solution)/shard_map/ppermute | solution.py:407
  160.9 27.9 %collective-permute-start.31 = (bf16[304,256]{1,0:T(8,128)(2,1)}, bf16[304,256]{1,0:T(8,128)(2,1)S(1)}, u32[]{:S(2)}, u32[]{:S(2)}) collective-permute-start(bf16[304,256]{1,0:T(8,128)(2,1)} %get-tuple-element.142), channel_id=1, source_target_pairs={{0,20},{4,16},{8,28},{12,24},{16,4},{20,0},{24,12},{28,8},{1,21},{... | collective-permute-start | bytes 466952 | tf_op jit(solution)/shard_map/ppermute | solution.py:407
  164.1 30.1 %collective-permute-start.32 = (bf16[304,256]{1,0:T(8,128)(2,1)}, bf16[304,256]{1,0:T(8,128)(2,1)S(1)}, u32[]{:S(2)}, u32[]{:S(2)}) collective-permute-start(bf16[304,256]{1,0:T(8,128)(2,1)} %get-tuple-element.143), channel_id=1, source_target_pairs={{0,24},{4,28},{8,16},{12,20},{16,8},{20,12},{24,0},{28,4},{1,25},{... | collective-permute-start | bytes 466952 | tf_op jit(solution)/shard_map/ppermute | solution.py:407
  167.5 29.9 %collective-permute-start.33 = (bf16[304,256]{1,0:T(8,128)(2,1)}, bf16[304,256]{1,0:T(8,128)(2,1)S(1)}, u32[]{:S(2)}, u32[]{:S(2)}) collective-permute-start(bf16[304,256]{1,0:T(8,128)(2,1)} %get-tuple-element.144), channel_id=1, source_target_pairs={{0,28},{4,24},{8,20},{12,16},{16,12},{20,8},{24,4},{28,0},{1,29},{... | collective-permute-start | bytes 466952 | tf_op jit(solution)/shard_map/ppermute | solution.py:407
  170.5 27.0 %copy-start.10 = (bf16[304,256]{1,0:T(8,128)(2,1)S(1)}, bf16[304,256]{1,0:T(8,128)(2,1)}, u32[]{:S(2)}) copy-start(bf16[304,256]{1,0:T(8,128)(2,1)} %get-tuple-element.137.refs_0_) | copy-start | bytes 466948

commit v5 on v4

--- a/solution.py
+++ b/solution.py
@@ -106,19 +106,34 @@
         q_ref[0, at] = qk_refs[s][0]
         k_ref[0, at] = qk_refs[s][1]
     keys = k_ref[0]
-
-    def step(i, total_r):
-        at = chunk_rows(i, chunk)
-        s = dot_nt(q_ref[0, at], keys) * (SCALE * LOG2E)
+    count = tokens // chunk
+
+    def scores(i):
+        return dot_nt(q_ref[0, chunk_rows(i, chunk)], keys)
+
+    def reduce(i, raw):
+        s = raw * (SCALE * LOG2E)
         peak = jnp.max(s, axis=1, keepdims=True)
         e = jnp.exp2(s - peak)
         total = jnp.sum(e, axis=1, keepdims=True)
         p = (e * (1.0 / total)).astype(BF)
         lse = (peak + jnp.log2(total)) * (-1.0 / (SCALE * LOG2E))
-        aug_ref[0, at] = lanes_three(lse, (chunk, LANES), 0).astype(BF)
-        return total_r + dot_nn(mt_ref[i], p)
-
-    r = run_steps(tokens // chunk, step, jnp.zeros((RR, tokens), F32))
+        aug_ref[0, chunk_rows(i, chunk)] = lanes_three(lse, (chunk, LANES), 0).astype(BF)
+        return dot_nn(mt_ref[i], p)
+
+    if count <= 4:
+        ahead = scores(0)
+        r = None
+        for i in range(count):
+            now = ahead
+            if i + 1 < count:
+                ahead = scores(i + 1)
+            part = reduce(i, now)
+            r = part if r is None else r + part
+    else:
+        r = lax.fori_loop(
+            0, count, lambda i, r: r + reduce(i, scores(i)), jnp.zeros((RR, tokens), F32)
+        )
     for s in range(blocks):
         r_ref[s, 0] = r[:FR, s * LANES : (s + 1) * LANES].astype(BF)
 
@@ -413,7 +428,7 @@
     blocks = {s: query_key(s) for s in far}
     for s in far:
         qk[s] = send(blocks[s], s)
-    most = [qk[s] for s in far[: half - 1]]
+    most = [qk[s] for s in far[-2:]]
     every = [qk[s] for s in far]
     for s in near:
         behind = [qk[s - 1]] if s > 1 else list(blocks.values())
@@ -422,7 +437,7 @@
         behind = v[s - 1] if s > 1 else qk[s]
         v[s] = send(after(columns_for(value_in[0], s), behind), s)
     for i, s in enumerate(far):
-        v[s] = send(after(columns_for(value_in[0], s), *(most if i < 2 else every)), s)
+        v[s] = send(after(columns_for(value_in[0], s), *(most if i == half - 1 else every)), s)
     qk, v = [qk[s] for s in range(n)], [v[s] for s in range(n)]
 
     frames = frame_of_token[0]

time: 200 us -> 200 us (level)
    all_to_all x3, starting transfers between devices: 18.3 us -> 16.2 us  [exchange(): return lax.all_to_all(array, 'gen', split_axis=0, concat_axis=0, tiled=True)]
  transfers between devices with their start and end apart: 37 -> 37, of which waited for: 16 -> 17; matrix products, arithmetic and copies ran while one was open for 2% -> 2% of each run, Pallas kernels for 23% -> 22%
where the time goes in v5:
time: 200 us
  starting transfers between devices  76.1 us (38%)
  waiting for transfers between devices  65.5 us (33%)
  Pallas kernels  51.1 us (26%)
  local copies, waits for them, and re-layouts  3.27 us (2%)
    ppermute x32, waiting for transfers between devices, send(): return lax.ppermute(array, 'gen', [(i, i ^ s) for i in range(n)])  61.7 us
    ppermute x32, starting transfers between devices, send(): return lax.ppermute(array, 'gen', [(i, i ^ s) for i in range(n)])  58.3 us
    pallas_call x2, Pallas kernels, back(): pl.pallas_call(functools.partial(back_kernel, n, apart), grid=(last - fir...  16.3 us
    all_to_all x3, starting transfers between devices, exchange(): return lax.all_to_all(array, 'gen', split_axis=0, concat_axis=0, tiled=True)  16.2 us
    pallas_call x1, Pallas kernels, on_device(): pl.pallas_call(functools.partial(stats_kernel, n), grid=(heads,), in_spec...  9.98 us
    pallas_call x2, Pallas kernels, output(): pl.pallas_call(functools.partial(output_kernel, n), grid=(last - first,),...  9.89 us
    pallas_call x1, Pallas kernels, on_device(): pl.pallas_call(functools.partial(pool_kernel, n, heads, chunk), in_specs=...  5.14 us
  transfers between devices with their start and end apart: 37, of which 17 were waited for; matrix products, arithmetic and copies ran while one was open for 2% of the time, Pallas kernels for 22%

profile of v5, /device:TPU:8, one launch (start us, length us, event | category | flops | bytes accessed | tf_op | source)
XLA Modules:
  0.0 199.6 jit_solution(18047529324464600918)
XLA Ops:
  0.7 1.8 constant_dynamic-slice_fusion.1
  2.6 2.6 %collective-permute-start.7 = (bf16[2,128,512]{2,1,0:T(8,128)(2,1)S(1)}, bf16[2,128,512]{2,1,0:T(8,128)(2,1)}, u32[]{:S(2)}, u32[]{:S(2)}) collective-permute-start(bf16[2,128,512]{2,1,0:T(8,128)(2,1)S(1)} %pad_maximum_fusion.4), channel_id=1, source_target_pairs={{0,28},{4,24},{8,20},{12,16},{16,12},{20,8},{24,4},{28,0},{1,29},{... | collective-permute-start | bytes 786440 | tf_op jit(solution)/shard_map/ppermute | solution.py:422
  5.2 0.5 collective-permute-start.6
  5.8 4.4 %collective-permute-start.5 = (bf16[2,128,512]{2,1,0:T(8,128)(2,1)S(1)}, bf16[2,128,512]{2,1,0:T(8,128)(2,1)}, u32[]{:S(2)}, u32[]{:S(2)}) collective-permute-start(bf16[2,128,512]{2,1,0:T(8,128)(2,1)S(1)} %pad_maximum_fusion.2), channel_id=1, source_target_pairs={{0,20},{4,16},{8,28},{12,24},{16,4},{20,0},{24,12},{28,8},{1,21},{... | collective-permute-start | bytes 786440 | tf_op jit(solution)/shard_map/ppermute | solution.py:422
  10.2 1.6 collective-permute-start
  11.9 0.6 gather_fusion
  12.6 5.1 %collective-permute-done.refs_1_ = bf16[2,128,512]{2,1,0:T(8,128)(2,1)} collective-permute-done((bf16[2,128,512]{2,1,0:T(8,128)(2,1)S(1)}, bf16[2,128,512]{2,1,0:T(8,128)(2,1)}, u32[]{:S(2)}, u32[]{:S(2)}) %collective-permute-start) | collective-permute-done | bytes 262176 | tf_op jit(solution)/shard_map/ppermute | solution.py:422
  17.7 2.1 %collective-permute-start.12 = (bf16[2,128,512]{2,1,0:T(8,128)(2,1)S(1)}, bf16[2,128,512]{2,1,0:T(8,128)(2,1)S(1)}, u32[]{:S(2)}, u32[]{:S(2)}) collective-permute-start(bf16[2,128,512]{2,1,0:T(8,128)(2,1)S(1)} %pad_maximum_fusion.6), channel_id=1, source_target_pairs={{0,8},{4,12},{8,0},{12,4},{16,24},{20,28},{24,16},{28,20},{1,9},{5... | collective-permute-start | bytes 786440 | tf_op jit(solution)/shard_map/ppermute | solution.py:422
  19.8 0.8 dynamic-slice_bitcast_fusion
  20.5 1.4 collective-permute-start.1
  22.1 8.5 %collective-permute-done.12.refs_2_ = bf16[2,128,512]{2,1,0:T(8,128)(2,1)S(1)} collective-permute-done((bf16[2,128,512]{2,1,0:T(8,128)(2,1)S(1)}, bf16[2,128,512]{2,1,0:T(8,128)(2,1)S(1)}, u32[]{:S(2)}, u32[]{:S(2)}) %collective-permute-start.12) | collective-permute-done | bytes 262176 | tf_op jit(solution)/shard_map/ppermute | solution.py:422
  30.6 0.7 collective-permute-done.1.refs_1_
  31.3 0.2 collective-permute-start.13
  32.1 2.9 %collective-permute-start.2 = (bf16[128,512]{1,0:T(8,128)(2,1)S(1)}, bf16[128,512]{1,0:T(8,128)(2,1)S(1)}, u32[]{:S(2)}, u32[]{:S(2)}) collective-permute-start(bf16[128,512]{1,0:T(8,128)(2,1)S(1)} %get-tuple-element.81), channel_id=1, source_target_pairs={{0,8},{4,12},{8,0},{12,4},{16,24},{20,28},{24,16},{28,20},{1,9},{5... | collective-permute-start | bytes 393224 | tf_op jit(solution)/shard_map/ppermute | solution.py:422
  35.0 5.7 %collective-permute-done.6.refs_6_ = bf16[2,128,512]{2,1,0:T(8,128)(2,1)} collective-permute-done((bf16[2,128,512]{2,1,0:T(8,128)(2,1)S(1)}, bf16[2,128,512]{2,1,0:T(8,128)(2,1)}, u32[]{:S(2)}, u32[]{:S(2)}) %collective-permute-start.6) | collective-permute-done | bytes 262176 | tf_op jit(solution)/shard_map/ppermute | solution.py:422
  40.7 1.8 collective-permute-start.11
  42.6 5.9 %collective-permute-done.5.refs_5_ = bf16[2,128,512]{2,1,0:T(8,128)(2,1)} collective-permute-done((bf16[2,128,512]{2,1,0:T(8,128)(2,1)S(1)}, bf16[2,128,512]{2,1,0:T(8,128)(2,1)}, u32[]{:S(2)}, u32[]{:S(2)}) %collective-permute-start.5) | collective-permute-done | bytes 262176 | tf_op jit(solution)/shard_map/ppermute | solution.py:422
  48.5 5.6 %collective-permute-done.4.refs_4_ = bf16[2,128,512]{2,1,0:T(8,128)(2,1)S(1)} collective-permute-done((bf16[2,128,512]{2,1,0:T(8,128)(2,1)S(1)}, bf16[2,128,512]{2,1,0:T(8,128)(2,1)S(1)}, u32[]{:S(2)}, u32[]{:S(2)}) %collective-permute-start.4) | collective-permute-done | bytes 262176 | tf_op jit(solution)/shard_map/ppermute | solution.py:422
  54.1 0.2 collective-permute-start.10
  54.3 4.3 %collective-permute-start.9 = (bf16[128,512]{1,0:T(8,128)(2,1)S(1)}, bf16[128,512]{1,0:T(8,128)(2,1)S(1)}, u32[]{:S(2)}, u32[]{:S(2)}) collective-permute-start(bf16[128,512]{1,0:T(8,128)(2,1)S(1)} %get-tuple-element.84), channel_id=1, source_target_pairs={{0,20},{4,16},{8,28},{12,24},{16,4},{20,0},{24,12},{28,8},{1,21},{... | collective-permute-start | bytes 393224 | tf_op jit(solution)/shard_map/ppermute | solution.py:422
  58.7 4.1 %collective-permute-start.3 = (bf16[128,512]{1,0:T(8,128)(2,1)S(1)}, bf16[128,512]{1,0:T(8,128)(2,1)S(1)}, u32[]{:S(2)}, u32[]{:S(2)}) collective-permute-start(bf16[128,512]{1,0:T(8,128)(2,1)S(1)} %get-tuple-element.82), channel_id=1, source_target_pairs={{0,12},{4,8},{8,4},{12,0},{16,28},{20,24},{24,20},{28,16},{1,13},{... | collective-permute-start | bytes 393224 | tf_op jit(solution)/shard_map/ppermute | solution.py:422
  62.8 0.7 pad_maximum_fusion.5.refs_0_
  63.5 10.0 %softmax_stats.1 = (bf16[4,1024,128]{2,1,0:T(8,128)(2,1)}, bf16[8,4,24,128]{3,2,1,0:T(8,128)(2,1)}, bf16[4,1024,128]{2,1,0:T(8,128)(2,1)}, bf16[4,1024,128]{2,1,0:T(8,128)(2,1)}) custom-call(bf16[2,128,512]{2,1,0:T(8,128)(2,1)} %pad_maximum_fusion.5.refs_0_, bf16[2,128,512]{2,1,0:T(8,128)(2,1)} %collective-permute-done.refs_1_, ...), custom_call_target="tpu_custom_call" | custom-call | flops 1073741824 | bytes 4194304 | tf_op jit(solution)/shard_map/softmax_stats/pallas_call | solution.py:478
  73.6 5.1 %pool_project.1 = (bf16[8,24,768]{2,1,0:T(8,128)(2,1)}, f32[24,512]{1,0:T(8,128)S(1)}) custom-call(bf16[128,512]{1,0:T(8,128)(2,1)S(1)} %get-tuple-element.175.refs_0_, bf16[128,512]{1,0:T(8,128)(2,1)S(1)} %collective-permute-done.1.refs_1_, bf16[128,512]{1,0:T(8,128)(2,1)S(1)} %collective-permute-done.2.refs_2_, ...), custom_call_target="tpu_custom_call" | custom-call | tf_op jit(solution)/shard_map/pool_project/pallas_call | solution.py:497
  78.8 5.1 %all-to-all-start = ((bf16[8,24,768]{2,1,0:T(8,128)(2,1)}), bf16[8,24,768]{2,1,0:T(8,128)(2,1)S(1)}, u32[]{:S(2)}, u32[]{:S(2)}) async-start(bf16[8,24,768]{2,1,0:T(8,128)(2,1)} %get-tuple-element.93), calls=%async_computation | async-start | bytes 589824 | tf_op jit(solution)/shard_map/all_to_all | solution.py:396
  84.1 4.9 %attention_output.2 = (bf16[152,512]{1,0:T(8,128)(2,1)}, bf16[152,512]{1,0:T(8,128)(2,1)}, bf16[152,512]{1,0:T(8,128)(2,1)}, bf16[152,512]{1,0:T(8,128)(2,1)}, b...) custom-call(bf16[128,512]{1,0:T(8,128)(2,1)} %copy-done.1, ...), custom_call_target="tpu_custom_call" | custom-call | flops 1073741824 | bytes 2097152 | tf_op jit(solution)/shard_map/attention_output/pallas_call | solution.py:526
  89.0 2.4 %collective-permute-start.17 = (bf16[152,256]{1,0:T(8,128)(2,1)}, bf16[152,256]{1,0:T(8,128)(2,1)S(1)}, u32[]{:S(2)}, u32[]{:S(2)}) collective-permute-start(bf16[152,256]{1,0:T(8,128)(2,1)} %get-tuple-element.108), channel_id=1, source_target_pairs={{0,16},{4,20},{8,24},{12,28},{16,0},{20,4},{24,8},{28,12},{1,17},{... | collective-permute-start | bytes 233480 | tf_op jit(solution)/shard_map/ppermute | solution.py:422
  91.4 0.2 multiply_reduce_fusion.rows_ref
  91.6 0.5 all-to-all-done.got_ref
  92.2 0.9 discriminator.1
  93.1 1.6 collective-permute-done.17.refs_4_
  94.7 6.7 %all-to-all-start.1 = ((bf16[8,24,768]{2,1,0:T(8,128)(2,1)}), bf16[8,24,768]{2,1,0:T(8,128)(2,1)S(1)}, u32[]{:S(2)}, u32[]{:S(2)}) async-start(bf16[8,24,768]{2,1,0:T(8,128)(2,1)} %get-tuple-element.113), calls=%async_computation.1 | async-start | bytes 589824 | tf_op jit(solution)/shard_map/all_to_all | solution.py:396
  101.4 3.3 %collective-permute-start.18 = (bf16[152,256]{1,0:T(8,128)(2,1)}, bf16[152,256]{1,0:T(8,128)(2,1)S(1)}, u32[]{:S(2)}, u32[]{:S(2)}) collective-permute-start(bf16[152,256]{1,0:T(8,128)(2,1)} %get-tuple-element.109), channel_id=1, source_target_pairs={{0,20},{4,16},{8,28},{12,24},{16,4},{20,0},{24,12},{28,8},{1,21},{... | collective-permute-start | bytes 233480 | tf_op jit(solution)/shard_map/ppermute | solution.py:422
  104.7 2.0 %collective-permute-start.20 = (bf16[152,256]{1,0:T(8,128)(2,1)}, bf16[152,256]{1,0:T(8,128)(2,1)S(1)}, u32[]{:S(2)}, u32[]{:S(2)}) collective-permute-start(bf16[152,256]{1,0:T(8,128)(2,1)} %get-tuple-element.111), channel_id=1, source_target_pairs={{0,28},{4,24},{8,20},{12,16},{16,12},{20,8},{24,4},{28,0},{1,29},{... | collective-permute-start | bytes 233480 | tf_op jit(solution)/shard_map/ppermute | solution.py:422
  106.7 4.9 %attention_output.3 = (bf16[152,512]{1,0:T(8,128)(2,1)}, bf16[152,512]{1,0:T(8,128)(2,1)}, bf16[152,512]{1,0:T(8,128)(2,1)}, bf16[152,512]{1,0:T(8,128)(2,1)}, b...) custom-call(bf16[128,512]{1,0:T(8,128)(2,1)} %copy-done.1, ...), custom_call_target="tpu_custom_call", output_to_operand_aliasing={{0}: (12, {}), {1}: (13, {}), {2}: (14, {}), {3}: (15, {}),... | custom-call | flops 1073741824 | bytes 2097152 | tf_op jit(solution)/shard_map/attention_output/pallas_call | solution.py:526
  111.7 1.5 collective-permute-start.14
  113.2 2.4 %collective-permute-start.15 = (bf16[152,512]{1,0:T(8,128)(2,1)}, bf16[152,512]{1,0:T(8,128)(2,1)S(1)}, u32[]{:S(2)}, u32[]{:S(2)}) collective-permute-start(bf16[152,512]{1,0:T(8,128)(2,1)} %get-tuple-element.106), channel_id=1, source_target_pairs={{0,8},{4,12},{8,0},{12,4},{16,24},{20,28},{24,16},{28,20},{1,9},{5... | collective-permute-start | bytes 466952 | tf_op jit(solution)/shard_map/ppermute | solution.py:422
  115.5 2.3 %collective-permute-start.16 = (bf16[152,512]{1,0:T(8,128)(2,1)}, bf16[152,512]{1,0:T(8,128)(2,1)S(1)}, u32[]{:S(2)}, u32[]{:S(2)}) collective-permute-start(bf16[152,512]{1,0:T(8,128)(2,1)} %get-tuple-element.107), channel_id=1, source_target_pairs={{0,12},{4,8},{8,4},{12,0},{16,28},{20,24},{24,20},{28,16},{1,13},{... | collective-permute-start | bytes 466952 | tf_op jit(solution)/shard_map/ppermute | solution.py:422
  117.9 0.4 collective-permute-done.20.refs_7_
  118.3 3.1 %pooled_gradient.1 = (bf16[128,512]{1,0:T(8,128)(2,1)S(1)}, f32[8,640]{1,0:T(8,128)S(1)}) custom-call(bf16[8,24,768]{2,1,0:T(8,128)(2,1)S(1)} %all-to-all-done.1.got_ref, bf16[512,5120]{1,0:T(8,128)(2,1)} %w_hbm.1, f32[24,512]{1,0:T(8,128)S(1)} %get-tuple-element.117.pooled_ref, f32[24,128]{1,0:T(8,128)S(1)} %broadcast_select_fusion.refs_9_.meta_ref, ...), custom_call_target="tpu_custom_call" | custom-call | tf_op jit(solution)/shard_map/pooled_gradient/pallas_call | solution.py:570
  121.7 0.2 fusion.m_ref
  121.9 1.0 collective-permute-done.25
  122.8 1.6 collective-permute-start.24
  124.4 1.1 collective-permute-start.23
  125.5 5.0 %collective-permute-start.22 = (bf16[152,256]{1,0:T(8,128)(2,1)S(1)}, bf16[152,256]{1,0:T(8,128)(2,1)S(1)}, u32[]{:S(2)}, u32[]{:S(2)}) collective-permute-start(bf16[152,256]{1,0:T(8,128)(2,1)S(1)} %copy-done.16), channel_id=1, source_target_pairs={{0,20},{4,16},{8,28},{12,24},{16,4},{20,0},{24,12},{28,8},{1,21},{... | collective-permute-start | bytes 233480 | tf_op jit(solution)/shard_map/ppermute | solution.py:422
  130.5 8.1 %attention_back.2 = bf16[8,280,256]{2,1,0:T(8,128)(2,1)} custom-call(bf16[4,1024,128]{2,1,0:T(8,128)(2,1)} %get-tuple-element.89.refs_8_.q_ref, bf16[4,1024,128]{2,1,0:T(8,128)(2,1)} %get-tuple-element.90.refs_9_.k_ref, bf16[4,1024,128]{2,1,0:T(8,128)(2,1)} %get-tuple-element.130.v_ref, bf16[4,1024,128]{2,1,0:T(8,128)(2,1)} %get-tuple-element.115.o_ref, ...), custom_call_target="tpu_custom_call" | custom-call | flops 2147483648 | bytes 4194304 | tf_op jit(solution)/shard_map/attention_back/pallas_call | solution.py:591
  138.6 4.3 %all-to-all-start.2 = ((bf16[8,280,256]{2,1,0:T(8,128)(2,1)}), bf16[8,280,256]{2,1,0:T(8,128)(2,1)}, u32[]{:S(2)}, u32[]{:S(2)}) async-start(bf16[8,280,256]{2,1,0:T(8,128)(2,1)} %attention_back.2), calls=%async_computation.2 | async-start | bytes 2293760 | tf_op jit(solution)/shard_map/all_to_all | solution.py:396
  142.9 1.5 collective-permute-start.26
  144.4 2.3 %collective-permute-done.26 = f32[8,640]{1,0:T(8,128)S(1)} collective-permute-done((f32[8,640]{1,0:T(8,128)S(1)}, f32[8,640]{1,0:T(8,128)S(1)}, u32[]{:S(2)}, u32[]{:S(2)}) %collective-permute-start.26) | collective-permute-done | bytes 20512 | tf_op jit(solution)/shard_map/ppermute | solution.py:627
  146.7 8.2 %attention_back.3 = (bf16[304,256]{1,0:T(8,128)(2,1)}, bf16[304,256]{1,0:T(8,128)(2,1)}, bf16[304,256]{1,0:T(8,128)(2,1)}, bf16[304,256]{1,0:T(8,128)(2,1)}, bf1...) custom-call(bf16[4,1024,128]{2,1,0:T(8,128)(2,1)} %get-tuple-element.89.r, ...), custom_call_target="tpu_custom_call" | custom-call | flops 2147483648 | bytes 4194304 | tf_op jit(solution)/shard_map/attention_back/pallas_call | solution.py:591
  154.9 1.5 collective-permute-start.27
  156.4 0.5 collective-permute-start.28
  157.0 1.5 collective-permute-start.29
  158.5 2.4 %collective-permute-start.30 = (bf16[304,256]{1,0:T(8,128)(2,1)}, bf16[304,256]{1,0:T(8,128)(2,1)S(1)}, u32[]{:S(2)}, u32[]{:S(2)}) collective-permute-start(bf16[304,256]{1,0:T(8,128)(2,1)} %get-tuple-element.141), channel_id=1, source_target_pairs={{0,16},{4,20},{8,24},{12,28},{16,0},{20,4},{24,8},{28,12},{1,17},{... | collective-permute-start | bytes 466952 | tf_op jit(solution)/shard_map/ppermute | solution.py:422
  160.9 1.4 collective-permute-start.31
  162.3 1.5 collective-permute-done.27.refs_1_
  163.8 3.4 %collective-permute-done.28.refs_2_ = bf16[304,256]{1,0:T(8,128)(2,1)S(1)} collective-permute-done((bf16[304,256]{1,0:T(8,128)(2,1)}, bf16[304,256]{1,0:T(8,128)(2,1)S(1)}, u32[]{:S(2)}, u32[]{:S(2)}) %collective-permute-start.28) | collective-permute-done | bytes 155680 | tf_op jit(solution)/shard_map/ppermute | solution.py:422
  167.2 3.2 %collective-permute-start.33 = (bf16[304,256]{1,0:T(8,128)(2,1)}, bf16[304,256]{1,0:T(8,128)(2,1)S(1)}, u32[]{:S(2)}, u32[]{:S(2)}) collective-permute-start(bf16[304,256]{1,0:T(8,128)(2,1)} %get-tuple-element.144), channel_id=1, source_target_pairs={{0,28},{4,24},{8,20},{12,16},{16,12},{20,8},{24,4},{28,0},{1,29},{... | collective-permute-start | bytes 466952 | tf_op jit(solution)/shard_map/ppermute | solution.py:422
  170.4 3.6 %settle.1 = (bf16[128,4096]{1,0:T(8,128)(2,1)}, bf16[8,24,256]{2,1,0:T(8,128)(2,1)S(1)}, bf16[128,4096]{1,0:T(8,128)(2,1)}, bf16[128,4096]{1,0:T(8,128)(2,1)}, bf16[128,4096]{1,0:T(8,128)(2,1)}) custom-call(bf16[152,512]{1,0:T(8,128)(2,1)S(1)} %copy-done.9, bf16[152,512]{1,0:T(8,128)(2,1)S(1)} %collective-permute-done.14.refs_1_, ...), custom_call_target="tpu_custom_call" | custom-call | tf_op jit(solution)/shard_map/settle/pallas_call | solution.py:642
  174.0 11.1 %collective-permute-done.30.refs_4_ = bf16[304,256]{1,0:T(8,128)(2,1)S(1)} collective-permute-done((bf16[304,256]{1,0:T(8,128)(2,1)}, bf16[304,256]{1,0:T(8,128)(2,1)S(1)}, u32[]{:S(2)}, u32[]{:S(2)}) %collective-permute-start.30) | collective-permute-done | bytes 155680 | tf_op jit(solution)/shard_map/ppermute | solution.py:422
  185.1 3.3 %collective-permute-done.31.refs_5_ = bf16[304,256]{1,0:T(8,128)(2,1)S(1)} collective-permute-done((bf16[304,256]{1,0:T(8,128)(2,1)}, bf16[304,256]{1,0:T(8,128)(2,1)S(1)}, u32[]{:S(2)}, u32[]{:S(2)}) %collective-permute-start.31) | collective-permute-done | bytes 155680 | tf_op jit(solution)/shard_map/ppermute | solution.py:422
  188.5 5.6 %collective-permute-done.32.refs_6_ = bf16[304,256]{1,0:T(8,128)(2,1)S(1)} collective-permute-done((bf16[304,256]{1,0:T(8,128)(2,1)}, bf16[304,256]{1,0:T(8,128)(2,1)S(1)}, u32[]{:S(2)}, u32[]{:S(2)}) %collective-permute-start.32) | collective-permute-done | bytes 155680 | tf_op jit(solution)/shard_map/ppermute | solution.py:422
  194.1 3.1 %collective-permute-done.33.refs_7_ = bf16[304,256]{1,0:T(8,128)(2,1)S(1)} collective-permute-done((bf16[304,256]{1,0:T(8,128)(2,1)}, bf16[304,256]{1,0:T(8,128)(2,1)S(1)}, u32[]{:S(2)}, u32[]{:S(2)}) %collective-permute-start.33) | collective-permute-done | bytes 155680 | tf_op jit(solution)/shard_map/ppermute | solution.py:422
  197.3 2.2 %finish.1 = (bf16[128,4096]{1,0:T(8,128)(2,1)}, bf16[128,4096]{1,0:T(8,128)(2,1)}, bf16[128,4096]{1,0:T(8,128)(2,1)}, f32[8,5120]{1,0:T(8,128)}) custom-call(bf16[304,256]{1,0:T(8,128)(2,1)S(1)} %copy-done.10, bf16[304,256]{1,0:T(8,128)(2,1)S(1)} %collective-permute-done.27.refs_1_, ...), custom_call_target="tpu_custom_call", output_to_operand_aliasing={{0}: (9, {}), {1}: (10, {}), {2}: (11, {})} | custom-call | tf_op jit(solution)/shard_map/finish/pallas_call | solution.py:649
  (93 shorter events, 1.0 us)
Async XLA Ops:
  0.6 83.4 %copy-start = (f32[8,5120]{1,0:T(8,128)S(1)}, f32[8,5120]{1,0:T(8,128)}, u32[]{:S(2)}) copy-start(f32[8,5120]{1,0:T(8,128)} %param.12) | copy-start | bytes 491524
  2.6 9.3 %copy-start.12 = (s32[1,1024]{1,0:T(1,128)S(1)}, s32[1,1024]{1,0:T(1,128)}, u32[]{:S(2)}) copy-start(s32[1,1024]{1,0:T(1,128)} %param.13) | copy-start | bytes 12292
  2.6 29.5 %collective-permute-start.7 = (bf16[2,128,512]{2,1,0:T(8,128)(2,1)S(1)}, bf16[2,128,512]{2,1,0:T(8,128)(2,1)}, u32[]{:S(2)}, u32[]{:S(2)}) collective-permute-start(bf16[2,128,512]{2,1,0:T(8,128)(2,1)S(1)} %pad_maximum_fusion.4), channel_id=1, source_target_pairs={{0,28},{4,24},{8,20},{12,16},{16,12},{20,8},{24,4},{28,0},{1,29},{... | collective-permute-start | bytes 786440 | tf_op jit(solution)/shard_map/ppermute | solution.py:422
  5.2 14.6 %copy-start.11 = (bf16[1,128,4096]{2,1,0:T(8,128)(2,1)S(1)}, bf16[1,128,4096]{2,1,0:T(8,128)(2,1)}, u32[]{:S(2)}) copy-start(bf16[1,128,4096]{2,1,0:T(8,128)(2,1)} %param.10) | copy-start | bytes 3145732
  5.2 35.5 %collective-permute-start.6 = (bf16[2,128,512]{2,1,0:T(8,128)(2,1)S(1)}, bf16[2,128,512]{2,1,0:T(8,128)(2,1)}, u32[]{:S(2)}, u32[]{:S(2)}) collective-permute-start(bf16[2,128,512]{2,1,0:T(8,128)(2,1)S(1)} %pad_maximum_fusion.3), channel_id=1, source_target_pairs={{0,24},{4,28},{8,16},{12,20},{16,8},{20,12},{24,0},{28,4},{1,25},{... | collective-permute-start | bytes 786440 | tf_op jit(solution)/shard_map/ppermute | solution.py:422
  5.8 42.7 %collective-permute-start.5 = (bf16[2,128,512]{2,1,0:T(8,128)(2,1)S(1)}, bf16[2,128,512]{2,1,0:T(8,128)(2,1)}, u32[]{:S(2)}, u32[]{:S(2)}) collective-permute-start(bf16[2,128,512]{2,1,0:T(8,128)(2,1)S(1)} %pad_maximum_fusion.2), channel_id=1, source_target_pairs={{0,20},{4,16},{8,28},{12,24},{16,4},{20,0},{24,12},{28,8},{1,21},{... | collective-permute-start | bytes 786440 | tf_op jit(solution)/shard_map/ppermute | solution.py:422
  10.2 7.5 %collective-permute-start = (bf16[2,128,512]{2,1,0:T(8,128)(2,1)S(1)}, bf16[2,128,512]{2,1,0:T(8,128)(2,1)}, u32[]{:S(2)}, u32[]{:S(2)}) collective-permute-start(bf16[2,128,512]{2,1,0:T(8,128)(2,1)S(1)} %pad_maximum_fusion), channel_id=1, source_target_pairs={{0,4},{4,0},{8,12},{12,8},{16,20},{20,16},{24,28},{28,24},{1,5},{5... | collective-permute-start | bytes 786440 | tf_op jit(solution)/shard_map/ppermute | solution.py:422
  12.6 50.9 %copy-start.20 = (s32[1,21]{1,0:T(1,128)S(1)}, s32[1,21]{1,0:T(1,128)}, u32[]{:S(2)}) copy-start(s32[1,21]{1,0:T(1,128)} %param.14) | copy-start | bytes 256
  17.7 12.9 %collective-permute-start.12 = (bf16[2,128,512]{2,1,0:T(8,128)(2,1)S(1)}, bf16[2,128,512]{2,1,0:T(8,128)(2,1)S(1)}, u32[]{:S(2)}, u32[]{:S(2)}) collective-permute-start(bf16[2,128,512]{2,1,0:T(8,128)(2,1)S(1)} %pad_maximum_fusion.6), channel_id=1, source_target_pairs={{0,8},{4,12},{8,0},{12,4},{16,24},{20,28},{24,16},{28,20},{1,9},{5... | collective-permute-start | bytes 786440 | tf_op jit(solution)/shard_map/ppermute | solution.py:422
  20.5 53.1 %copy-start.1 = (bf16[128,512]{1,0:T(8,128)(2,1)}, bf16[128,512]{1,0:T(8,128)(2,1)S(1)}, u32[]{:S(2)}) copy-start(bf16[128,512]{1,0:T(8,128)(2,1)S(1)} %get-tuple-element.175.refs_0_) | copy-start | bytes 393220
  20.5 10.7 %collective-permute-start.1 = (bf16[128,512]{1,0:T(8,128)(2,1)S(1)}, bf16[128,512]{1,0:T(8,128)(2,1)S(1)}, u32[]{:S(2)}, u32[]{:S(2)}) collective-permute-start(bf16[128,512]{1,0:T(8,128)(2,1)S(1)} %get-tuple-element.80), channel_id=1, source_target_pairs={{0,4},{4,0},{8,12},{12,8},{16,20},{20,16},{24,28},{28,24},{1,5},{5... | collective-permute-start | bytes 393224 | tf_op jit(solution)/shard_map/ppermute | solution.py:422
  30.6 32.2 %copy-start.13 = (bf16[2,128,512]{2,1,0:T(8,128)(2,1)}, bf16[2,128,512]{2,1,0:T(8,128)(2,1)S(1)}, u32[]{:S(2)}) copy-start(bf16[2,128,512]{2,1,0:T(8,128)(2,1)S(1)} %collective-permute-done.12.refs_2_) | copy-start | bytes 786436
  30.6 23.5 %collective-permute-start.4 = (bf16[2,128,512]{2,1,0:T(8,128)(2,1)S(1)}, bf16[2,128,512]{2,1,0:T(8,128)(2,1)S(1)}, u32[]{:S(2)}, u32[]{:S(2)}) collective-permute-start(bf16[2,128,512]{2,1,0:T(8,128)(2,1)S(1)} %pad_maximum_fusion.1), channel_id=1, source_target_pairs={{0,16},{4,20},{8,24},{12,28},{16,0},{20,4},{24,8},{28,12},{1,17},{... | collective-permute-start | bytes 786440 | tf_op jit(solution)/shard_map/ppermute | solution.py:422
  31.3 42.4 %copy-start.2 = (bf16[128,512]{1,0:T(8,128)(2,1)}, bf16[128,512]{1,0:T(8,128)(2,1)S(1)}, u32[]{:S(2)}) copy-start(bf16[128,512]{1,0:T(8,128)(2,1)S(1)} %collective-permute-done.1.refs_1_) | copy-start | bytes 393220
  31.3 27.4 %collective-permute-start.13 = (bf16[2,128,512]{2,1,0:T(8,128)(2,1)S(1)}, bf16[2,128,512]{2,1,0:T(8,128)(2,1)S(1)}, u32[]{:S(2)}, u32[]{:S(2)}) collective-permute-start(bf16[2,128,512]{2,1,0:T(8,128)(2,1)S(1)} %pad_maximum_fusion.7), channel_id=1, source_target_pairs={{0,12},{4,8},{8,4},{12,0},{16,28},{20,24},{24,20},{28,16},{1,13},{... | collective-permute-start | bytes 786440 | tf_op jit(solution)/shard_map/ppermute | solution.py:422
  32.1 26.6 %collective-permute-start.2 = (bf16[128,512]{1,0:T(8,128)(2,1)S(1)}, bf16[128,512]{1,0:T(8,128)(2,1)S(1)}, u32[]{:S(2)}, u32[]{:S(2)}) collective-permute-start(bf16[128,512]{1,0:T(8,128)(2,1)S(1)} %get-tuple-element.81), channel_id=1, source_target_pairs={{0,8},{4,12},{8,0},{12,4},{16,24},{20,28},{24,16},{28,20},{1,9},{5... | collective-permute-start | bytes 393224 | tf_op jit(solution)/shard_map/ppermute | solution.py:422
  40.7 32.8 %collective-permute-start.11 = (bf16[128,512]{1,0:T(8,128)(2,1)}, bf16[128,512]{1,0:T(8,128)(2,1)S(1)}, u32[]{:S(2)}, u32[]{:S(2)}) collective-permute-start(bf16[128,512]{1,0:T(8,128)(2,1)} %get-tuple-element.86), channel_id=1, source_target_pairs={{0,28},{4,24},{8,20},{12,16},{16,12},{20,8},{24,4},{28,0},{1,29},{... | collective-permute-start | bytes 393224 | tf_op jit(solution)/shard_map/ppermute | solution.py:422
  54.1 9.4 %copy-start.14 = (bf16[2,128,512]{2,1,0:T(8,128)(2,1)}, bf16[2,128,512]{2,1,0:T(8,128)(2,1)S(1)}, u32[]{:S(2)}) copy-start(bf16[2,128,512]{2,1,0:T(8,128)(2,1)S(1)} %collective-permute-done.4.refs_4_) | copy-start | bytes 786436
  54.1 19.4 %collective-permute-start.10 = (bf16[128,512]{1,0:T(8,128)(2,1)S(1)}, bf16[128,512]{1,0:T(8,128)(2,1)S(1)}, u32[]{:S(2)}, u32[]{:S(2)}) collective-permute-start(bf16[128,512]{1,0:T(8,128)(2,1)S(1)} %get-tuple-element.85), channel_id=1, source_target_pairs={{0,24},{4,28},{8,16},{12,20},{16,8},{20,12},{24,0},{28,4},{1,25},{... | collective-permute-start | bytes 393224 | tf_op jit(solution)/shard_map/ppermute | solution.py:422
  54.3 19.2 %collective-permute-start.9 = (bf16[128,512]{1,0:T(8,128)(2,1)S(1)}, bf16[128,512]{1,0:T(8,128)(2,1)S(1)}, u32[]{:S(2)}, u32[]{:S(2)}) collective-permute-start(bf16[128,512]{1,0:T(8,128)(2,1)S(1)} %get-tuple-element.84), channel_id=1, source_target_pairs={{0,20},{4,16},{8,28},{12,24},{16,4},{20,0},{24,12},{28,8},{1,21},{... | collective-permute-start | bytes 393224 | tf_op jit(solution)/shard_map/ppermute | solution.py:422
  58.7 15.0 %copy-start.3 = (bf16[128,512]{1,0:T(8,128)(2,1)}, bf16[128,512]{1,0:T(8,128)(2,1)S(1)}, u32[]{:S(2)}) copy-start(bf16[128,512]{1,0:T(8,128)(2,1)S(1)} %collective-permute-done.2.refs_2_) | copy-start | bytes 393220
  58.7 14.9 %collective-permute-start.8 = (bf16[128,512]{1,0:T(8,128)(2,1)S(1)}, bf16[128,512]{1,0:T(8,128)(2,1)S(1)}, u32[]{:S(2)}, u32[]{:S(2)}) collective-permute-start(bf16[128,512]{1,0:T(8,128)(2,1)S(1)} %get-tuple-element.83), channel_id=1, source_target_pairs={{0,16},{4,20},{8,24},{12,28},{16,0},{20,4},{24,8},{28,12},{1,17},{... | collective-permute-start | bytes 393224 | tf_op jit(solution)/shard_map/ppermute | solution.py:422
  58.7 4.1 %copy-start.15 = (bf16[2,128,512]{2,1,0:T(8,128)(2,1)}, bf16[2,128,512]{2,1,0:T(8,128)(2,1)S(1)}, u32[]{:S(2)}) copy-start(bf16[2,128,512]{2,1,0:T(8,128)(2,1)S(1)} %collective-permute-done.13.refs_3_) | copy-start | bytes 786436
  58.7 14.9 %collective-permute-start.3 = (bf16[128,512]{1,0:T(8,128)(2,1)S(1)}, bf16[128,512]{1,0:T(8,128)(2,1)S(1)}, u32[]{:S(2)}, u32[]{:S(2)}) collective-permute-start(bf16[128,512]{1,0:T(8,128)(2,1)S(1)} %get-tuple-element.82), channel_id=1, source_target_pairs={{0,12},{4,8},{8,4},{12,0},{16,28},{20,24},{24,20},{28,16},{1,13},{... | collective-permute-start | bytes 393224 | tf_op jit(solution)/shard_map/ppermute | solution.py:422
  73.5 5.3 %copy-start.4 = (bf16[128,512]{1,0:T(8,128)(2,1)}, bf16[128,512]{1,0:T(8,128)(2,1)S(1)}, u32[]{:S(2)}) copy-start(bf16[128,512]{1,0:T(8,128)(2,1)S(1)} %collective-permute-done.11.refs_7_) | copy-start | bytes 393220
  73.5 5.3 %copy-start.5 = (bf16[128,512]{1,0:T(8,128)(2,1)}, bf16[128,512]{1,0:T(8,128)(2,1)S(1)}, u32[]{:S(2)}) copy-start(bf16[128,512]{1,0:T(8,128)(2,1)S(1)} %collective-permute-done.10.refs_6_) | copy-start | bytes 393220
  73.6 5.2 %copy-start.6 = (bf16[128,512]{1,0:T(8,128)(2,1)}, bf16[128,512]{1,0:T(8,128)(2,1)S(1)}, u32[]{:S(2)}) copy-start(bf16[128,512]{1,0:T(8,128)(2,1)S(1)} %collective-permute-done.9.refs_5_) | copy-start | bytes 393220
  73.6 5.2 %copy-start.7 = (bf16[128,512]{1,0:T(8,128)(2,1)}, bf16[128,512]{1,0:T(8,128)(2,1)S(1)}, u32[]{:S(2)}) copy-start(bf16[128,512]{1,0:T(8,128)(2,1)S(1)} %collective-permute-done.8.refs_4_) | copy-start | bytes 393220
  73.6 5.2 %copy-start.8 = (bf16[128,512]{1,0:T(8,128)(2,1)}, bf16[128,512]{1,0:T(8,128)(2,1)S(1)}, u32[]{:S(2)}) copy-start(bf16[128,512]{1,0:T(8,128)(2,1)S(1)} %collective-permute-done.3.refs_3_) | copy-start | bytes 393220
  78.8 13.3 %all-to-all-start = ((bf16[8,24,768]{2,1,0:T(8,128)(2,1)}), bf16[8,24,768]{2,1,0:T(8,128)(2,1)S(1)}, u32[]{:S(2)}, u32[]{:S(2)}) async-start(bf16[8,24,768]{2,1,0:T(8,128)(2,1)} %get-tuple-element.93), calls=%async_computation | async-start | bytes 589824 | tf_op jit(solution)/shard_map/all_to_all | solution.py:396
  89.0 5.7 %collective-permute-start.17 = (bf16[152,256]{1,0:T(8,128)(2,1)}, bf16[152,256]{1,0:T(8,128)(2,1)S(1)}, u32[]{:S(2)}, u32[]{:S(2)}) collective-permute-start(bf16[152,256]{1,0:T(8,128)(2,1)} %get-tuple-element.108), channel_id=1, source_target_pairs={{0,16},{4,20},{8,24},{12,28},{16,0},{20,4},{24,8},{28,12},{1,17},{... | collective-permute-start | bytes 233480 | tf_op jit(solution)/shard_map/ppermute | solution.py:422
  94.7 23.6 %all-to-all-start.1 = ((bf16[8,24,768]{2,1,0:T(8,128)(2,1)}), bf16[8,24,768]{2,1,0:T(8,128)(2,1)S(1)}, u32[]{:S(2)}, u32[]{:S(2)}) async-start(bf16[8,24,768]{2,1,0:T(8,128)(2,1)} %get-tuple-element.113), calls=%async_computation.1 | async-start | bytes 589824 | tf_op jit(solution)/shard_map/all_to_all | solution.py:396
  101.4 14.1 %collective-permute-start.18 = (bf16[152,256]{1,0:T(8,128)(2,1)}, bf16[152,256]{1,0:T(8,128)(2,1)S(1)}, u32[]{:S(2)}, u32[]{:S(2)}) collective-permute-start(bf16[152,256]{1,0:T(8,128)(2,1)} %get-tuple-element.109), channel_id=1, source_target_pairs={{0,20},{4,16},{8,28},{12,24},{16,4},{20,0},{24,12},{28,8},{1,21},{... | collective-permute-start | bytes 233480 | tf_op jit(solution)/shard_map/ppermute | solution.py:422
  104.7 13.2 %collective-permute-start.19 = (bf16[152,256]{1,0:T(8,128)(2,1)}, bf16[152,256]{1,0:T(8,128)(2,1)S(1)}, u32[]{:S(2)}, u32[]{:S(2)}) collective-permute-start(bf16[152,256]{1,0:T(8,128)(2,1)} %get-tuple-element.110), channel_id=1, source_target_pairs={{0,24},{4,28},{8,16},{12,20},{16,8},{20,12},{24,0},{28,4},{1,25},{... | collective-permute-start | bytes 233480 | tf_op jit(solution)/shard_map/ppermute | solution.py:422
  104.7 13.6 %collective-permute-start.20 = (bf16[152,256]{1,0:T(8,128)(2,1)}, bf16[152,256]{1,0:T(8,128)(2,1)S(1)}, u32[]{:S(2)}, u32[]{:S(2)}) collective-permute-start(bf16[152,256]{1,0:T(8,128)(2,1)} %get-tuple-element.111), channel_id=1, source_target_pairs={{0,28},{4,24},{8,20},{12,16},{16,12},{20,8},{24,4},{28,0},{1,29},{... | collective-permute-start | bytes 233480 | tf_op jit(solution)/shard_map/ppermute | solution.py:422
  111.7 12.8 %collective-permute-start.14 = (bf16[152,512]{1,0:T(8,128)(2,1)}, bf16[152,512]{1,0:T(8,128)(2,1)S(1)}, u32[]{:S(2)}, u32[]{:S(2)}) collective-permute-start(bf16[152,512]{1,0:T(8,128)(2,1)} %get-tuple-element.105), channel_id=1, source_target_pairs={{0,4},{4,0},{8,12},{12,8},{16,20},{20,16},{24,28},{28,24},{1,5},{5... | collective-permute-start | bytes 466952 | tf_op jit(solution)/shard_map/ppermute | solution.py:422
  113.2 12.3 %collective-permute-start.15 = (bf16[152,512]{1,0:T(8,128)(2,1)}, bf16[152,512]{1,0:T(8,128)(2,1)S(1)}, u32[]{:S(2)}, u32[]{:S(2)}) collective-permute-start(bf16[152,512]{1,0:T(8,128)(2,1)} %get-tuple-element.106), channel_id=1, source_target_pairs={{0,8},{4,12},{8,0},{12,4},{16,24},{20,28},{24,16},{28,20},{1,9},{5... | collective-permute-start | bytes 466952 | tf_op jit(solution)/shard_map/ppermute | solution.py:422
  115.5 14.9 %collective-permute-start.16 = (bf16[152,512]{1,0:T(8,128)(2,1)}, bf16[152,512]{1,0:T(8,128)(2,1)S(1)}, u32[]{:S(2)}, u32[]{:S(2)}) collective-permute-start(bf16[152,512]{1,0:T(8,128)(2,1)} %get-tuple-element.107), channel_id=1, source_target_pairs={{0,12},{4,8},{8,4},{12,0},{16,28},{20,24},{24,20},{28,16},{1,13},{... | collective-permute-start | bytes 466952 | tf_op jit(solution)/shard_map/ppermute | solution.py:422
  118.3 3.2 %copy-start.19 = (bf16[152,256]{1,0:T(8,128)(2,1)S(1)}, bf16[152,256]{1,0:T(8,128)(2,1)}, u32[]{:S(2)}) copy-start(bf16[152,256]{1,0:T(8,128)(2,1)} %get-tuple-element.121) | copy-start | bytes 233476
  118.3 4.5 %copy-start.18 = (bf16[152,256]{1,0:T(8,128)(2,1)S(1)}, bf16[152,256]{1,0:T(8,128)(2,1)}, u32[]{:S(2)}) copy-start(bf16[152,256]{1,0:T(8,128)(2,1)} %get-tuple-element.127) | copy-start | bytes 233476
  118.3 6.1 %copy-start.17 = (bf16[152,256]{1,0:T(8,128)(2,1)S(1)}, bf16[152,256]{1,0:T(8,128)(2,1)}, u32[]{:S(2)}) copy-start(bf16[152,256]{1,0:T(8,128)(2,1)} %get-tuple-element.125) | copy-start | bytes 233476
  118.3 7.2 %copy-start.16 = (bf16[152,256]{1,0:T(8,128)(2,1)S(1)}, bf16[152,256]{1,0:T(8,128)(2,1)}, u32[]{:S(2)}) copy-start(bf16[152,256]{1,0:T(8,128)(2,1)} %get-tuple-element.123) | copy-start | bytes 233476
  121.5 9.0 %collective-permute-start.21 = (bf16[152,256]{1,0:T(8,128)(2,1)S(1)}, bf16[152,256]{1,0:T(8,128)(2,1)S(1)}, u32[]{:S(2)}, u32[]{:S(2)}) collective-permute-start(bf16[152,256]{1,0:T(8,128)(2,1)S(1)} %copy-done.19), channel_id=1, source_target_pairs={{0,16},{4,20},{8,24},{12,28},{16,0},{20,4},{24,8},{28,12},{1,17},{... | collective-permute-start | bytes 233480 | tf_op jit(solution)/shard_map/ppermute | solution.py:422
  121.6 1.3 collective-permute-start.25
  122.8 15.7 %collective-permute-start.24 = (bf16[152,256]{1,0:T(8,128)(2,1)S(1)}, bf16[152,256]{1,0:T(8,128)(2,1)S(1)}, u32[]{:S(2)}, u32[]{:S(2)}) collective-permute-start(bf16[152,256]{1,0:T(8,128)(2,1)S(1)} %copy-done.18), channel_id=1, source_target_pairs={{0,28},{4,24},{8,20},{12,16},{16,12},{20,8},{24,4},{28,0},{1,29},{... | collective-permute-start | bytes 233480 | tf_op jit(solution)/shard_map/ppermute | solution.py:422
  124.4 14.1 %collective-permute-start.23 = (bf16[152,256]{1,0:T(8,128)(2,1)S(1)}, bf16[152,256]{1,0:T(8,128)(2,1)S(1)}, u32[]{:S(2)}, u32[]{:S(2)}) collective-permute-start(bf16[152,256]{1,0:T(8,128)(2,1)S(1)} %copy-done.17), channel_id=1, source_target_pairs={{0,24},{4,28},{8,16},{12,20},{16,8},{20,12},{24,0},{28,4},{1,25},{... | collective-permute-start | bytes 233480 | tf_op jit(solution)/shard_map/ppermute | solution.py:422
  125.5 13.1 %collective-permute-start.22 = (bf16[152,256]{1,0:T(8,128)(2,1)S(1)}, bf16[152,256]{1,0:T(8,128)(2,1)S(1)}, u32[]{:S(2)}, u32[]{:S(2)}) collective-permute-start(bf16[152,256]{1,0:T(8,128)(2,1)S(1)} %copy-done.16), channel_id=1, source_target_pairs={{0,20},{4,16},{8,28},{12,24},{16,4},{20,0},{24,12},{28,8},{1,21},{... | collective-permute-start | bytes 233480 | tf_op jit(solution)/shard_map/ppermute | solution.py:422
  138.6 31.9 %all-to-all-start.2 = ((bf16[8,280,256]{2,1,0:T(8,128)(2,1)}), bf16[8,280,256]{2,1,0:T(8,128)(2,1)}, u32[]{:S(2)}, u32[]{:S(2)}) async-start(bf16[8,280,256]{2,1,0:T(8,128)(2,1)} %attention_back.2), calls=%async_computation.2 | async-start | bytes 2293760 | tf_op jit(solution)/shard_map/all_to_all | solution.py:396
  142.9 3.8 %collective-permute-start.26 = (f32[8,640]{1,0:T(8,128)S(1)}, f32[8,640]{1,0:T(8,128)S(1)}, u32[]{:S(2)}, u32[]{:S(2)}) collective-permute-start(f32[8,640]{1,0:T(8,128)S(1)} %add.89), channel_id=1, source_target_pairs={{0,2},{1,3},{2,0},{3,1},{4,6},{5,7},{6,4},{7,5},{8,10},{9,11},{10,... | collective-permute-start | bytes 61448 | tf_op jit(solution)/shard_map/ppermute | solution.py:627
  146.7 23.7 %copy-start.9 = (bf16[152,512]{1,0:T(8,128)(2,1)S(1)}, bf16[152,512]{1,0:T(8,128)(2,1)}, u32[]{:S(2)}) copy-start(bf16[152,512]{1,0:T(8,128)(2,1)} %get-tuple-element.104.refs_0_) | copy-start | bytes 466948
  154.9 8.9 %collective-permute-start.27 = (bf16[304,256]{1,0:T(8,128)(2,1)}, bf16[304,256]{1,0:T(8,128)(2,1)S(1)}, u32[]{:S(2)}, u32[]{:S(2)}) collective-permute-start(bf16[304,256]{1,0:T(8,128)(2,1)} %get-tuple-element.138), channel_id=1, source_target_pairs={{0,4},{4,0},{8,12},{12,8},{16,20},{20,16},{24,28},{28,24},{1,5},{5... | collective-permute-start | bytes 466952 | tf_op jit(solution)/shard_map/ppermute | solution.py:422
  156.4 10.8 %collective-permute-start.28 = (bf16[304,256]{1,0:T(8,128)(2,1)}, bf16[304,256]{1,0:T(8,128)(2,1)S(1)}, u32[]{:S(2)}, u32[]{:S(2)}) collective-permute-start(bf16[304,256]{1,0:T(8,128)(2,1)} %get-tuple-element.139), channel_id=1, source_target_pairs={{0,8},{4,12},{8,0},{12,4},{16,24},{20,28},{24,16},{28,20},{1,9},{5... | collective-permute-start | bytes 466952 | tf_op jit(solution)/shard_map/ppermute | solution.py:422
  157.0 17.0 %collective-permute-start.29 = (bf16[304,256]{1,0:T(8,128)(2,1)}, bf16[304,256]{1,0:T(8,128)(2,1)S(1)}, u32[]{:S(2)}, u32[]{:S(2)}) collective-permute-start(bf16[304,256]{1,0:T(8,128)(2,1)} %get-tuple-element.140), channel_id=1, source_target_pairs={{0,12},{4,8},{8,4},{12,0},{16,28},{20,24},{24,20},{28,16},{1,13},{... | collective-permute-start | bytes 466952 | tf_op jit(solution)/shard_map/ppermute | solution.py:422
  158.5 26.7 %collective-permute-start.30 = (bf16[304,256]{1,0:T(8,128)(2,1)}, bf16[304,256]{1,0:T(8,128)(2,1)S(1)}, u32[]{:S(2)}, u32[]{:S(2)}) collective-permute-start(bf16[304,256]{1,0:T(8,128)(2,1)} %get-tuple-element.141), channel_id=1, source_target_pairs={{0,16},{4,20},{8,24},{12,28},{16,0},{20,4},{24,8},{28,12},{1,17},{... | collective-permute-start | bytes 466952 | tf_op jit(solution)/shard_map/ppermute | solution.py:422
  160.9 27.6 %collective-permute-start.31 = (bf16[304,256]{1,0:T(8,128)(2,1)}, bf16[304,256]{1,0:T(8,128)(2,1)S(1)}, u32[]{:S(2)}, u32[]{:S(2)}) collective-permute-start(bf16[304,256]{1,0:T(8,128)(2,1)} %get-tuple-element.142), channel_id=1, source_target_pairs={{0,20},{4,16},{8,28},{12,24},{16,4},{20,0},{24,12},{28,8},{1,21},{... | collective-permute-start | bytes 466952 | tf_op jit(solution)/shard_map/ppermute | solution.py:422
  163.8 30.3 %collective-permute-start.32 = (bf16[304,256]{1,0:T(8,128)(2,1)}, bf16[304,256]{1,0:T(8,128)(2,1)S(1)}, u32[]{:S(2)}, u32[]{:S(2)}) collective-permute-start(bf16[304,256]{1,0:T(8,128)(2,1)} %get-tuple-element.143), channel_id=1, source_target_pairs={{0,24},{4,28},{8,16},{12,20},{16,8},{20,12},{24,0},{28,4},{1,25},{... | collective-permute-start | bytes 466952 | tf_op jit(solution)/shard_map/ppermute | solution.py:422
  167.2 30.0 %collective-permute-start.33 = (bf16[304,256]{1,0:T(8,128)(2,1)}, bf16[304,256]{1,0:T(8,128)(2,1)S(1)}, u32[]{:S(2)}, u32[]{:S(2)}) collective-permute-start(bf16[304,256]{1,0:T(8,128)(2,1)} %get-tuple-element.144), channel_id=1, source_target_pairs={{0,28},{4,24},{8,20},{12,16},{16,12},{20,8},{24,4},{28,0},{1,29},{... | collective-permute-start | bytes 466952 | tf_op jit(solution)/shard_map/ppermute | solution.py:422
  170.4 26.8 %copy-start.10 = (bf16[304,256]{1,0:T(8,128)(2,1)S(1)}, bf16[304,256]{1,0:T(8,128)(2,1)}, u32[]{:S(2)}) copy-start(bf16[304,256]{1,0:T(8,128)(2,1)} %get-tuple-element.137.refs_0_) | copy-start | bytes 466948
